TPU v7x, 256 devices: a whole 4x4x8 slice. The times are simulated.
256 devices in a mesh: dp: 16 (over z_hi, y), section: 2 (over core), tensor: 8 (over x, z_lo).
Axes of the slice: x: 4, y: 4, z: 8 (z_hi: 4, z_lo: 2; z = z_hi * 2 + z_lo), core: 2. Of those that a mesh axis runs over, the one named last changes fastest.
Arguments:
- residual: bfloat16 [2, 16, 128, 6144], P('section', 'dp'), may hold values from -6 to 6
- queries: bfloat16 [2, 16, 128, 6144], P('section', 'dp', None, 'tensor'), may hold values from -6 to 6
- key_vectors: bfloat16 [2, 16, 128, 6144], P('section', 'dp', None, 'tensor'), may hold values from -6 to 6
- value_vectors: bfloat16 [2, 16, 128, 6144], P('section', 'dp', None, 'tensor'), may hold values from -6 to 6
- block_mask: int32 [2, 16, 4, 4], P('section', 'dp'), may hold values from 0 to 1, as said below
- out_weight: bfloat16 [2, 6144, 6144], P('section', 'tensor', 'dp'), may hold values from -0.078125 to 0.078125
- codebook: bfloat16 [2, 6144, 768], P('section', 'dp'), may hold values from -0.078125 to 0.078125
- norm_gain: float32 [2, 6144], P('section'), may hold values from 0.1 to 1.9
- norm_bias: float32 [2, 6144], P('section'), may hold values from -3 to 3
- receiver_order: int32 [2, 128], P('section', ('dp', 'tensor')), may hold values from 0 to 127, each once within a row
- upstream: bfloat16 [2, 16, 128, 6144], P('section', 'dp'), may hold values from -6 to 6
Outputs:
- received: bfloat16 [2, 128, 16, 768], P('section', ('dp', 'tensor'))
- grad_residual: bfloat16 [2, 16, 128, 6144], P('section', 'dp', 'tensor')
- grad_queries: bfloat16 [2, 16, 128, 6144], P('section', 'dp', None, 'tensor')
- grad_keys: bfloat16 [2, 16, 128, 6144], P('section', 'dp', None, 'tensor')
- grad_values: bfloat16 [2, 16, 128, 6144], P('section', 'dp', None, 'tensor')
Inputs may be any that keep to these rules, and one draw needn't show every extreme that they name: `block_mask`: block (i, i) is 1 and block (i, j) with j > i is 0. `receiver_order`: each row is a permutation.
All inputs are finite; a program needn't handle non-finite values.
Results may differ from a plain program's by a relative error of at most 0.015.
Values may be sent and summed in bfloat16 or wider, within the bound.
No kernel may reach another device: no remote copies, remote signals or barrier semaphores. Data moves between devices by JAX's collectives and lax.ppermute only.
A program may use at most 64 MiB of HBM per device.

v0:
```python
import jax
import jax.numpy as jnp
from jax import lax
from jax.sharding import PartitionSpec as P

HEAD = 128
L = 128
BLK = 32


EPSILON = 1e-05


def swapped_2(value, axis, distance):
    return lax.ppermute(value, axis, [(i, i ^ 1 << distance) for i in range(lax.axis_size(axis))])


def allowed_pairs(mask_blocks):
    block_table = jnp.repeat(jnp.repeat(mask_blocks, BLK, axis=0), BLK, axis=1) == 1
    position = lax.broadcasted_iota(jnp.int32, (L, L), 0)
    column = lax.broadcasted_iota(jnp.int32, (L, L), 1)
    return block_table & (position >= column)


def attend(query_rows, key_rows, value_rows, allowed):
    length = query_rows.shape[0]
    heads_here = query_rows.shape[1] // HEAD
    query_heads = query_rows.reshape(length, heads_here, HEAD)
    key_heads = key_rows.reshape(length, heads_here, HEAD)
    value_heads = value_rows.reshape(length, heads_here, HEAD)
    scores = jnp.einsum(
        "ihd,jhd->hij", query_heads, key_heads, preferred_element_type=jnp.float32
    ) * HEAD ** (-0.5)
    scores = jnp.where(allowed[None], scores, -1e30)
    probabilities = jax.nn.softmax(scores, axis=-1).astype(jnp.bfloat16)
    mixture = jnp.einsum(
        "hij,jhd->ihd", probabilities, value_heads, preferred_element_type=jnp.float32
    )
    return mixture.reshape(length, heads_here * HEAD).astype(jnp.bfloat16)


def times_transposed(left_side, right_side):
    return lax.dot_general(
        left_side, right_side, (((1,), (1,)), ((), ())), preferred_element_type=jnp.float32
    )


def finish_rows(code_total, residual_rows, upstream_rows, code_book, gain_row, bias_row):
    decoded = times_transposed(code_total, code_book)
    hidden = residual_rows.astype(jnp.float32) + decoded
    center_mean = jnp.mean(hidden, axis=-1, keepdims=True)
    centered = hidden - center_mean
    variance = jnp.mean(centered * centered, axis=-1, keepdims=True)
    inv_std = lax.rsqrt(variance + EPSILON)
    normed = centered * inv_std
    normed_out = normed * gain_row + bias_row
    boundary_codes = jnp.dot(
        normed_out.astype(jnp.bfloat16), code_book, preferred_element_type=jnp.float32
    ).astype(jnp.bfloat16)
    scaled = upstream_rows.astype(jnp.float32) * gain_row
    first_mean = jnp.mean(scaled, axis=-1, keepdims=True)
    second_mean = jnp.mean(scaled * normed, axis=-1, keepdims=True)
    grad_hidden = (inv_std * (scaled - first_mean - normed * second_mean)).astype(jnp.bfloat16)
    grad_code = jnp.dot(grad_hidden, code_book, preferred_element_type=jnp.float32).astype(
        jnp.bfloat16
    )
    return (boundary_codes, grad_hidden, grad_code)


def on_device(
    residual,
    queries,
    key_vectors,
    value_vectors,
    block_mask,
    out_weight,
    codebook,
    norm_gain,
    norm_bias,
    receiver_order,
    upstream,
):
    out_full, code_book = (
        lax.all_gather(out_weight[0], "dp", axis=1, tiled=True),
        lax.all_gather(codebook[0], "dp", axis=0, tiled=True),
    )
    joined = jnp.dot(out_full, code_book, preferred_element_type=jnp.float32).astype(jnp.bfloat16)
    allowed = allowed_pairs(block_mask[0, 0])
    query_rows = queries[0, 0]
    key_rows = key_vectors[0, 0]
    value_rows = value_vectors[0, 0]
    context = attend(query_rows, key_rows, value_rows, allowed)
    code_part = jnp.dot(context, joined, preferred_element_type=jnp.float32)
    tensor_count = lax.axis_size("tensor")
    tensor_rank = lax.axis_index("tensor")
    length = residual.shape[2]
    piece_rows = length // tensor_count
    gain_row = norm_gain[0]
    bias_row = norm_bias[0]
    code_total = lax.psum(code_part, "tensor").astype(jnp.bfloat16)
    boundary_codes, grad_hidden, grad_code = finish_rows(
        code_total, residual[0, 0], upstream[0, 0], code_book, gain_row, bias_row
    )
    codes_piece = lax.dynamic_slice_in_dim(boundary_codes, tensor_rank * piece_rows, piece_rows, 0)
    grad_residual = lax.dynamic_slice_in_dim(grad_hidden, tensor_rank * piece_rows, piece_rows, 0)
    grad_context = times_transposed(grad_code, joined).astype(jnp.bfloat16)

    def attend_only(query_in, key_in, value_in):
        return attend(query_in, key_in, value_in, allowed)

    _, pullback = jax.vjp(attend_only, query_rows, key_rows, value_rows)
    grad_query, grad_key, grad_value = pullback(grad_context)
    swapped = swapped_2(codes_piece, "section", 0)
    wanted_piece = receiver_order[0, 0]
    arrived = lax.all_gather(swapped, ("dp", "tensor"), axis=0, tiled=True)
    arrived_rows = arrived.shape[0]
    offset = wanted_piece * piece_rows
    inside = (offset >= 0) & (offset + piece_rows <= arrived_rows)
    selected = lax.dynamic_slice_in_dim(
        arrived, jnp.clip(offset, 0, arrived_rows - piece_rows), piece_rows, 0
    )
    received = jnp.where(inside, selected, jnp.zeros_like(swapped))
    return (
        received[None, None],
        grad_residual[None, None],
        grad_query[None, None],
        grad_key[None, None],
        grad_value[None, None],
    )


def solution(mesh):
    in_specs = (
        P("section", "dp", None, None),
        P("section", "dp", None, "tensor"),
        P("section", "dp", None, "tensor"),
        P("section", "dp", None, "tensor"),
        P("section", "dp", None, None),
        P("section", "tensor", "dp"),
        P("section", "dp", None),
        P("section", None),
        P("section", None),
        P("section", ("dp", "tensor")),
        P("section", "dp", None, None),
    )
    out_specs = (
        P("section", ("dp", "tensor"), None, None),
        P("section", "dp", "tensor", None),
        P("section", "dp", None, "tensor"),
        P("section", "dp", None, "tensor"),
        P("section", "dp", None, "tensor"),
    )
    return jax.shard_map(
        on_device, mesh=mesh, in_specs=in_specs, out_specs=out_specs, check_vma=False
    )
```

profile of v0, /device:TPU:0, one launch (start us, length us, event | category | flops | bytes accessed | tf_op | source)
XLA Modules:
  0.0 1003.0 jit_solution(2874240600612383904)
XLA Ops:
  7.2 0.0 all-gather.8.cloned.1.call-start
  7.2 0.7 all-gather.8.cloned.1.call-update
  7.9 0.0 all-gather.10.cloned.1.call-start
  7.9 0.7 all-gather.10.cloned.1.call-update
  8.6 0.0 all-gather.6.cloned.1.call-start
  8.7 0.7 compare_bitcast_fusion
  9.4 0.1 copy.31
  9.5 0.1 broadcast_in_dim.55
  9.6 0.1 eq.24
  9.7 1.1 copy.32
  10.8 0.0 copy-start.8
  10.8 1.2 copy.33
  12.0 0.0 copy-start.10
  12.0 1.2 copy.36
  13.1 0.3 fusion.31
  13.4 0.8 fusion.40
  14.2 0.3 convolution_convert_fusion
  14.5 132.9 %all-gather.8.cloned.1.call-done = bf16[1,768,6144]{2,1,0:T(8,128)(2,1)} async-done(((bf16[1,768,384]{2,1,0:T(8,128)(2,1)}), bf16[1,768,6144]{2,1,0:T(8,128)(2,1)}) %all-gather.8.cloned.1.call-update) | async-done | bytes 9437200 | tf_op jit(solution)/shard_map/all_gather | solution.py:84
  147.4 117.1 %all-gather.10.cloned.1.call-done = bf16[1,6144,768]{2,1,0:T(8,128)(2,1)} async-done(((bf16[1,384,768]{2,1,0:T(8,128)(2,1)}), bf16[1,6144,768]{2,1,0:T(8,128)(2,1)}) %all-gather.10.cloned.1.call-update) | async-done | bytes 9437200 | tf_op jit(solution)/shard_map/all_gather | solution.py:85
  264.5 12.8 %fusion.24 = bf16[768,768]{1,0:T(8,128)(2,1)S(1)} fusion(bf16[1,6144,768]{2,1,0:T(8,128)(2,1)} %all-gather.10.cloned.1.call-done, bf16[1,768,6144]{2,1,0:T(8,128)(2,1)} %all-gather.8.cloned.1.call-done), kind=kOutput, calls=%fused_computation.26 | convolution fusion | flops 7248347136 | bytes 20054016 | tf_op jit(solution)/shard_map/dot_general | solution.py:87
  277.2 0.0 copy-done.8
  277.3 0.0 copy-done.10
  277.3 0.0 copy-start.4
  277.3 1.0 copy-done.3
  278.3 0.4 fusion.42
  278.7 0.0 slice-start
  278.7 53.5 %all-reduce.1 = bf16[128,768]{1,0:T(8,128)(2,1)} all-reduce(f32[128,768]{1,0:T(8,128)S(1)} %fusion.42), channel_id=1, replica_groups=mesh['dp'=16,'section'=2,'tensor'=8] {'tensor'}, use_global_device_ids=true, to_apply=%region_2.3 | all-reduce | flops 98304 | bytes 589824 | tf_op jit(solution)/shard_map/psum | solution.py:100
  332.1 7.2 fusion.41
  339.3 0.0 copy-start
  339.3 0.0 copy-start.12
  339.3 0.0 copy-start.14
  339.4 0.5 multiply_reduce_fusion
  339.8 0.0 copy-start.20
  339.8 0.0 slice-done
  339.9 0.0 slice-done.1
  339.9 0.0 slice-done.2
  339.9 0.2 copy-done.12
  340.0 0.1 copy-done.14
  340.1 1.6 fusion.3
  341.8 0.0 copy-done
  341.8 0.0 copy-done.18
  341.8 0.0 copy-done.20
  341.9 0.3 collective-permute-start
  342.1 1.3 collective-permute-done
  343.4 0.0 all-gather.6.cloned.1.call-update
  343.5 0.0 copy-start.2
  343.5 0.0 copy-start.13
  344.3 1.3 multiply_divide_fusion
  345.6 3.3 fusion.15
  348.9 2.3 fusion.18
  351.3 6.7 convolution_convert_fusion.5
  358.0 0.0 copy-start.11
  358.0 0.2 copy.38
  358.1 0.0 copy-start.9
  358.2 0.3 multiply_reduce_fusion.1
  358.5 0.3 convolution_convert_fusion.1
  358.8 0.8 copy.45
  359.6 0.3 convolution_convert_fusion.3
  359.9 0.8 copy.43
  360.7 0.3 convolution_convert_fusion.2
  361.1 0.8 copy.44
  361.9 1.6 dynamic-slice_bitcast_fusion
  363.5 631.6 %all-gather.6.cloned.1.call-done = bf16[2048,768]{1,0:T(8,128)(2,1)} async-done(((bf16[16,768]{1,0:T(8,128)(2,1)}), bf16[2048,768]{1,0:T(8,128)(2,1)}) %all-gather.6.cloned.1.call-update) | async-done | bytes 3145744 | tf_op jit(solution)/shard_map/all_gather | solution.py:115
  995.1 1.4 select_bitcast_fusion
  (34 shorter events, 0.1 us)
Async XLA Ops:
  7.2 140.2 %all-gather.8.cloned.1.call-start = ((), (), s32[]{:S(2)}) async-start(), calls=%async_computation.1 | async-start | bytes 10027008 | tf_op jit(solution)/shard_map/all_gather | solution.py:84
  7.9 256.6 %all-gather.10.cloned.1.call-start = ((), (), s32[]{:S(2)}) async-start(), calls=%async_computation.2 | async-start | bytes 10027008 | tf_op jit(solution)/shard_map/all_gather | solution.py:85
  8.6 986.5 %all-gather.6.cloned.1.call-start = ((), (), s32[]{:S(2)}) async-start(), calls=%async_computation | async-start | bytes 3170304 | tf_op jit(solution)/shard_map/all_gather | solution.py:115
  10.8 266.5 %copy-start.8 = (bf16[1,1,128,768]{2,3,1,0:T(8,128)(2,1)}, bf16[1,1,128,768]{2,3,1,0:T(8,128)(2,1)S(1)}, u32[]{:S(2)}) copy-start(bf16[1,1,128,768]{2,3,1,0:T(8,128)(2,1)S(1)} %copy.32) | copy-start | bytes 589828
  12.0 265.3 %copy-start.10 = (bf16[1,1,128,768]{2,3,1,0:T(8,128)(2,1)}, bf16[1,1,128,768]{2,3,1,0:T(8,128)(2,1)S(1)}, u32[]{:S(2)}) copy-start(bf16[1,1,128,768]{2,3,1,0:T(8,128)(2,1)S(1)} %copy.33) | copy-start | bytes 589828
  13.1 264.1 %copy-start.6 = (bf16[1,1,128,768]{2,3,1,0:T(8,128)(2,1)}, bf16[1,1,128,768]{2,3,1,0:T(8,128)(2,1)S(1)}, u32[]{:S(2)}) copy-start(bf16[1,1,128,768]{2,3,1,0:T(8,128)(2,1)S(1)} %copy.36) | copy-start | bytes 589828
  14.2 263.0 %copy-start.15 = (f32[6,128]{1,0:T(8,128)}, f32[6,128]{1,0:T(8,128)S(1)}, u32[]{:S(2)}) copy-start(f32[6,128]{1,0:T(8,128)S(1)} %get-tuple-element.17) | copy-start | bytes 9220
  277.3 1.0 copy-start.3
  277.3 54.8 %copy-start.4 = (bf16[1,1,128,6144]{3,2,1,0:T(8,128)(2,1)S(1)}, bf16[1,1,128,6144]{3,2,1,0:T(8,128)(2,1)}, u32[]{:S(2)}) copy-start(bf16[1,1,128,6144]{3,2,1,0:T(8,128)(2,1)} %param.11) | copy-start | bytes 4718596
  278.7 61.2 %slice-start = ((s8[9437184]{0:T(1024)(128)(4,1)}), s8[1048576]{0:T(1024)(128)(4,1)S(1)}, s32[]{:S(2)}) async-start(s8[9437184]{0:T(1024)(128)(4,1)} %bitcast.82), calls=%async_computation.3 | async-start | bytes 2097152
  332.1 7.7 slice-start.1
  332.1 7.7 slice-start.2
  339.3 2.5 copy-start
  339.3 0.7 copy-start.12
  339.3 0.8 copy-start.14
  339.3 2.5 copy-start.18
  339.8 2.0 copy-start.20
  341.8 7.0 copy-start.1
  341.9 1.6 collective-permute-start
  343.5 5.4 copy-start.2
  343.5 5.4 copy-start.13
  343.5 5.4 copy-start.19
  343.5 5.4 copy-start.21
  351.2 6.9 copy-start.5
  351.2 6.9 copy-start.7
  351.2 6.9 copy-start.17
  351.2 7.2 copy-start.16
  358.0 1.6 copy-start.11
  358.1 2.6 copy-start.9
Sparse Core Ops, SparseCore 0:
  10.4 136.9 all-gather.7
  149.8 114.6 all-gather.9
  343.6 651.4 all-gather.5
where the time goes:
time: 1000 us
  waiting for transfers between devices  884 us (88%)
  blocking collectives  53.5 us (5%)
  matrix products  30.3 us (3%)
  between operations  14.9 us (1%)
  other arithmetic  10.3 us (1%)
    all_gather x1, waiting for transfers between devices, on_device(): arrived = lax.all_gather(swapped, ('dp', 'tensor'), axis=0, tiled=True)  632 us
    all_gather x1, waiting for transfers between devices, on_device(): lax.all_gather(out_weight[0], 'dp', axis=1, tiled=True)  133 us
    all_gather x1, waiting for transfers between devices, on_device(): lax.all_gather(codebook[0], 'dp', axis=0, tiled=True)  117 us
    psum x1, blocking collectives, on_device(): code_total = lax.psum(code_part, 'tensor').astype(jnp.bfloat16)  53.5 us
  transfers between devices with their start and end apart: 4, of which 4 were waited for; matrix products, arithmetic and copies ran while one was open for 2% of the time, Pallas kernels for 0%

commit v1 on v0

v1 whole, which is shorter than its diff:
```python
import jax
import jax.numpy as jnp
from jax import lax
from jax.sharding import PartitionSpec as P

HEAD = 128
L = 128
BLK = 32


EPSILON = 1e-05


def swapped_2(value, axis, distance):
    return lax.ppermute(value, axis, [(i, i ^ 1 << distance) for i in range(lax.axis_size(axis))])


def exchanged(value, axis):
    return lax.all_to_all(value, axis, 0, 0)


def gathered(value, axis):
    copies = jnp.broadcast_to(value[None], (lax.axis_size(axis),) + value.shape)
    return exchanged(copies, axis)


def summed(pieces):
    return jnp.sum(pieces.astype(jnp.float32), axis=0).astype(jnp.bfloat16)


def allowed_pairs(mask_blocks):
    block_table = jnp.repeat(jnp.repeat(mask_blocks, BLK, axis=0), BLK, axis=1) == 1
    position = lax.broadcasted_iota(jnp.int32, (L, L), 0)
    column = lax.broadcasted_iota(jnp.int32, (L, L), 1)
    return block_table & (position >= column)


def attend(query_rows, key_rows, value_rows, allowed):
    length = query_rows.shape[0]
    heads_here = query_rows.shape[1] // HEAD
    query_heads = query_rows.reshape(length, heads_here, HEAD)
    key_heads = key_rows.reshape(length, heads_here, HEAD)
    value_heads = value_rows.reshape(length, heads_here, HEAD)
    scores = jnp.einsum(
        "ihd,jhd->hij", query_heads, key_heads, preferred_element_type=jnp.float32
    ) * HEAD ** (-0.5)
    scores = jnp.where(allowed[None], scores, -1e30)
    probabilities = jax.nn.softmax(scores, axis=-1).astype(jnp.bfloat16)
    mixture = jnp.einsum(
        "hij,jhd->ihd", probabilities, value_heads, preferred_element_type=jnp.float32
    )
    return mixture.reshape(length, heads_here * HEAD).astype(jnp.bfloat16)


def times_transposed(left_side, right_side):
    return lax.dot_general(
        left_side, right_side, (((1,), (1,)), ((), ())), preferred_element_type=jnp.float32
    )


def on_device(
    residual,
    queries,
    key_vectors,
    value_vectors,
    block_mask,
    out_weight,
    codebook,
    norm_gain,
    norm_bias,
    receiver_order,
    upstream,
):
    n_dp = lax.axis_size("dp")
    n_tensor = lax.axis_size("tensor")
    rank = lax.axis_index("tensor")
    length, width = residual.shape[2:]
    code_book = codebook[0]
    shard, code_width = code_book.shape
    piece = shard // n_tensor
    rows = length // n_tensor
    features = n_dp * piece

    wanted = swapped_2(receiver_order[0], "section", 0)
    wanted_all = lax.all_gather(wanted, "dp", axis=0, tiled=True)
    own_slice = lax.dynamic_slice_in_dim(code_book, rank * piece, piece, 0)
    book_here = lax.all_gather(own_slice, "dp", axis=0, tiled=True)

    joined_part = jnp.dot(out_weight[0], code_book, preferred_element_type=jnp.float32)
    joined_part = joined_part.astype(jnp.bfloat16).reshape(n_dp, -1, code_width)
    joined_rows = summed(exchanged(joined_part, "dp"))
    joined = gathered(joined_rows, "dp").reshape(-1, code_width)

    def own_features(array):
        parts = array.reshape(array.shape[0], n_dp, shard)
        parts = lax.dynamic_slice_in_dim(parts, rank * piece, piece, 2)
        return parts.reshape(array.shape[0], features)

    residual_here = own_features(residual[0, 0]).astype(jnp.float32)
    gain_here = own_features(norm_gain)
    bias_here = own_features(norm_bias)
    scaled = own_features(upstream[0, 0]).astype(jnp.float32) * gain_here

    allowed = allowed_pairs(block_mask[0, 0])
    query_rows = queries[0, 0]
    key_rows = key_vectors[0, 0]
    value_rows = value_vectors[0, 0]

    def attend_only(query_in, key_in, value_in):
        return attend(query_in, key_in, value_in, allowed)

    context, pullback = jax.vjp(attend_only, query_rows, key_rows, value_rows)
    code_part = jnp.dot(context, joined, preferred_element_type=jnp.float32).astype(jnp.bfloat16)
    code_rows = summed(exchanged(code_part.reshape(n_tensor, rows, code_width), "tensor"))
    code_total = gathered(code_rows, "tensor").reshape(length, code_width)

    hidden = residual_here + times_transposed(code_total, book_here)
    near_mean = jnp.mean(hidden, axis=-1)
    near = hidden - near_mean[:, None]
    near_square = jnp.sum(near * near, axis=-1)
    scaled_sum = jnp.sum(scaled, axis=-1)
    scaled_near = jnp.sum(scaled * near, axis=-1)
    own_stats = jnp.stack([near_mean, near_square, scaled_sum, scaled_near])
    all_stats = gathered(own_stats, "tensor")
    means, squares, sums, products = (all_stats[:, i] for i in range(4))
    center_mean = jnp.mean(means, axis=0)
    offsets = means - center_mean
    variance = jnp.sum(squares + features * offsets * offsets, axis=0) / width
    inv_std = lax.rsqrt(variance + EPSILON)
    first_mean = jnp.sum(sums, axis=0) / width
    second_mean = inv_std * jnp.sum(products + offsets * sums, axis=0) / width

    normed = (hidden - center_mean[:, None]) * inv_std[:, None]
    normed_out = (normed * gain_here + bias_here).astype(jnp.bfloat16)
    grad_hidden = inv_std[:, None] * (
        scaled - first_mean[:, None] - normed * second_mean[:, None]
    )
    grad_hidden = grad_hidden.astype(jnp.bfloat16)
    codes_part = jnp.dot(normed_out, book_here, preferred_element_type=jnp.float32)
    grad_part = jnp.dot(grad_hidden, book_here, preferred_element_type=jnp.float32)
    sent = jnp.concatenate(
        [codes_part.astype(jnp.bfloat16), grad_part.astype(jnp.bfloat16), grad_hidden], axis=1
    )
    arrived = exchanged(sent.reshape(n_tensor, rows, -1), "tensor")
    code_rows = summed(arrived[:, :, : 2 * code_width])
    grad_residual = arrived[:, :, 2 * code_width :].reshape(n_tensor, rows, n_dp, piece)
    grad_residual = grad_residual.transpose(1, 2, 0, 3).reshape(rows, width)

    both = gathered(code_rows, "tensor")
    codes = both[:, :, :code_width]
    grad_code = both[:, :, code_width:].reshape(length, code_width)

    slots = jnp.take(codes, wanted_all % n_tensor, axis=0)
    routed = exchanged(slots, "dp")
    chosen = lax.dynamic_index_in_dim(routed, wanted[0] // n_tensor, 0, keepdims=False)
    received = swapped_2(chosen, "section", 0)

    grad_context = times_transposed(grad_code, joined).astype(jnp.bfloat16)
    grad_query, grad_key, grad_value = pullback(grad_context)
    return (
        received[None, None],
        grad_residual[None, None],
        grad_query[None, None],
        grad_key[None, None],
        grad_value[None, None],
    )


def solution(mesh):
    in_specs = (
        P("section", "dp", None, None),
        P("section", "dp", None, "tensor"),
        P("section", "dp", None, "tensor"),
        P("section", "dp", None, "tensor"),
        P("section", "dp", None, None),
        P("section", "tensor", "dp"),
        P("section", "dp", None),
        P("section", None),
        P("section", None),
        P("section", ("dp", "tensor")),
        P("section", "dp", None, None),
    )
    out_specs = (
        P("section", ("dp", "tensor"), None, None),
        P("section", "dp", "tensor", None),
        P("section", "dp", None, "tensor"),
        P("section", "dp", None, "tensor"),
        P("section", "dp", None, "tensor"),
    )
    return jax.shard_map(
        on_device, mesh=mesh, in_specs=in_specs, out_specs=out_specs, check_vma=False
    )
```

time: 1000 us -> 221 us (0.22)
  the two profiles are of different devices: /device:TPU:0 before, /device:TPU:1 now
where the time goes in v1:
time: 221 us; the launch traced here: 220 us
  blocking collectives  64.1 us (29%)
  waiting for transfers between devices  47.3 us (21%)
  starting transfers between devices  38 us (17%)
  local copies, waits for them, and re-layouts  28.9 us (13%)
  between operations  17 us (8%)
  other arithmetic  13.4 us (6%)
  matrix products  11.2 us (5%)
    all_to_all x2, blocking collectives, exchanged(): return lax.all_to_all(value, axis, 0, 0)  51.8 us
    all_to_all x6, waiting for transfers between devices, exchanged(): return lax.all_to_all(value, axis, 0, 0)  39.6 us
    all_to_all x6, starting transfers between devices, exchanged(): return lax.all_to_all(value, axis, 0, 0)  27.8 us
    unnamed x52, local copies, waits for them, and re-layouts  13.1 us
    unnamed x1, blocking collectives  12.3 us
    ppermute x2, starting transfers between devices, swapped_2(): lax.ppermute(value, axis, [(i, i ^ 1 << distance) for i in range(lax.axis...  10.2 us
    all_gather x1, waiting for transfers between devices, on_device(): book_here = lax.all_gather(own_slice, 'dp', axis=0, tiled=True)  7.29 us
  transfers between devices with their start and end apart: 9, of which 5 were waited for; matrix products, arithmetic and copies ran while one was open for 16% of the time, Pallas kernels for 0%

profile of v1, /device:TPU:1, one launch (start us, length us, event | category | flops | bytes accessed | tf_op | source)
XLA Modules:
  0.0 219.9 jit_solution(9127279218389113727)
XLA Ops:
  7.2 1.1 copy-done
  8.2 1.8 convolution_convert_fusion
  10.1 41.4 %all_to_all.40 = bf16[16,48,768]{2,1,0:T(8,128)(2,1)S(1)} all-to-all(bf16[16,48,768]{2,1,0:T(8,128)(2,1)S(1)} %bitcast.111), channel_id=1, replica_groups=mesh['dp'=16,'section'=2,'tensor'=8] {'dp'}, dimensions={0} | all-to-all | bytes 2359296 | tf_op jit(solution)/shard_map/all_to_all | solution.py:19
  51.6 1.1 broadcast_in_dim.82
  52.7 6.3 %all-to-all-start.1 = ((bf16[16,48,768]{2,1,0:T(8,128)(2,1)}), bf16[16,48,768]{2,1,0:T(8,128)(2,1)S(1)}, u32[]{:S(2)}, u32[]{:S(2)}) async-start(bf16[16,48,768]{2,1,0:T(8,128)(2,1)} %broadcast_in_dim.82), calls=%async_computation.1 | async-start | bytes 2359296 | tf_op jit(solution)/shard_map/all_to_all | solution.py:19
  59.1 0.6 constant_dynamic-slice_fusion.2
  60.9 0.9 fusion.29
  62.1 28.1 %all-to-all-done.1 = bf16[16,48,768]{2,1,0:T(8,128)(2,1)S(1)} async-done(((bf16[16,48,768]{2,1,0:T(8,128)(2,1)}), bf16[16,48,768]{2,1,0:T(8,128)(2,1)S(1)}, u32[]{:S(2)}, u32[]{:S(2)}) %all-to-all-start.1) | async-done | bytes 1179680 | tf_op jit(solution)/shard_map/all_to_all | solution.py:19
  90.2 1.0 convolution_convert_fusion.7
  91.3 4.0 %all-to-all-start.2 = ((bf16[8,16,768]{2,1,0:T(8,128)(2,1)}), bf16[8,16,768]{2,1,0:T(8,128)(2,1)}, u32[]{:S(2)}, u32[]{:S(2)}) async-start(bf16[8,16,768]{2,1,0:T(8,128)(2,1)} %bitcast.15), calls=%async_computation.2 | async-start | bytes 393216 | tf_op jit(solution)/shard_map/all_to_all | solution.py:19
  95.3 1.9 copy.87
  97.2 2.6 %copy.78 = bf16[1,1,128,6144]{2,3,1,0:T(8,128)(2,1)} copy(bf16[1,1,128,6144]{3,2,1,0:T(8,128)(2,1)} %param.11) | data formatting | bytes 3145728 | tf_op args[0]
  99.8 1.8 dynamic-slice_convert_fusion
  101.6 1.6 reduce_sum.132
  103.2 1.4 broadcast_in_dim.83
  104.6 5.1 %all-to-all-start.3 = ((bf16[8,16,768]{2,1,0:T(8,128)(2,1)}), bf16[8,16,768]{2,1,0:T(8,128)(2,1)}, u32[]{:S(2)}, u32[]{:S(2)}) async-start(bf16[8,16,768]{2,1,0:T(8,128)(2,1)} %broadcast_in_dim.83), calls=%async_computation.3 | async-start | bytes 393216 | tf_op jit(solution)/shard_map/all_to_all | solution.py:19
  109.7 1.7 bitcast_convert_fusion
  111.4 1.9 copy.88
  113.3 1.9 copy.86
  115.2 0.7 copy.117
  116.0 0.7 copy.118
  116.7 0.7 constant_dynamic-slice_fusion
  117.6 7.3 %all-gather.3.cloned.1.call-done = bf16[1,768,768]{2,1,0:T(8,128)(2,1)} async-done(((bf16[1,48,768]{2,1,0:T(8,128)(2,1)}), bf16[1,768,768]{2,1,0:T(8,128)(2,1)}) %all-gather.3.cloned.1.call-update) | async-done | bytes 1179664 | tf_op jit(solution)/shard_map/all_gather | solution.py:87
  124.9 2.1 fusion.30
  127.0 1.3 multiply_reduce_fusion.3
  128.3 0.6 broadcast_in_dim.84
  128.9 4.8 %all-to-all-start.4 = ((f32[8,4,128]{2,1,0:T(4,128)}), f32[8,4,128]{2,1,0:T(4,128)}, u32[]{:S(2)}, u32[]{:S(2)}) async-start(f32[8,4,128]{2,1,0:T(4,128)} %broadcast_in_dim.84), calls=%async_computation.4 | async-start | bytes 32768 | tf_op jit(solution)/shard_map/all_to_all | solution.py:19
  133.8 5.1 %all-to-all-done.4 = f32[8,4,128]{2,1,0:T(4,128)} async-done(((f32[8,4,128]{2,1,0:T(4,128)}), f32[8,4,128]{2,1,0:T(4,128)}, u32[]{:S(2)}, u32[]{:S(2)}) %all-to-all-start.4) | async-done | bytes 16416 | tf_op jit(solution)/shard_map/all_to_all | solution.py:19
  138.9 1.5 fusion.28
  140.4 0.5 reduce_sum.137
  140.9 1.2 broadcast_multiply_fusion.1
  142.1 0.5 reduce_sum.139
  142.6 0.7 broadcast_multiply_fusion
  143.2 0.7 fusion.24
  144.0 1.2 multiply_convert_fusion
  145.2 0.3 fusion.12
  145.5 0.4 fusion.9
  146.0 10.4 %all_to_all.41 = bf16[8,16,2304]{2,1,0:T(8,128)(2,1)S(1)} all-to-all(bf16[8,16,2304]{2,1,0:T(8,128)(2,1)S(1)} %bitcast.114), channel_id=1, replica_groups=mesh['dp'=16,'section'=2,'tensor'=8] {'tensor'}, dimensions={0} | all-to-all | bytes 1179648 | tf_op jit(solution)/shard_map/all_to_all | solution.py:19
  156.4 0.8 broadcast_in_dim.85
  157.2 3.5 %all-to-all-start.6 = ((bf16[8,16,1536]{2,1,0:T(8,128)(2,1)}), bf16[8,16,1536]{2,1,0:T(8,128)(2,1)S(1)}, u32[]{:S(2)}, u32[]{:S(2)}) async-start(bf16[8,16,1536]{2,1,0:T(8,128)(2,1)} %broadcast_in_dim.85), calls=%async_computation.6 | async-start | bytes 786432 | tf_op jit(solution)/shard_map/all_to_all | solution.py:19
  160.7 3.9 %collective-permute-start = (s32[1]{0:T(128)}, s32[1]{0:T(128)}, u32[]{:S(2)}, u32[]{:S(2)}) collective-permute-start(s32[1]{0:T(128)} %bitcast), channel_id=1, source_target_pairs={{0,8},{8,0},{1,9},{9,1},{2,10},{10,2},{3,11},{11,3},{4,12},{12,4},... | collective-permute-start | bytes 20 | tf_op jit(solution)/shard_map/ppermute | solution.py:15
  164.6 0.6 dynamic-slice.1
  165.2 0.4 collective-permute-done
  168.1 1.4 dynamic-update-slice
  169.5 12.3 %all-reduce = s32[16]{0:T(128)S(1)} all-reduce(s32[16]{0:T(128)S(1)} %dynamic-update-slice), channel_id=1, replica_groups=mesh['dp'=16,'section'=2,'tensor'=8] {'dp'}, use_global_device_ids=true, to_apply=%add | all-reduce | flops 16 | bytes 128
  181.8 0.7 slice.40
  182.5 1.5 reshape.148
  184.1 0.3 copy.116
  184.4 1.5 broadcast_in_dim_reshape.3
  185.9 0.6 gather_fusion
  186.5 0.8 broadcast_select_fusion
  187.4 4.1 %all-to-all-start.7 = ((bf16[16,16,768]{2,1,0:T(8,128)(2,1)}), bf16[16,16,768]{2,1,0:T(8,128)(2,1)S(1)}, u32[]{:S(2)}, u32[]{:S(2)}) async-start(bf16[16,16,768]{2,1,0:T(8,128)(2,1)} %broadcast_select_fusion), calls=%async_computation.7 | async-start | bytes 786432 | tf_op jit(solution)/shard_map/all_to_all | solution.py:19
  191.5 0.5 convolution_convert_fusion.6
  192.2 0.3 copy-done.3
  192.5 0.3 multiply_reduce_fusion
  193.0 1.4 convolution_convert_fusion.4
  194.5 1.4 convolution_convert_fusion.3
  195.9 6.4 %all-to-all-done.7 = bf16[16,16,768]{2,1,0:T(8,128)(2,1)S(1)} async-done(((bf16[16,16,768]{2,1,0:T(8,128)(2,1)}), bf16[16,16,768]{2,1,0:T(8,128)(2,1)S(1)}, u32[]{:S(2)}, u32[]{:S(2)}) %all-to-all-start.7) | async-done | bytes 393248 | tf_op jit(solution)/shard_map/all_to_all | solution.py:19
  202.3 6.2 %collective-permute-start.1 = (bf16[16,768]{1,0:T(8,128)(2,1)S(1)}, bf16[16,768]{1,0:T(8,128)(2,1)S(1)}, u32[]{:S(2)}, u32[]{:S(2)}) collective-permute-start(bf16[16,768]{1,0:T(8,128)(2,1)S(1)} %dynamic-slice_bitcast_fusion), channel_id=1, source_target_pairs={{0,8},{8,0},{1,9},{9,1},{2,10},{10,2},{3,11},{11,3},{4,12},{12,4},... | collective-permute-start | bytes 73736 | tf_op jit(solution)/shard_map/ppermute | solution.py:15
  208.6 1.4 convolution_convert_fusion.2
  210.0 0.8 copy.98
  210.8 0.8 copy.99
  211.6 0.8 copy.100
  212.5 0.6 copy.121
  (69 shorter events, 2.5 us)
Async XLA Ops:
  7.2 1.1 copy-start
  52.7 7.1 %copy-start.8 = (bf16[1,1,128,768]{3,2,1,0:T(8,128)(2,1)S(1)}, bf16[1,1,128,768]{3,2,1,0:T(8,128)(2,1)}, u32[]{:S(2)}) copy-start(bf16[1,1,128,768]{3,2,1,0:T(8,128)(2,1)} %param.14) | copy-start | bytes 589828
  52.7 7.2 %copy-start.9 = (bf16[1,1,128,768]{3,2,1,0:T(8,128)(2,1)S(1)}, bf16[1,1,128,768]{3,2,1,0:T(8,128)(2,1)}, u32[]{:S(2)}) copy-start(bf16[1,1,128,768]{3,2,1,0:T(8,128)(2,1)} %param.12) | copy-start | bytes 589828
  52.7 7.4 %copy-start.10 = (bf16[1,1,128,768]{3,2,1,0:T(8,128)(2,1)S(1)}, bf16[1,1,128,768]{3,2,1,0:T(8,128)(2,1)}, u32[]{:S(2)}) copy-start(bf16[1,1,128,768]{3,2,1,0:T(8,128)(2,1)} %param.13) | copy-start | bytes 589828
  52.7 37.5 %all-to-all-start.1 = ((bf16[16,48,768]{2,1,0:T(8,128)(2,1)}), bf16[16,48,768]{2,1,0:T(8,128)(2,1)S(1)}, u32[]{:S(2)}, u32[]{:S(2)}) async-start(bf16[16,48,768]{2,1,0:T(8,128)(2,1)} %broadcast_in_dim.82), calls=%async_computation.1 | async-start | bytes 2359296 | tf_op jit(solution)/shard_map/all_to_all | solution.py:19
  59.0 1.3 copy-start.17
  59.1 65.9 %all-gather.3.cloned.1.call-start = ((), (), s32[]{:S(2)}) async-start(), calls=%async_computation.8 | async-start | bytes 1253376 | tf_op jit(solution)/shard_map/all_gather | solution.py:87
  60.1 1.9 copy-start.4
  60.3 1.8 copy-start.6
  60.7 1.2 copy-start.11
  60.9 1.2 copy-start.2
  61.8 29.5 %copy-start.14 = (f32[6,128]{1,0:T(8,128)}, f32[6,128]{1,0:T(8,128)S(1)}, u32[]{:S(2)}) copy-start(f32[6,128]{1,0:T(8,128)S(1)} %get-tuple-element.41) | copy-start | bytes 9220
  91.3 10.3 %all-to-all-start.2 = ((bf16[8,16,768]{2,1,0:T(8,128)(2,1)}), bf16[8,16,768]{2,1,0:T(8,128)(2,1)}, u32[]{:S(2)}, u32[]{:S(2)}) async-start(bf16[8,16,768]{2,1,0:T(8,128)(2,1)} %bitcast.15), calls=%async_computation.2 | async-start | bytes 393216 | tf_op jit(solution)/shard_map/all_to_all | solution.py:19
  104.6 20.3 %all-to-all-start.3 = ((bf16[8,16,768]{2,1,0:T(8,128)(2,1)}), bf16[8,16,768]{2,1,0:T(8,128)(2,1)}, u32[]{:S(2)}, u32[]{:S(2)}) async-start(bf16[8,16,768]{2,1,0:T(8,128)(2,1)} %broadcast_in_dim.83), calls=%async_computation.3 | async-start | bytes 393216 | tf_op jit(solution)/shard_map/all_to_all | solution.py:19
  124.9 8.8 %copy-start.13 = (f32[1,16,48]{2,1,0:T(8,128)S(1)}, f32[1,16,48]{2,1,0:T(8,128)}, u32[]{:S(2)}) copy-start(f32[1,16,48]{2,1,0:T(8,128)} %get-tuple-element.49) | copy-start | bytes 9220
  127.0 18.2 %copy-start.1 = (bf16[1,768,768]{2,1,0:T(8,128)(2,1)S(1)}, bf16[1,768,768]{2,1,0:T(8,128)(2,1)}, u32[]{:S(2)}) copy-start(bf16[1,768,768]{2,1,0:T(8,128)(2,1)} %all-gather.3.cloned.1.call-done) | copy-start | bytes 3538948
  128.9 9.9 %all-to-all-start.4 = ((f32[8,4,128]{2,1,0:T(4,128)}), f32[8,4,128]{2,1,0:T(4,128)}, u32[]{:S(2)}, u32[]{:S(2)}) async-start(f32[8,4,128]{2,1,0:T(4,128)} %broadcast_in_dim.84), calls=%async_computation.4 | async-start | bytes 32768 | tf_op jit(solution)/shard_map/all_to_all | solution.py:19
  144.0 1.5 copy-start.16
  146.0 18.6 %copy-start.18 = (u32[256]{0:T(256)S(1)}, u32[256]{0:T(256)}, u32[]{:S(2)}) copy-start(u32[256]{0:T(256)} %constant.102) | copy-start | bytes 3076
  146.0 19.2 %copy-start.15 = (f32[6,128]{1,0:T(8,128)S(1)}, f32[6,128]{1,0:T(8,128)}, u32[]{:S(2)}) copy-start(f32[6,128]{1,0:T(8,128)} %copy-done.14) | copy-start | bytes 9220
  157.2 28.7 %all-to-all-start.6 = ((bf16[8,16,1536]{2,1,0:T(8,128)(2,1)}), bf16[8,16,1536]{2,1,0:T(8,128)(2,1)S(1)}, u32[]{:S(2)}, u32[]{:S(2)}) async-start(bf16[8,16,1536]{2,1,0:T(8,128)(2,1)} %broadcast_in_dim.85), calls=%async_computation.6 | async-start | bytes 786432 | tf_op jit(solution)/shard_map/all_to_all | solution.py:19
  160.7 4.9 %collective-permute-start = (s32[1]{0:T(128)}, s32[1]{0:T(128)}, u32[]{:S(2)}, u32[]{:S(2)}) collective-permute-start(s32[1]{0:T(128)} %bitcast), channel_id=1, source_target_pairs={{0,8},{8,0},{1,9},{9,1},{2,10},{10,2},{3,11},{11,3},{4,12},{12,4},... | collective-permute-start | bytes 20 | tf_op jit(solution)/shard_map/ppermute | solution.py:15
  187.4 15.0 %all-to-all-start.7 = ((bf16[16,16,768]{2,1,0:T(8,128)(2,1)}), bf16[16,16,768]{2,1,0:T(8,128)(2,1)S(1)}, u32[]{:S(2)}, u32[]{:S(2)}) async-start(bf16[16,16,768]{2,1,0:T(8,128)(2,1)} %broadcast_select_fusion), calls=%async_computation.7 | async-start | bytes 786432 | tf_op jit(solution)/shard_map/all_to_all | solution.py:19
  191.5 1.0 copy-start.3
  192.1 1.0 copy-start.7
  192.1 1.0 copy-start.12
  192.8 1.7 copy-start.5
  202.3 10.1 %collective-permute-start.1 = (bf16[16,768]{1,0:T(8,128)(2,1)S(1)}, bf16[16,768]{1,0:T(8,128)(2,1)S(1)}, u32[]{:S(2)}, u32[]{:S(2)}) collective-permute-start(bf16[16,768]{1,0:T(8,128)(2,1)S(1)} %dynamic-slice_bitcast_fusion), channel_id=1, source_target_pairs={{0,8},{8,0},{1,9},{9,1},{2,10},{10,2},{3,11},{11,3},{4,12},{12,4},... | collective-permute-start | bytes 73736 | tf_op jit(solution)/shard_map/ppermute | solution.py:15
Sparse Core Ops, SparseCore 0:
  62.9 61.9 all-gather.2

commit v2 on v1

v2 whole, which is shorter than its diff:
```python
import jax
import jax.numpy as jnp
from jax import lax
from jax.experimental import pallas as pl
from jax.experimental.pallas import tpu as pltpu
from jax.sharding import PartitionSpec as P

HEAD = 128
L = 128
BLK = 32


EPSILON = 1e-05
N_HIGH = 4
N_LOW = 4
EXTRA_ROWS = 16
VMEM_BYTES = 40 * 1024 * 1024
HIGH_GROUPS = [[z * N_LOW + y for z in range(N_HIGH)] for y in range(N_LOW)]
LOW_GROUPS = [[z * N_LOW + y for y in range(N_LOW)] for z in range(N_HIGH)]


def swapped_2(value, axis, distance):
    return lax.ppermute(value, axis, [(i, i ^ 1 << distance) for i in range(lax.axis_size(axis))])


def exchanged(value, axis, groups=None):
    return lax.all_to_all(value, axis, 0, 0, axis_index_groups=groups)


def turned(value, high, low):
    pairs = [
        (z * N_LOW + y, (z + high) % N_HIGH * N_LOW + (y + low) % N_LOW)
        for z in range(N_HIGH)
        for y in range(N_LOW)
    ]
    return lax.ppermute(value, "dp", pairs)


def transposed_owner(value, count):
    pairs = [
        ((half * count + d) * count + t, (half * count + t) * count + d)
        for half in range(2)
        for d in range(count)
        for t in range(count)
    ]
    return lax.ppermute(value, ("dp", "tensor"), pairs)


def summed(pieces):
    return jnp.sum(pieces.astype(jnp.float32), axis=0).astype(jnp.bfloat16)


def copies_of(value, count):
    return jnp.broadcast_to(value[None], (count,) + value.shape)


def allowed_pairs(mask_blocks):
    block_table = jnp.repeat(jnp.repeat(mask_blocks, BLK, axis=0), BLK, axis=1) == 1
    position = lax.broadcasted_iota(jnp.int32, (L, L), 0)
    column = lax.broadcasted_iota(jnp.int32, (L, L), 1)
    return block_table & (position >= column)


def times(left_side, right_side):
    return jnp.dot(left_side, right_side, preferred_element_type=jnp.float32)


def times_transposed(left_side, right_side):
    return lax.dot_general(
        left_side, right_side, (((1,), (1,)), ((), ())), preferred_element_type=jnp.float32
    )


def transposed_times(left_side, right_side):
    return lax.dot_general(
        left_side, right_side, (((0,), (0,)), ((), ())), preferred_element_type=jnp.float32
    )


def call(kernel, *shapes, flops=1):
    return pl.pallas_call(
        kernel,
        out_shape=[jax.ShapeDtypeStruct(shape, dtype) for shape, dtype in shapes],
        cost_estimate=pl.CostEstimate(flops=flops, bytes_accessed=4_000_000, transcendentals=0),
        compiler_params=pltpu.CompilerParams(vmem_limit_bytes=VMEM_BYTES),
    )


def placed_call(kernel, count, *shapes):
    return pl.pallas_call(
        kernel,
        out_shape=[jax.ShapeDtypeStruct(shape, dtype) for shape, dtype in shapes],
        in_specs=[pl.BlockSpec(memory_space=pltpu.SMEM)]
        + [pl.BlockSpec(memory_space=pltpu.VMEM)] * (count - 1),
        cost_estimate=pl.CostEstimate(flops=1, bytes_accessed=4_000_000, transcendentals=0),
        compiler_params=pltpu.CompilerParams(vmem_limit_bytes=VMEM_BYTES),
    )


def attend_kernel(query_ref, key_ref, value_ref, allowed_ref, context_ref, chance_ref):
    allowed = allowed_ref[...] > 0.5
    for head in range(query_ref.shape[1] // HEAD):
        columns = slice(head * HEAD, (head + 1) * HEAD)
        scores = times_transposed(query_ref[:, columns], key_ref[:, columns]) * HEAD ** (-0.5)
        scores = jnp.where(allowed, scores, -1e30)
        raised = jnp.exp(scores - jnp.max(scores, axis=-1, keepdims=True))
        chances = raised / jnp.sum(raised, axis=-1, keepdims=True)
        chance_ref[head] = chances
        mixture = times(chances.astype(jnp.bfloat16), value_ref[:, columns])
        context_ref[:, columns] = mixture.astype(jnp.bfloat16)


def code_kernel(context_ref, joined_ref, out_ref):
    code = times(context_ref[...], joined_ref[...]).astype(jnp.bfloat16)
    for copy in range(out_ref.shape[0]):
        out_ref[copy] = code


def feature_kernel(parts_ref, book_ref, residual_ref, gain_ref, scaled_ref, out_ref):
    total = parts_ref[0].astype(jnp.float32)
    for part in range(1, parts_ref.shape[0]):
        total += parts_ref[part].astype(jnp.float32)
    book = book_ref[...]
    width = book.shape[1]
    decoded = times_transposed(total.astype(jnp.bfloat16), book)
    hidden = residual_ref[...] + decoded
    out_ref[:, 3 * width :] = decoded.astype(jnp.bfloat16)
    out_ref[:, :width] = times(hidden.astype(jnp.bfloat16), book).astype(jnp.bfloat16)
    gained = (hidden * gain_ref[...]).astype(jnp.bfloat16)
    out_ref[:, width : 2 * width] = times(gained, book).astype(jnp.bfloat16)
    out_ref[:, 2 * width : 3 * width] = scaled_ref[...]


def row_kernel(arrived_ref, residual_ref, scaled_ref, sums_ref, both_ref, grad_ref):
    count = arrived_ref.shape[0]
    width = sums_ref.shape[1]
    size = residual_ref.shape[1]
    part = size // count // 2
    total = arrived_ref[0, :, : 3 * width].astype(jnp.float32)
    for rank in range(1, count):
        total += arrived_ref[rank, :, : 3 * width].astype(jnp.float32)
    hidden_code = total[:, :width]
    gained_code = total[:, width : 2 * width]
    scaled_code = total[:, 2 * width :]
    decoded = [
        arrived_ref[rank, :, 3 * width + half * part : 3 * width + (half + 1) * part]
        for half in range(2)
        for rank in range(count)
    ]
    hidden = residual_ref[...] + jnp.concatenate(decoded, axis=1).astype(jnp.float32)
    mean = jnp.sum(hidden, axis=-1, keepdims=True) / size
    centered = hidden - mean
    variance = jnp.sum(centered * centered, axis=-1, keepdims=True) / size
    inv_std = lax.rsqrt(variance + EPSILON)
    scaled = scaled_ref[...]
    product = jnp.sum(scaled * centered, axis=-1, keepdims=True) / size
    share = inv_std * inv_std * product
    grad_ref[...] = (inv_std * (scaled - centered * share)).astype(jnp.bfloat16)
    ones_sum, gain_sum, bias_sum = sums_ref[0:1], sums_ref[1:2], sums_ref[2:3]
    codes = inv_std * (gained_code - mean * gain_sum) + bias_sum
    grad_code = inv_std * (scaled_code - share * (hidden_code - mean * ones_sum))
    for copy in range(count):
        both_ref[copy, :, :width] = codes.astype(jnp.bfloat16)
        both_ref[copy, :, width:] = grad_code.astype(jnp.bfloat16)


def slot_kernel(order_ref, both_ref, slots_ref):
    width = slots_ref.shape[2]
    for slot in range(slots_ref.shape[0]):
        slots_ref[slot] = both_ref[order_ref[slot], :, :width]


def back_kernel(
    both_ref,
    joined_ref,
    query_ref,
    key_ref,
    value_ref,
    chance_ref,
    grad_query_ref,
    grad_key_ref,
    grad_value_ref,
):
    length, width = query_ref.shape
    code_width = joined_ref.shape[1]
    grad_code = both_ref[:, :, code_width:].reshape(length, code_width)
    for head in range(width // HEAD):
        columns = slice(head * HEAD, (head + 1) * HEAD)
        grad_context = times_transposed(grad_code, joined_ref[columns]).astype(jnp.bfloat16)
        chances = chance_ref[head]
        grad_value = transposed_times(chances.astype(jnp.bfloat16), grad_context)
        grad_value_ref[:, columns] = grad_value.astype(jnp.bfloat16)
        grad_chances = times_transposed(grad_context, value_ref[:, columns])
        grad_chances = grad_chances.astype(jnp.bfloat16).astype(jnp.float32)
        shift = jnp.sum(grad_chances * chances, axis=-1, keepdims=True)
        grad_scores = chances * (grad_chances - shift) * HEAD ** (-0.5)
        grad_scores = grad_scores.astype(jnp.bfloat16)
        grad_query = times(grad_scores, key_ref[:, columns])
        grad_query_ref[:, columns] = grad_query.astype(jnp.bfloat16)
        grad_key = transposed_times(grad_scores, query_ref[:, columns])
        grad_key_ref[:, columns] = grad_key.astype(jnp.bfloat16)


def extra_kernel(places_ref, book_ref, gain_ref, bias_ref, out_ref):
    shard = book_ref.shape[0]
    columns = pl.ds(pl.multiple_of(places_ref[1] * shard, HEAD), shard)
    row = lax.broadcasted_iota(jnp.int32, (EXTRA_ROWS, shard), 0)
    weights = jnp.where(row == 0, 1.0, jnp.where(row == 1, gain_ref[:, columns], 0.0))
    rest = jnp.where(row == 2, bias_ref[:, columns], weights)
    book = book_ref[...]
    total = jnp.zeros((EXTRA_ROWS, book.shape[1]), jnp.float32)
    for _ in range(3):
        top = rest.astype(jnp.bfloat16)
        rest = rest - top.astype(jnp.float32)
        total += times(top, book)
    high = total.astype(jnp.bfloat16).astype(jnp.float32)
    low = pltpu.roll(total - high, 3, 0)
    row = lax.broadcasted_iota(jnp.int32, total.shape, 0)
    wanted = places_ref[2].astype(jnp.float32)
    both = jnp.where(row < 3, high, jnp.where(row < 6, low, jnp.where(row == 6, wanted, 0.0)))
    out_ref[...] = both.astype(jnp.bfloat16)


def prepare_kernel(
    places_ref,
    residual_ref,
    upstream_ref,
    gain_ref,
    residual_here_ref,
    scaled_here_ref,
    gain_here_ref,
    residual_rows_ref,
    scaled_rows_ref,
):
    length = residual_ref.shape[0]
    rows, width = residual_rows_ref.shape
    part = gain_here_ref.shape[1] // 2
    rank = places_ref[0]
    gain = gain_ref[...]

    def centered(ref, start, scale):
        wide = ref[pl.ds(start, rows), :].astype(jnp.float32)
        wide = wide if scale is None else wide * scale
        return wide - jnp.sum(wide, axis=-1, keepdims=True) / width

    def places(half):
        start = pl.multiple_of((rank + half * (width // part // 2)) * part, HEAD)
        return slice(half * part, (half + 1) * part), pl.ds(start, part)

    for half in range(2):
        here, there = places(half)
        gain_here_ref[:, here] = gain_ref[:, there]
    for start in range(0, length, rows):
        block = slice(start, start + rows)
        wide = residual_ref[block, :].astype(jnp.float32)
        mean = jnp.sum(wide, axis=-1, keepdims=True) / width
        wide = upstream_ref[block, :].astype(jnp.float32) * gain
        scaled_mean = jnp.sum(wide, axis=-1, keepdims=True) / width
        for half in range(2):
            here, there = places(half)
            residual_here_ref[block, here] = residual_ref[block, there].astype(jnp.float32) - mean
            scaled = upstream_ref[block, there].astype(jnp.float32) * gain_ref[:, there]
            scaled_here_ref[block, here] = (scaled - scaled_mean).astype(jnp.bfloat16)
    own = pl.multiple_of(rank * rows, rows)
    residual_rows_ref[...] = centered(residual_ref, own, None)
    scaled_rows_ref[...] = centered(upstream_ref, own, gain)


def assemble_kernel(places_ref, *refs):
    column_refs, (scaled_ref, book_ref, scaled_code_ref, sums_ref, order_ref) = refs[:-5], refs[-5:]
    piece = book_ref.shape[1]
    high, low = places_ref[1] // N_LOW, places_ref[1] % N_LOW
    total = jnp.zeros((EXTRA_ROWS, book_ref.shape[2]), jnp.float32)
    for low_step, column_ref in enumerate(column_refs):
        for high_step in range(N_HIGH):
            place = (high + N_HIGH - high_step) % N_HIGH * N_LOW + (low + N_LOW - low_step) % N_LOW
            book_ref[place] = column_ref[high_step, :piece]
            extra = column_ref[high_step, piece:].astype(jnp.float32)
            order_ref[place] = extra[:, :HEAD]
            total += extra
    sums_ref[...] = total + pltpu.roll(total, EXTRA_ROWS - 3, 0)
    book = book_ref[...].reshape(-1, book_ref.shape[2])
    scaled_code_ref[...] = times(scaled_ref[...], book).astype(jnp.bfloat16)


def on_device(
    residual,
    queries,
    key_vectors,
    value_vectors,
    block_mask,
    out_weight,
    codebook,
    norm_gain,
    norm_bias,
    receiver_order,
    upstream,
):
    n_dp = lax.axis_size("dp")
    n_tensor = lax.axis_size("tensor")
    rank = lax.axis_index("tensor")
    dp_rank = lax.axis_index("dp")
    length, width = residual.shape[2:]
    code_book = codebook[0]
    shard, code_width = code_book.shape
    piece = shard // n_tensor
    rows = length // n_tensor
    features = n_dp * piece
    heads = queries.shape[3] // HEAD
    bf16, f32 = jnp.bfloat16, jnp.float32

    joined_part = times(out_weight[0], code_book).astype(bf16)
    joined_part = joined_part.reshape(N_LOW, -1, code_width)
    joined_rows = summed(exchanged(joined_part, "dp", LOW_GROUPS))

    own_slice = lax.dynamic_slice_in_dim(code_book, rank * piece, piece, 0)
    own_slice = transposed_owner(own_slice, n_tensor)
    wanted = swapped_2(receiver_order[0], "section", 0)
    places = jnp.stack([rank, dp_rank, wanted[0]])
    extra = placed_call(extra_kernel, 4, ((EXTRA_ROWS, code_width), bf16))(
        places, code_book, norm_gain, norm_bias
    )[0]
    payload = jnp.concatenate([own_slice, extra], axis=0)
    column = jnp.stack([payload] + [turned(payload, step, 0) for step in range(1, N_HIGH)])
    residual, upstream, queries, key_vectors, value_vectors, joined_rows = lax.optimization_barrier(
        (residual, upstream, queries, key_vectors, value_vectors, joined_rows)
    )

    joined_rows = joined_rows.reshape(N_HIGH, -1, code_width)
    joined_rows = summed(exchanged(joined_rows, "dp", HIGH_GROUPS))
    joined_rows = exchanged(copies_of(joined_rows, N_HIGH), "dp", HIGH_GROUPS)
    columns = [column] + [turned(column, 0, step) for step in range(1, N_LOW)]
    joined_rows = joined_rows.reshape(-1, code_width)
    joined = exchanged(copies_of(joined_rows, N_LOW), "dp", LOW_GROUPS)
    joined = joined.reshape(-1, code_width)

    allowed = allowed_pairs(block_mask[0, 0]).astype(f32)
    query_rows = queries[0, 0]
    key_rows = key_vectors[0, 0]
    value_rows = value_vectors[0, 0]
    context, chances = call(
        attend_kernel, ((length, heads * HEAD), bf16), ((heads, length, length), f32)
    )(query_rows, key_rows, value_rows, allowed)
    residual_here, scaled_here, gain_here, residual_rows, scaled_rows = placed_call(
        prepare_kernel,
        4,
        ((length, features), f32),
        ((length, features), bf16),
        ((1, features), f32),
        ((rows, width), f32),
        ((rows, width), f32),
    )(places, residual[0, 0], upstream[0, 0], norm_gain)
    book_here, scaled_code, sums, orders = placed_call(
        assemble_kernel,
        N_LOW + 2,
        ((n_dp, piece, code_width), bf16),
        ((length, code_width), bf16),
        ((EXTRA_ROWS, code_width), f32),
        ((n_dp, EXTRA_ROWS, HEAD), f32),
    )(places, *columns, scaled_here)
    book_here = book_here.reshape(features, code_width)
    wanted_all = orders[:, 6, 0].astype(jnp.int32) % n_tensor

    ready = (joined, context, book_here, residual_here, gain_here, scaled_code)
    ready += (residual_rows, scaled_rows, sums, chances, wanted_all)
    ready = lax.optimization_barrier(ready)
    joined, context, book_here, residual_here, gain_here, scaled_code = ready[:6]
    residual_rows, scaled_rows, sums, chances, wanted_all = ready[6:]

    (code_copies,) = call(code_kernel, ((n_tensor, length, code_width), bf16))(context, joined)
    code_parts = exchanged(code_copies, "tensor")
    (sent,) = call(feature_kernel, ((length, 3 * code_width + features), bf16))(
        code_parts, book_here, residual_here, gain_here, scaled_code
    )
    arrived = exchanged(sent.reshape(n_tensor, rows, -1), "tensor")
    both, grad_residual = call(
        row_kernel,
        ((n_tensor, rows, 2 * code_width), bf16),
        ((rows, width), bf16),
    )(arrived, residual_rows, scaled_rows, sums)
    both = exchanged(both, "tensor")

    (slots,) = placed_call(slot_kernel, 2, ((n_dp, rows, code_width), bf16))(wanted_all, both)
    routed = exchanged(slots, "dp")
    grad_query, grad_key, grad_value = call(
        back_kernel, *[((length, heads * HEAD), bf16)] * 3
    )(both, joined, query_rows, key_rows, value_rows, chances)
    routed, grad_query, grad_key, grad_value = lax.optimization_barrier(
        (routed, grad_query, grad_key, grad_value)
    )
    chosen = lax.dynamic_index_in_dim(routed, wanted[0] // n_tensor, 0, keepdims=False)
    received = swapped_2(chosen, "section", 0)
    return (
        received[None, None],
        grad_residual[None, None],
        grad_query[None, None],
        grad_key[None, None],
        grad_value[None, None],
    )


def solution(mesh):
    in_specs = (
        P("section", "dp", None, None),
        P("section", "dp", None, "tensor"),
        P("section", "dp", None, "tensor"),
        P("section", "dp", None, "tensor"),
        P("section", "dp", None, None),
        P("section", "tensor", "dp"),
        P("section", "dp", None),
        P("section", None),
        P("section", None),
        P("section", ("dp", "tensor")),
        P("section", "dp", None, None),
    )
    out_specs = (
        P("section", ("dp", "tensor"), None, None),
        P("section", "dp", "tensor", None),
        P("section", "dp", None, "tensor"),
        P("section", "dp", None, "tensor"),
        P("section", "dp", None, "tensor"),
    )
    return jax.shard_map(
        on_device, mesh=mesh, in_specs=in_specs, out_specs=out_specs, check_vma=False
    )
```

time: 221 us -> 187 us (0.85)
  waiting for transfers between devices: 47.3 us -> 24.9 us
  blocking collectives: 64.1 us -> 85.2 us
  local copies, waits for them, and re-layouts: 28.9 us -> 8.37 us
  Pallas kernels: 0 us -> 13.6 us
  between operations: 17 us -> 3.7 us
  other arithmetic: 13.4 us -> 3.87 us
  matrix products: 11.2 us -> 1.83 us
  starting transfers between devices: 38 us -> 44.6 us
    all_to_all x6 -> x3, waiting for transfers between devices: 39.6 us -> 4.38 us  [exchanged(): return lax.all_to_all(value, axis, 0, 0, axis_index_groups=groups)]
    all_to_all x2 -> x5, blocking collectives: 51.8 us -> 85.2 us  [exchanged(): return lax.all_to_all(value, axis, 0, 0, axis_index_groups=groups)]
    ppermute x0 -> x7, starting transfers between devices: none -> 21.5 us  [the longest x6 20.9 us: turned(): return lax.ppermute(value, 'dp', pairs)]
    ppermute x0 -> x7, waiting for transfers between devices: none -> 19.4 us  [the longest x6 19.4 us: turned(): return lax.ppermute(value, 'dp', pairs)]
    pallas_call x0 -> x9, Pallas kernels: none -> 13.6 us  [the longest x1 3.7 us: on_device(): call(back_kernel, *[((length, heads * HEAD), bf16)] * 3)]
    all_to_all x6 -> x3, starting transfers between devices: 27.8 us -> 14.3 us  [exchanged(): return lax.all_to_all(value, axis, 0, 0, axis_index_groups=groups)]
    unnamed x1 -> x0, blocking collectives: 12.3 us -> none
    dot_general x12 -> x1, matrix products: 11.2 us -> 1.83 us  [times(): return jnp.dot(left_side, right_side, preferred_element_type=jnp.float32)]
  transfers between devices with their start and end apart: 9 -> 12, of which waited for: 5 -> 6; matrix products, arithmetic and copies ran while one was open for 16% -> 3% of each run, Pallas kernels for 0% -> 5%
where the time goes in v2:
time: 187 us; the launch traced here: 186 us
  blocking collectives  85.2 us (46%)
  starting transfers between devices  44.6 us (24%)
  waiting for transfers between devices  24.9 us (13%)
  Pallas kernels  13.6 us (7%)
  local copies, waits for them, and re-layouts  8.37 us (4%)
  other arithmetic  3.87 us (2%)
  between operations  3.7 us (2%)
    all_to_all x5, blocking collectives, exchanged(): return lax.all_to_all(value, axis, 0, 0, axis_index_groups=groups)  85.2 us
    ppermute x6, starting transfers between devices, turned(): return lax.ppermute(value, 'dp', pairs)  20.9 us
    ppermute x6, waiting for transfers between devices, turned(): return lax.ppermute(value, 'dp', pairs)  19.4 us
    all_to_all x3, starting transfers between devices, exchanged(): return lax.all_to_all(value, axis, 0, 0, axis_index_groups=groups)  14.3 us
    ppermute x2, starting transfers between devices, swapped_2(): lax.ppermute(value, axis, [(i, i ^ 1 << distance) for i in range(lax.axis...  8.78 us
    unnamed x51, local copies, waits for them, and re-layouts  6.11 us
    all_to_all x3, waiting for transfers between devices, exchanged(): return lax.all_to_all(value, axis, 0, 0, axis_index_groups=groups)  4.38 us
  transfers between devices with their start and end apart: 12, of which 6 were waited for; matrix products, arithmetic and copies ran while one was open for 3% of the time, Pallas kernels for 5%

profile of v2, /device:TPU:1, one launch (start us, length us, event | category | flops | bytes accessed | tf_op | source)
XLA Modules:
  0.0 186.1 jit_solution(9530010351600728072)
XLA Ops:
  0.6 0.0 copy-start
  0.6 1.1 copy-done
  1.7 1.8 convolution_convert_fusion
  3.5 20.4 %all_to_all.40 = bf16[4,192,768]{2,1,0:T(8,128)(2,1)S(1)} all-to-all(bf16[4,192,768]{2,1,0:T(8,128)(2,1)S(1)} %bitcast.53), channel_id=1, replica_groups={{0,16,32,48},{64,80,96,112},{128,144,160,176},{192,208,224,240},{1,17,3..., dimensions={0} | all-to-all | bytes 2359296 | tf_op jit(solution)/shard_map/all_to_all | solution.py:27
  23.9 0.3 reduce_sum.24
  24.2 0.0 copy-start.1
  24.2 0.0 copy-start.19
  24.2 0.0 copy-start.23
  24.3 16.8 %all_to_all.41 = bf16[4,48,768]{2,1,0:T(8,128)(2,1)S(1)} all-to-all(bf16[4,48,768]{2,1,0:T(8,128)(2,1)S(1)} %bitcast.55), channel_id=1, replica_groups={{0,64,128,192},{16,80,144,208},{32,96,160,224},{48,112,176,240},{1,65,1..., dimensions={0} | all-to-all | bytes 589824 | tf_op jit(solution)/shard_map/all_to_all | solution.py:27
  41.1 0.7 broadcast_in_dim.34
  41.8 4.3 %all-to-all-start.2 = ((bf16[4,48,768]{2,1,0:T(8,128)(2,1)}), bf16[4,48,768]{2,1,0:T(8,128)(2,1)S(1)}, u32[]{:S(2)}, u32[]{:S(2)}) async-start(bf16[4,48,768]{2,1,0:T(8,128)(2,1)} %broadcast_in_dim.34), calls=%async_computation.2 | async-start | bytes 589824 | tf_op jit(solution)/shard_map/all_to_all | solution.py:27
  46.1 3.1 %collective-permute-start = (s32[1]{0:T(128)}, s32[1]{0:T(128)}, u32[]{:S(2)}, u32[]{:S(2)}) collective-permute-start(s32[1]{0:T(128)} %bitcast.13), channel_id=1, source_target_pairs={{0,8},{8,0},{1,9},{9,1},{2,10},{10,2},{3,11},{11,3},{4,12},{12,4},... | collective-permute-start | bytes 20 | tf_op jit(solution)/shard_map/ppermute | solution.py:23
  49.2 0.7 collective-permute-start.1
  49.9 0.3 collective-permute-done
  50.1 0.7 pad_add_fusion.places_ref
  50.9 0.9 shard_map.147
  51.8 0.0 collective-permute-done.1
  51.8 0.7 fusion.5
  52.5 5.5 %collective-permute-start.3 = (bf16[64,768]{1,0:T(8,128)(2,1)}, bf16[64,768]{1,0:T(8,128)(2,1)S(1)}, u32[]{:S(2)}, u32[]{:S(2)}) collective-permute-start(bf16[64,768]{1,0:T(8,128)(2,1)} %get-tuple-element.80), channel_id=1, source_target_pairs={{0,128},{16,144},{32,160},{48,176},{64,192},{80,208},{96,224},{112... | collective-permute-start | bytes 294920 | tf_op jit(solution)/shard_map/ppermute | solution.py:36
  58.0 9.4 %collective-permute-start.2 = (bf16[64,768]{1,0:T(8,128)(2,1)}, bf16[64,768]{1,0:T(8,128)(2,1)}, u32[]{:S(2)}, u32[]{:S(2)}) collective-permute-start(bf16[64,768]{1,0:T(8,128)(2,1)} %get-tuple-element.80), channel_id=1, source_target_pairs={{0,64},{16,80},{32,96},{48,112},{64,128},{80,144},{96,160},{112,17... | collective-permute-start | bytes 294920 | tf_op jit(solution)/shard_map/ppermute | solution.py:36
  67.3 0.4 collective-permute-start.4
  67.7 0.0 all-to-all-done.2
  67.7 1.1 broadcast_in_dim.36
  68.9 5.5 %all-to-all-start.3 = ((bf16[4,192,768]{2,1,0:T(8,128)(2,1)}), bf16[4,192,768]{2,1,0:T(8,128)(2,1)S(1)}, u32[]{:S(2)}, u32[]{:S(2)}) async-start(bf16[4,192,768]{2,1,0:T(8,128)(2,1)} %broadcast_in_dim.36), calls=%async_computation.3 | async-start | bytes 2359296 | tf_op jit(solution)/shard_map/all_to_all | solution.py:27
  74.3 0.0 collective-permute-done.2
  74.4 0.0 collective-permute-done.4
  74.4 1.7 pad_maximum_fusion.refs_0_
  76.1 5.0 %collective-permute-start.7 = (bf16[4,64,768]{2,1,0:T(8,128)(2,1)}, bf16[4,64,768]{2,1,0:T(8,128)(2,1)}, u32[]{:S(2)}, u32[]{:S(2)}) collective-permute-start(bf16[4,64,768]{2,1,0:T(8,128)(2,1)} %pad_maximum_fusion.refs_0_), channel_id=1, source_target_pairs={{0,48},{16,0},{32,16},{48,32},{64,112},{80,64},{96,80},{112,96},{1... | collective-permute-start | bytes 1179656 | tf_op jit(solution)/shard_map/ppermute | solution.py:36
  81.1 0.6 collective-permute-start.5
  81.7 0.1 copy.18
  81.8 0.1 broadcast_in_dim.37
  81.9 0.1 eq.22
  82.0 0.1 copy.19
  82.1 0.0 copy-start.3
  82.2 1.4 copy-done.3
  83.6 0.7 copy-done.20
  84.3 1.3 shard_map.148
  85.7 2.0 %shard_map.146 = (bf16[128,768]{1,0:T(8,128)(2,1)S(1)}, f32[6,128,128]{2,1,0:T(8,128)S(1)}) custom-call(bf16[128,768]{1,0:T(8,128)(2,1)S(1)} %bitcast.47, bf16[128,768]{1,0:T(8,128)(2,1)S(1)} %bitcast.49, bf16[128,768]{1,0:T(8,128)(2,1)S(1)} %bitcast.51, f32[128,128]{1,0:T(8,128)S(1)} %fusion.2.allowed_ref), custom_call_target="tpu_custom_call" | custom-call | flops 1 | bytes 4000000 | tf_op jit(solution)/shard_map/pallas_call | solution.py:341
  87.8 0.0 copy-start.17
  87.8 8.1 %collective-permute-done.7.refs_3_ = bf16[4,64,768]{2,1,0:T(8,128)(2,1)} collective-permute-done((bf16[4,64,768]{2,1,0:T(8,128)(2,1)}, bf16[4,64,768]{2,1,0:T(8,128)(2,1)}, u32[]{:S(2)}, u32[]{:S(2)}) %collective-permute-start.7) | collective-permute-done | bytes 393248 | tf_op jit(solution)/shard_map/ppermute | solution.py:36
  95.9 1.5 collective-permute-done.6.refs_2_
  97.4 9.8 %collective-permute-done.5.refs_1_ = bf16[4,64,768]{2,1,0:T(8,128)(2,1)} collective-permute-done((bf16[4,64,768]{2,1,0:T(8,128)(2,1)}, bf16[4,64,768]{2,1,0:T(8,128)(2,1)}, u32[]{:S(2)}, u32[]{:S(2)}) %collective-permute-start.5) | collective-permute-done | bytes 393248 | tf_op jit(solution)/shard_map/ppermute | solution.py:36
  107.2 1.8 shard_map.149
  109.0 0.0 copy-start.15
  109.1 0.7 copy-done.15
  109.7 0.6 copy-done.21
  110.3 0.4 convert_reduce_fusion
  110.8 0.0 copy-start.18
  110.8 0.9 copy-done.18
  111.7 0.4 shard_map.150
  112.1 0.0 copy-start.16
  112.1 25.9 %all_to_all.42.parts_ref = bf16[8,128,768]{2,1,0:T(8,128)(2,1)S(1)} all-to-all(bf16[8,128,768]{2,1,0:T(8,128)(2,1)S(1)} %shard_map.150), channel_id=1, replica_groups=mesh['dp'=16,'section'=2,'tensor'=8] {'tensor'}, dimensions={0} | all-to-all | bytes 3145728 | tf_op jit(solution)/shard_map/all_to_all | solution.py:27
  138.0 1.1 shard_map.151
  139.1 0.0 copy-start.22
  139.1 12.7 %all_to_all.43.arrived_ref = bf16[8,16,3072]{2,1,0:T(8,128)(2,1)S(1)} all-to-all(bf16[8,16,3072]{2,1,0:T(8,128)(2,1)S(1)} %bitcast.42), channel_id=1, replica_groups=mesh['dp'=16,'section'=2,'tensor'=8] {'tensor'}, dimensions={0} | all-to-all | bytes 1572864 | tf_op jit(solution)/shard_map/all_to_all | solution.py:27
  151.8 1.0 shard_map.152
  152.8 9.5 %all_to_all.44.both_ref = bf16[8,16,1536]{2,1,0:T(8,128)(2,1)S(1)} all-to-all(bf16[8,16,1536]{2,1,0:T(8,128)(2,1)S(1)} %get-tuple-element.69), channel_id=1, replica_groups=mesh['dp'=16,'section'=2,'tensor'=8] {'tensor'}, dimensions={0} | all-to-all | bytes 786432 | tf_op jit(solution)/shard_map/all_to_all | solution.py:27
  162.3 1.3 shard_map.153
  163.6 4.5 %all-to-all-start.7 = ((bf16[16,16,768]{2,1,0:T(8,128)(2,1)}), bf16[16,16,768]{2,1,0:T(8,128)(2,1)S(1)}, u32[]{:S(2)}, u32[]{:S(2)}) async-start(bf16[16,16,768]{2,1,0:T(8,128)(2,1)} %shard_map.153), calls=%async_computation.7 | async-start | bytes 786432 | tf_op jit(solution)/shard_map/all_to_all | solution.py:27
  170.9 3.7 %shard_map.154 = (bf16[128,768]{1,0:T(8,128)(2,1)}, bf16[128,768]{1,0:T(8,128)(2,1)}, bf16[128,768]{1,0:T(8,128)(2,1)}) custom-call(bf16[8,16,1536]{2,1,0:T(8,128)(2,1)S(1)} %all_to_all.44.both_ref, bf16[768,768]{1,0:T(8,128)(2,1)S(1)} %bitcast.41, bf16[128,768]{1,0:T(8,128)(2,1)S(1)} %bitcast.48, bf16[128,768]{1,0:T(8,128)(2,1)S(1)} %bitcast.50, ...), custom_call_target="tpu_custom_call" | custom-call | flops 1 | bytes 4000000 | tf_op jit(solution)/shard_map/pallas_call | solution.py:385
  174.6 4.4 %all-to-all-done.7 = bf16[16,16,768]{2,1,0:T(8,128)(2,1)S(1)} async-done(((bf16[16,16,768]{2,1,0:T(8,128)(2,1)}), bf16[16,16,768]{2,1,0:T(8,128)(2,1)S(1)}, u32[]{:S(2)}, u32[]{:S(2)}) %all-to-all-start.7) | async-done | bytes 393248 | tf_op jit(solution)/shard_map/all_to_all | solution.py:27
  178.9 5.7 %collective-permute-start.8 = (bf16[16,768]{1,0:T(8,128)(2,1)S(1)}, bf16[16,768]{1,0:T(8,128)(2,1)S(1)}, u32[]{:S(2)}, u32[]{:S(2)}) collective-permute-start(bf16[16,768]{1,0:T(8,128)(2,1)S(1)} %dynamic-slice_bitcast_fusion.1), channel_id=1, source_target_pairs={{0,8},{8,0},{1,9},{9,1},{2,10},{10,2},{3,11},{11,3},{4,12},{12,4},... | collective-permute-start | bytes 73736 | tf_op jit(solution)/shard_map/ppermute | solution.py:23
  184.6 0.8 collective-permute-done.8
  185.5 0.6 copy.21
  (44 shorter events, 0.2 us)
Async XLA Ops:
  0.6 1.1 copy-start
  24.2 25.0 %copy-start.1 = (bf16[1,384,768]{2,1,0:T(8,128)(2,1)S(1)}, bf16[1,384,768]{2,1,0:T(8,128)(2,1)}, u32[]{:S(2)}) copy-start(bf16[1,384,768]{2,1,0:T(8,128)(2,1)} %param.17) | copy-start | bytes 1769476
  24.2 26.6 %copy-start.19 = (f32[1,6144]{1,0:T(1,128)S(1)}, f32[1,6144]{1,0:T(1,128)}, u32[]{:S(2)}) copy-start(f32[1,6144]{1,0:T(1,128)} %gain_ref.3) | copy-start | bytes 73732
  24.2 26.6 %copy-start.23 = (f32[1,6144]{1,0:T(1,128)S(1)}, f32[1,6144]{1,0:T(1,128)}, u32[]{:S(2)}) copy-start(f32[1,6144]{1,0:T(1,128)} %bias_ref.1) | copy-start | bytes 73732
  41.8 25.9 %all-to-all-start.2 = ((bf16[4,48,768]{2,1,0:T(8,128)(2,1)}), bf16[4,48,768]{2,1,0:T(8,128)(2,1)S(1)}, u32[]{:S(2)}, u32[]{:S(2)}) async-start(bf16[4,48,768]{2,1,0:T(8,128)(2,1)} %broadcast_in_dim.34), calls=%async_computation.2 | async-start | bytes 589824 | tf_op jit(solution)/shard_map/all_to_all | solution.py:27
  46.1 4.0 %collective-permute-start = (s32[1]{0:T(128)}, s32[1]{0:T(128)}, u32[]{:S(2)}, u32[]{:S(2)}) collective-permute-start(s32[1]{0:T(128)} %bitcast.13), channel_id=1, source_target_pairs={{0,8},{8,0},{1,9},{9,1},{2,10},{10,2},{3,11},{11,3},{4,12},{12,4},... | collective-permute-start | bytes 20 | tf_op jit(solution)/shard_map/ppermute | solution.py:23
  49.2 2.6 %collective-permute-start.1 = (bf16[48,768]{1,0:T(8,128)(2,1)S(1)}, bf16[48,768]{1,0:T(8,128)(2,1)S(1)}, u32[]{:S(2)}, u32[]{:S(2)}) collective-permute-start(bf16[48,768]{1,0:T(8,128)(2,1)S(1)} %dynamic-slice_bitcast_fusion), channel_id=1, source_target_pairs={{0,0},{1,16},{2,32},{3,48},{4,64},{5,80},{6,96},{7,112},{16,1},{17... | collective-permute-start | bytes 221192 | tf_op jit(solution)/shard_map/ppermute | solution.py:46
  52.5 21.9 %collective-permute-start.3 = (bf16[64,768]{1,0:T(8,128)(2,1)}, bf16[64,768]{1,0:T(8,128)(2,1)S(1)}, u32[]{:S(2)}, u32[]{:S(2)}) collective-permute-start(bf16[64,768]{1,0:T(8,128)(2,1)} %get-tuple-element.80), channel_id=1, source_target_pairs={{0,128},{16,144},{32,160},{48,176},{64,192},{80,208},{96,224},{112... | collective-permute-start | bytes 294920 | tf_op jit(solution)/shard_map/ppermute | solution.py:36
  58.0 16.4 %collective-permute-start.2 = (bf16[64,768]{1,0:T(8,128)(2,1)}, bf16[64,768]{1,0:T(8,128)(2,1)}, u32[]{:S(2)}, u32[]{:S(2)}) collective-permute-start(bf16[64,768]{1,0:T(8,128)(2,1)} %get-tuple-element.80), channel_id=1, source_target_pairs={{0,64},{16,80},{32,96},{48,112},{64,128},{80,144},{96,160},{112,17... | collective-permute-start | bytes 294920 | tf_op jit(solution)/shard_map/ppermute | solution.py:36
  67.3 7.0 %collective-permute-start.4 = (bf16[64,768]{1,0:T(8,128)(2,1)}, bf16[64,768]{1,0:T(8,128)(2,1)}, u32[]{:S(2)}, u32[]{:S(2)}) collective-permute-start(bf16[64,768]{1,0:T(8,128)(2,1)} %get-tuple-element.80), channel_id=1, source_target_pairs={{0,192},{16,208},{32,224},{48,240},{64,0},{80,16},{96,32},{112,48}... | collective-permute-start | bytes 294920 | tf_op jit(solution)/shard_map/ppermute | solution.py:36
  68.8 12.8 %copy-start.24 = (s32[1,1,4,4]{3,2,1,0:T(4,128)S(1)}, s32[1,1,4,4]{3,2,1,0:T(4,128)}, u32[]{:S(2)}) copy-start(s32[1,1,4,4]{3,2,1,0:T(4,128)} %param.15) | copy-start | bytes 196
  68.8 13.3 %copy-start.2 = (bf16[1,1,128,6144]{3,2,1,0:T(8,128)(2,1)S(1)}, bf16[1,1,128,6144]{3,2,1,0:T(8,128)(2,1)}, u32[]{:S(2)}) copy-start(bf16[1,1,128,6144]{3,2,1,0:T(8,128)(2,1)} %param.11) | copy-start | bytes 4718596
  68.9 41.9 %all-to-all-start.3 = ((bf16[4,192,768]{2,1,0:T(8,128)(2,1)}), bf16[4,192,768]{2,1,0:T(8,128)(2,1)S(1)}, u32[]{:S(2)}, u32[]{:S(2)}) async-start(bf16[4,192,768]{2,1,0:T(8,128)(2,1)} %broadcast_in_dim.36), calls=%async_computation.3 | async-start | bytes 2359296 | tf_op jit(solution)/shard_map/all_to_all | solution.py:27
  76.1 19.8 %collective-permute-start.7 = (bf16[4,64,768]{2,1,0:T(8,128)(2,1)}, bf16[4,64,768]{2,1,0:T(8,128)(2,1)}, u32[]{:S(2)}, u32[]{:S(2)}) collective-permute-start(bf16[4,64,768]{2,1,0:T(8,128)(2,1)} %pad_maximum_fusion.refs_0_), channel_id=1, source_target_pairs={{0,48},{16,0},{32,16},{48,32},{64,112},{80,64},{96,80},{112,96},{1... | collective-permute-start | bytes 1179656 | tf_op jit(solution)/shard_map/ppermute | solution.py:36
  81.1 16.3 %collective-permute-start.6 = (bf16[4,64,768]{2,1,0:T(8,128)(2,1)}, bf16[4,64,768]{2,1,0:T(8,128)(2,1)}, u32[]{:S(2)}, u32[]{:S(2)}) collective-permute-start(bf16[4,64,768]{2,1,0:T(8,128)(2,1)} %pad_maximum_fusion.refs_0_), channel_id=1, source_target_pairs={{0,32},{16,48},{32,0},{48,16},{64,96},{80,112},{96,64},{112,80},{1... | collective-permute-start | bytes 1179656 | tf_op jit(solution)/shard_map/ppermute | solution.py:36
  81.1 26.1 %collective-permute-start.5 = (bf16[4,64,768]{2,1,0:T(8,128)(2,1)}, bf16[4,64,768]{2,1,0:T(8,128)(2,1)}, u32[]{:S(2)}, u32[]{:S(2)}) collective-permute-start(bf16[4,64,768]{2,1,0:T(8,128)(2,1)} %pad_maximum_fusion.refs_0_), channel_id=1, source_target_pairs={{0,16},{16,32},{32,48},{48,0},{64,80},{80,96},{96,112},{112,64},{1... | collective-permute-start | bytes 1179656 | tf_op jit(solution)/shard_map/ppermute | solution.py:36
  82.1 1.4 copy-start.3
  83.6 0.7 copy-start.20
  84.3 1.4 copy-start.4
  84.3 1.4 copy-start.5
  84.3 1.4 copy-start.7
  85.6 23.4 %copy-start.9 = (f32[128,768]{1,0:T(8,128)}, f32[128,768]{1,0:T(8,128)S(1)}, u32[]{:S(2)}) copy-start(f32[128,768]{1,0:T(8,128)S(1)} %get-tuple-element.63.residual_ref) | copy-start | bytes 1179652
  85.7 23.4 %copy-start.11 = (f32[16,6144]{1,0:T(8,128)}, f32[16,6144]{1,0:T(8,128)S(1)}, u32[]{:S(2)}) copy-start(f32[16,6144]{1,0:T(8,128)S(1)} %get-tuple-element.66.residual_ref) | copy-start | bytes 1179652
  85.7 23.4 %copy-start.13 = (f32[16,6144]{1,0:T(8,128)}, f32[16,6144]{1,0:T(8,128)S(1)}, u32[]{:S(2)}) copy-start(f32[16,6144]{1,0:T(8,128)S(1)} %get-tuple-element.67.scaled_ref) | copy-start | bytes 1179652
  87.8 23.0 %copy-start.17 = (bf16[128,768]{1,0:T(8,128)(2,1)}, bf16[128,768]{1,0:T(8,128)(2,1)S(1)}, u32[]{:S(2)}) copy-start(bf16[128,768]{1,0:T(8,128)(2,1)S(1)} %get-tuple-element.60.context_ref) | copy-start | bytes 589828
  109.0 0.7 copy-start.15
  109.7 0.6 copy-start.21
  110.8 0.9 copy-start.18
  112.0 25.9 %copy-start.10 = (f32[128,768]{1,0:T(8,128)S(1)}, f32[128,768]{1,0:T(8,128)}, u32[]{:S(2)}) copy-start(f32[128,768]{1,0:T(8,128)} %copy-done.9) | copy-start | bytes 1179652
  112.1 25.9 %copy-start.16 = (bf16[128,768]{1,0:T(8,128)(2,1)S(1)}, bf16[128,768]{1,0:T(8,128)(2,1)}, u32[]{:S(2)}) copy-start(bf16[128,768]{1,0:T(8,128)(2,1)} %copy-done.15) | copy-start | bytes 589828
  139.1 12.7 %copy-start.12 = (f32[16,6144]{1,0:T(8,128)S(1)}, f32[16,6144]{1,0:T(8,128)}, u32[]{:S(2)}) copy-start(f32[16,6144]{1,0:T(8,128)} %copy-done.11) | copy-start | bytes 1179652
  139.1 12.7 %copy-start.14 = (f32[16,6144]{1,0:T(8,128)S(1)}, f32[16,6144]{1,0:T(8,128)}, u32[]{:S(2)}) copy-start(f32[16,6144]{1,0:T(8,128)} %copy-done.13) | copy-start | bytes 1179652
  139.1 12.7 %copy-start.22 = (f32[16,768]{1,0:T(8,128)S(1)}, f32[16,768]{1,0:T(8,128)}, u32[]{:S(2)}) copy-start(f32[16,768]{1,0:T(8,128)} %copy-done.21) | copy-start | bytes 147460
  152.8 18.0 %copy-start.6 = (bf16[1,1,128,768]{3,2,1,0:T(8,128)(2,1)S(1)}, bf16[1,1,128,768]{3,2,1,0:T(8,128)(2,1)}, u32[]{:S(2)}) copy-start(bf16[1,1,128,768]{3,2,1,0:T(8,128)(2,1)} %param.13) | copy-start | bytes 589828
  152.8 18.0 %copy-start.8 = (bf16[1,1,128,768]{3,2,1,0:T(8,128)(2,1)S(1)}, bf16[1,1,128,768]{3,2,1,0:T(8,128)(2,1)}, u32[]{:S(2)}) copy-start(bf16[1,1,128,768]{3,2,1,0:T(8,128)(2,1)} %param.14) | copy-start | bytes 589828
  163.6 15.3 %all-to-all-start.7 = ((bf16[16,16,768]{2,1,0:T(8,128)(2,1)}), bf16[16,16,768]{2,1,0:T(8,128)(2,1)S(1)}, u32[]{:S(2)}, u32[]{:S(2)}) async-start(bf16[16,16,768]{2,1,0:T(8,128)(2,1)} %shard_map.153), calls=%async_computation.7 | async-start | bytes 786432 | tf_op jit(solution)/shard_map/all_to_all | solution.py:27
  178.9 6.6 %collective-permute-start.8 = (bf16[16,768]{1,0:T(8,128)(2,1)S(1)}, bf16[16,768]{1,0:T(8,128)(2,1)S(1)}, u32[]{:S(2)}, u32[]{:S(2)}) collective-permute-start(bf16[16,768]{1,0:T(8,128)(2,1)S(1)} %dynamic-slice_bitcast_fusion.1), channel_id=1, source_target_pairs={{0,8},{8,0},{1,9},{9,1},{2,10},{10,2},{3,11},{11,3},{4,12},{12,4},... | collective-permute-start | bytes 73736 | tf_op jit(solution)/shard_map/ppermute | solution.py:23

commit v3 on v2

v3 whole, which is shorter than its diff:
```python
import jax
import jax.numpy as jnp
from jax import lax
from jax.experimental import pallas as pl
from jax.experimental.pallas import tpu as pltpu
from jax.sharding import PartitionSpec as P

HEAD = 128
L = 128
BLK = 32


EPSILON = 1e-05
N_HIGH = 4
N_LOW = 4
N_TENSOR = 8
EXTRA_ROWS = 16
ORDER_ROW = 12
VMEM_BYTES = 20 * 1024 * 1024
HIGH_GROUPS = [[z * N_LOW + y for z in range(N_HIGH)] for y in range(N_LOW)]
LOW_GROUPS = [[z * N_LOW + y for y in range(N_LOW)] for z in range(N_HIGH)]


def swapped_2(value, axis, distance):
    return lax.ppermute(value, axis, [(i, i ^ 1 << distance) for i in range(lax.axis_size(axis))])


def exchanged(value, axis, groups=None):
    return lax.all_to_all(value, axis, 0, 0, axis_index_groups=groups)


def turned(value, high, low):
    pairs = [
        (z * N_LOW + y, (z + high) % N_HIGH * N_LOW + (y + low) % N_LOW)
        for z in range(N_HIGH)
        for y in range(N_LOW)
    ]
    return lax.ppermute(value, "dp", pairs)


def transposed_owner(value, count):
    pairs = [
        ((half * count + d) * count + t, (half * count + t) * count + d)
        for half in range(2)
        for d in range(count)
        for t in range(count)
    ]
    return lax.ppermute(value, ("dp", "tensor"), pairs)


def summed(pieces):
    return jnp.sum(pieces.astype(jnp.float32), axis=0).astype(jnp.bfloat16)


def copies_of(value, count):
    return jnp.broadcast_to(value[None], (count,) + value.shape)


def allowed_pairs(mask_blocks):
    block_table = jnp.repeat(jnp.repeat(mask_blocks, BLK, axis=0), BLK, axis=1) == 1
    position = lax.broadcasted_iota(jnp.int32, (L, L), 0)
    column = lax.broadcasted_iota(jnp.int32, (L, L), 1)
    return block_table & (position >= column)


def times(left_side, right_side):
    return jnp.dot(left_side, right_side, preferred_element_type=jnp.float32)


def times_transposed(left_side, right_side):
    return lax.dot_general(
        left_side, right_side, (((1,), (1,)), ((), ())), preferred_element_type=jnp.float32
    )


def transposed_times(left_side, right_side):
    return lax.dot_general(
        left_side, right_side, (((0,), (0,)), ((), ())), preferred_element_type=jnp.float32
    )


def call(kernel, shapes, *inputs, places=None, after=()):
    skipped = len(after)

    def body(*refs):
        kernel(*refs[skipped:])

    scalars = [] if places is None else [places]
    return pl.pallas_call(
        body,
        out_shape=[jax.ShapeDtypeStruct(shape, dtype) for shape, dtype in shapes],
        in_specs=[pl.BlockSpec(memory_space=pl.ANY)] * skipped
        + [pl.BlockSpec(memory_space=pltpu.SMEM)] * len(scalars)
        + [pl.BlockSpec(memory_space=pltpu.VMEM)] * len(inputs),
        cost_estimate=pl.CostEstimate(flops=1, bytes_accessed=4_000_000, transcendentals=0),
        compiler_params=pltpu.CompilerParams(vmem_limit_bytes=VMEM_BYTES),
    )(*after, *scalars, *inputs)


def attend_kernel(query_ref, key_ref, value_ref, allowed_ref, context_ref, chance_ref):
    allowed = allowed_ref[...] > 0.5
    for head in range(query_ref.shape[1] // HEAD):
        columns = slice(head * HEAD, (head + 1) * HEAD)
        scores = times_transposed(query_ref[:, columns], key_ref[:, columns]) * HEAD ** (-0.5)
        scores = jnp.where(allowed, scores, -1e30)
        raised = jnp.exp(scores - jnp.max(scores, axis=-1, keepdims=True))
        chances = raised / jnp.sum(raised, axis=-1, keepdims=True)
        chance_ref[head] = chances
        mixture = times(chances.astype(jnp.bfloat16), value_ref[:, columns])
        context_ref[:, columns] = mixture.astype(jnp.bfloat16)


def first_kernel(parts_ref, out_ref):
    total = parts_ref[0].astype(jnp.float32)
    for part in range(1, parts_ref.shape[0]):
        total += parts_ref[part].astype(jnp.float32)
    out_ref[...] = total.astype(jnp.bfloat16)


def second_kernel(parts_ref, out_ref):
    total = parts_ref[0].astype(jnp.float32)
    for part in range(1, parts_ref.shape[0]):
        total += parts_ref[part].astype(jnp.float32)
    total = total.astype(jnp.bfloat16)
    for copy in range(out_ref.shape[0]):
        out_ref[copy] = total


def third_kernel(parts_ref, slice_ref, out_ref, slice_copy_ref):
    slice_copy_ref[...] = slice_ref[...]
    for copy in range(out_ref.shape[0]):
        out_ref[copy] = parts_ref[...]


def stack_kernel(places_ref, *refs):
    for step in range(N_HIGH):
        refs[-1][(places_ref[1] + N_HIGH - step) % N_HIGH] = refs[step][...]


def code_kernel(context_ref, joined_ref, column_ref, code_ref, column_copy_ref):
    column_copy_ref[...] = column_ref[...]
    code_ref[...] = times(context_ref[...], joined_ref[...]).astype(jnp.bfloat16)


def total_kernel(parts_ref, out_ref):
    total = parts_ref[0].astype(jnp.float32)
    for part in range(1, parts_ref.shape[0]):
        total += parts_ref[part].astype(jnp.float32)
    total = total.astype(jnp.bfloat16)
    for copy in range(out_ref.shape[0]):
        out_ref[copy] = total


def weight_kernel(places_ref, *refs):
    scaled_ref, gain_ref, bias_ref, book_ref, scaled_code_ref, extra_ref = refs[N_LOW:]
    for high in range(N_HIGH):
        for step in range(N_LOW):
            place = high * N_LOW + (places_ref[2] + N_LOW - step) % N_LOW
            book_ref[place] = refs[step][high]
    features, width = scaled_ref.shape[1], book_ref.shape[2]
    book = book_ref[...].reshape(features, width)
    row = lax.broadcasted_iota(jnp.int32, (EXTRA_ROWS, features), 0)
    rest = jnp.where(row == 0, 1.0, jnp.where(row == 1, gain_ref[...], 0.0))
    rest = jnp.where(row == 2, bias_ref[...], rest)
    total = jnp.zeros((EXTRA_ROWS, width), jnp.float32)
    for _ in range(3):
        top = rest.astype(jnp.bfloat16)
        rest = rest - top.astype(jnp.float32)
        total += times(top, book)
    upper = total.astype(jnp.bfloat16).astype(jnp.float32)
    lower = pltpu.roll(total - upper, 3, 0)
    row = lax.broadcasted_iota(jnp.int32, total.shape, 0)
    both = jnp.where(row < 3, upper, jnp.where(row < 6, lower, 0.0))
    half = width // 2
    extra = both[:, :half] + pltpu.roll(both[:, half:], 6, 0)
    wanted = places_ref[3].astype(jnp.float32)
    extra = jnp.where(row[:, :half] == ORDER_ROW, wanted, extra)
    extra_ref[...] = extra.astype(jnp.bfloat16)
    scaled_code_ref[...] = times(scaled_ref[...], book).astype(jnp.bfloat16)


def feature_kernel(code_ref, book_ref, residual_ref, gain_ref, scaled_ref, extra_ref, out_ref):
    count, rows, _ = out_ref.shape
    features, width = book_ref.shape
    book = book_ref[...]
    code = code_ref[...].reshape(count * rows, width)

    def put(start, value):
        value = value.astype(jnp.bfloat16)
        out_ref[:, :, start : start + value.shape[1]] = value.reshape(count, rows, -1)

    decoded = times_transposed(code, book)
    put(3 * width, decoded)
    hidden = residual_ref[...] + decoded
    put(0, times(hidden.astype(jnp.bfloat16), book))
    put(width, times((hidden * gain_ref[...]).astype(jnp.bfloat16), book))
    put(2 * width, scaled_ref[...])
    for copy in range(count):
        out_ref[copy, :, 3 * width + features :] = extra_ref[...]


def row_kernel(
    arrived_ref, residual_ref, scaled_ref, codes_ref, grad_code_ref, grad_ref, order_ref
):
    count = arrived_ref.shape[0]
    size = residual_ref.shape[1]
    width = codes_ref.shape[2]
    part = size // count // 2
    last = 3 * width + 2 * part
    total = arrived_ref[0, :, : 3 * width].astype(jnp.float32)
    extra = arrived_ref[0, :, last:].astype(jnp.float32)
    order_ref[0] = extra[:, :HEAD]
    for rank in range(1, count):
        total += arrived_ref[rank, :, : 3 * width].astype(jnp.float32)
        part_extra = arrived_ref[rank, :, last:].astype(jnp.float32)
        order_ref[rank] = part_extra[:, :HEAD]
        extra += part_extra
    sums = extra + pltpu.roll(extra, EXTRA_ROWS - 3, 0)
    sums = jnp.concatenate([sums, pltpu.roll(sums, EXTRA_ROWS - 6, 0)], axis=1)
    ones_sum, gain_sum, bias_sum = sums[0:1], sums[1:2], sums[2:3]
    hidden_code = total[:, :width]
    gained_code = total[:, width : 2 * width]
    scaled_code = total[:, 2 * width :]
    decoded = [
        arrived_ref[rank, :, 3 * width + half * part : 3 * width + (half + 1) * part]
        for half in range(2)
        for rank in range(count)
    ]
    hidden = residual_ref[...] + jnp.concatenate(decoded, axis=1).astype(jnp.float32)
    mean = jnp.sum(hidden, axis=-1, keepdims=True) / size
    centered = hidden - mean
    variance = jnp.sum(centered * centered, axis=-1, keepdims=True) / size
    inv_std = lax.rsqrt(variance + EPSILON)
    scaled = scaled_ref[...]
    product = jnp.sum(scaled * centered, axis=-1, keepdims=True) / size
    share = inv_std * inv_std * product
    grad_ref[...] = (inv_std * (scaled - centered * share)).astype(jnp.bfloat16)
    codes = inv_std * (gained_code - mean * gain_sum) + bias_sum
    grad_code = inv_std * (scaled_code - share * (hidden_code - mean * ones_sum))
    grad_code_ref[...] = grad_code.astype(jnp.bfloat16)
    codes = codes.astype(jnp.bfloat16)
    for copy in range(codes_ref.shape[0]):
        codes_ref[copy] = codes


def slot_kernel(order_ref, blocks_ref, grad_code_ref, out_ref):
    width = grad_code_ref.shape[1]
    for slot in range(out_ref.shape[0]):
        out_ref[slot, :, :width] = blocks_ref[order_ref[slot] // N_TENSOR]
        out_ref[slot, :, width:] = grad_code_ref[...]


def chosen_kernel(wanted_ref, both_ref, out_ref):
    out_ref[...] = both_ref[wanted_ref[0] % N_TENSOR, :, : out_ref.shape[1]]


def back_kernel(
    both_ref,
    joined_ref,
    query_ref,
    key_ref,
    value_ref,
    chance_ref,
    grad_query_ref,
    grad_key_ref,
    grad_value_ref,
):
    length, width = query_ref.shape
    code_width = joined_ref.shape[1]
    grad_code = both_ref[:, :, code_width:].reshape(length, code_width)
    for head in range(width // HEAD):
        columns = slice(head * HEAD, (head + 1) * HEAD)
        grad_context = times_transposed(grad_code, joined_ref[columns]).astype(jnp.bfloat16)
        chances = chance_ref[head]
        grad_value = transposed_times(chances.astype(jnp.bfloat16), grad_context)
        grad_value_ref[:, columns] = grad_value.astype(jnp.bfloat16)
        grad_chances = times_transposed(grad_context, value_ref[:, columns])
        grad_chances = grad_chances.astype(jnp.bfloat16).astype(jnp.float32)
        shift = jnp.sum(grad_chances * chances, axis=-1, keepdims=True)
        grad_scores = chances * (grad_chances - shift) * HEAD ** (-0.5)
        grad_scores = grad_scores.astype(jnp.bfloat16)
        grad_query = times(grad_scores, key_ref[:, columns])
        grad_query_ref[:, columns] = grad_query.astype(jnp.bfloat16)
        grad_key = transposed_times(grad_scores, query_ref[:, columns])
        grad_key_ref[:, columns] = grad_key.astype(jnp.bfloat16)


def prepare_kernel(
    places_ref,
    residual_ref,
    upstream_ref,
    gain_ref,
    bias_ref,
    residual_here_ref,
    scaled_here_ref,
    gain_here_ref,
    bias_here_ref,
    residual_rows_ref,
    scaled_rows_ref,
):
    length = residual_ref.shape[0]
    rows, width = residual_rows_ref.shape
    part = gain_here_ref.shape[1] // 2
    rank = places_ref[0]
    gain = gain_ref[...]

    def centered(ref, start, scale):
        wide = ref[pl.ds(start, rows), :].astype(jnp.float32)
        wide = wide if scale is None else wide * scale
        return wide - jnp.sum(wide, axis=-1, keepdims=True) / width

    count = width // part // 2

    def places(half):
        start = pl.multiple_of((rank + half * count) * part, HEAD)
        return slice(half * part, (half + 1) * part), pl.ds(start, part)

    for half in range(2):
        here, there = places(half)
        gain_here_ref[:, here] = gain_ref[:, there]
        bias_here_ref[:, here] = bias_ref[:, there]
    for start in range(0, length, rows):
        block = slice(start, start + rows)
        wide = residual_ref[block, :].astype(jnp.float32)
        mean = jnp.sum(wide, axis=-1, keepdims=True) / width
        wide = upstream_ref[block, :].astype(jnp.float32) * gain
        scaled_mean = jnp.sum(wide, axis=-1, keepdims=True) / width
        for half in range(2):
            here, there = places(half)
            residual_here_ref[block, here] = residual_ref[block, there].astype(jnp.float32) - mean
            scaled = upstream_ref[block, there].astype(jnp.float32) * gain_ref[:, there]
            scaled_here_ref[block, here] = (scaled - scaled_mean).astype(jnp.bfloat16)
    own = pl.multiple_of(rank * rows, rows)
    residual_rows_ref[...] = centered(residual_ref, own, None)
    scaled_rows_ref[...] = centered(upstream_ref, own, gain)


def on_device(
    residual,
    queries,
    key_vectors,
    value_vectors,
    block_mask,
    out_weight,
    codebook,
    norm_gain,
    norm_bias,
    receiver_order,
    upstream,
):
    n_dp = lax.axis_size("dp")
    n_tensor = lax.axis_size("tensor")
    rank = lax.axis_index("tensor")
    length, width = residual.shape[2:]
    code_book = codebook[0]
    shard, code_width = code_book.shape
    piece = shard // n_tensor
    rows = length // n_tensor
    features = n_dp * piece
    heads = queries.shape[3] // HEAD
    share = out_weight.shape[1] // n_dp
    bf16, f32 = jnp.bfloat16, jnp.float32
    dp_rank = lax.axis_index("dp")
    wanted = swapped_2(receiver_order[0], "section", 0)
    places = jnp.stack([rank, dp_rank // N_LOW, dp_rank % N_LOW, wanted[0]])
    allowed = allowed_pairs(block_mask[0, 0]).astype(f32)

    joined_part = times(out_weight[0], code_book).astype(bf16)
    joined_parts = exchanged(joined_part.reshape(N_LOW, -1, code_width), "dp", LOW_GROUPS)
    own_slice = lax.dynamic_slice_in_dim(code_book, rank * piece, piece, 0)
    own_slice = transposed_owner(own_slice, n_tensor)
    residual_here, scaled_here, gain_here, bias_here, residual_rows, scaled_rows = call(
        prepare_kernel,
        [
            ((length, features), f32),
            ((length, features), bf16),
            ((1, features), f32),
            ((1, features), f32),
            ((rows, width), f32),
            ((rows, width), f32),
        ],
        residual[0, 0],
        upstream[0, 0],
        norm_gain,
        norm_bias,
        places=places,
        after=(joined_part,),
    )
    (joined_rows,) = call(
        first_kernel, [((N_HIGH * share, code_width), bf16)], joined_parts, after=(own_slice, gain_here)
    )
    joined_parts = exchanged(joined_rows.reshape(N_HIGH, share, code_width), "dp", HIGH_GROUPS)
    context, chances = call(
        attend_kernel,
        [((length, heads * HEAD), bf16), ((heads, length, length), f32)],
        queries[0, 0],
        key_vectors[0, 0],
        value_vectors[0, 0],
        allowed,
        after=(joined_rows,),
    )
    (joined_rows,) = call(
        second_kernel, [((N_HIGH, share, code_width), bf16)], joined_parts, after=(context,)
    )
    joined_rows = exchanged(joined_rows, "dp", HIGH_GROUPS)
    sent, own_slice = call(
        third_kernel,
        [((N_LOW, N_HIGH * share, code_width), bf16), ((piece, code_width), bf16)],
        joined_rows.reshape(N_HIGH * share, code_width),
        own_slice,
    )
    joined = exchanged(sent, "dp", LOW_GROUPS).reshape(n_dp * share, code_width)

    (column,) = call(
        stack_kernel,
        [((N_HIGH, piece, code_width), bf16)],
        own_slice,
        *[turned(own_slice, step, 0) for step in range(1, N_HIGH)],
        places=places,
    )
    code_part, column = call(
        code_kernel,
        [((length, code_width), bf16), ((N_HIGH, piece, code_width), bf16)],
        context,
        joined,
        column,
    )
    columns = [column] + [turned(column, 0, step) for step in range(1, N_LOW)]
    code_parts = exchanged(code_part.reshape(n_tensor, rows, code_width), "tensor")
    (code_copies,) = call(
        total_kernel, [((n_tensor, rows, code_width), bf16)], code_parts, after=columns[1:]
    )
    code = exchanged(code_copies, "tensor")
    book_here, scaled_code, extra = call(
        weight_kernel,
        [
            ((n_dp, piece, code_width), bf16),
            ((length, code_width), bf16),
            ((EXTRA_ROWS, code_width // 2), bf16),
        ],
        *columns,
        scaled_here,
        gain_here,
        bias_here,
        places=places,
    )
    (sent,) = call(
        feature_kernel,
        [((n_tensor, rows, 3 * code_width + features + code_width // 2), bf16)],
        code,
        book_here.reshape(features, code_width),
        residual_here,
        gain_here,
        scaled_code,
        extra,
    )
    arrived = exchanged(sent, "tensor")
    codes, grad_code, grad_residual, orders = call(
        row_kernel,
        [
            ((n_dp, rows, code_width), bf16),
            ((rows, code_width), bf16),
            ((rows, width), bf16),
            ((n_tensor, EXTRA_ROWS, HEAD), f32),
        ],
        arrived,
        residual_rows,
        scaled_rows,
    )

    blocks = exchanged(codes, "dp")
    order_here = orders[:, ORDER_ROW, 0].astype(jnp.int32)
    (both,) = call(
        slot_kernel,
        [((n_tensor, rows, 2 * code_width), bf16)],
        blocks,
        grad_code,
        places=order_here,
    )
    both = exchanged(both, "tensor")
    (chosen,) = call(chosen_kernel, [((rows, code_width), bf16)], both, places=wanted)
    received = swapped_2(chosen, "section", 0)
    grad_query, grad_key, grad_value = call(
        back_kernel,
        [((length, heads * HEAD), bf16)] * 3,
        both,
        joined,
        queries[0, 0],
        key_vectors[0, 0],
        value_vectors[0, 0],
        chances,
        after=(chosen,),
    )
    return (
        received[None, None],
        grad_residual[None, None],
        grad_query[None, None],
        grad_key[None, None],
        grad_value[None, None],
    )


def solution(mesh):
    in_specs = (
        P("section", "dp", None, None),
        P("section", "dp", None, "tensor"),
        P("section", "dp", None, "tensor"),
        P("section", "dp", None, "tensor"),
        P("section", "dp", None, None),
        P("section", "tensor", "dp"),
        P("section", "dp", None),
        P("section", None),
        P("section", None),
        P("section", ("dp", "tensor")),
        P("section", "dp", None, None),
    )
    out_specs = (
        P("section", ("dp", "tensor"), None, None),
        P("section", "dp", "tensor", None),
        P("section", "dp", None, "tensor"),
        P("section", "dp", None, "tensor"),
        P("section", "dp", None, "tensor"),
    )
    return jax.shard_map(
        on_device, mesh=mesh, in_specs=in_specs, out_specs=out_specs, check_vma=False
    )
```

time: 187 us -> 166 us (0.89)
  blocking collectives: 85.2 us -> 36.3 us
  waiting for transfers between devices: 24.9 us -> 39.4 us
  starting transfers between devices: 44.6 us -> 54.5 us
  local copies, waits for them, and re-layouts: 8.37 us -> 13.7 us
  Pallas kernels: 13.6 us -> 16.6 us
  other arithmetic: 3.87 us -> 0.91 us
  between operations: 3.7 us -> 0.85 us
    all_to_all x5 -> x3, blocking collectives: 85.2 us -> 36.3 us  [exchanged(): return lax.all_to_all(value, axis, 0, 0, axis_index_groups=groups)]
    all_to_all x3 -> x6, starting transfers between devices: 14.3 us -> 38.9 us  [exchanged(): return lax.all_to_all(value, axis, 0, 0, axis_index_groups=groups)]
    all_to_all x3 -> x6, waiting for transfers between devices: 4.38 us -> 23.6 us  [exchanged(): return lax.all_to_all(value, axis, 0, 0, axis_index_groups=groups)]
    ppermute x6, starting transfers between devices: 20.9 us -> 5.15 us  [turned(): return lax.ppermute(value, 'dp', pairs)]
    unnamed x51 -> x47, local copies, waits for them, and re-layouts: 6.11 us -> 12.7 us
    ppermute x6, waiting for transfers between devices: 19.4 us -> 15.9 us  [turned(): return lax.ppermute(value, 'dp', pairs)]
    pallas_call x9 -> x14, Pallas kernels: 13.6 us -> 16.6 us  [call(): pl.pallas_call(body, out_shape=[jax.ShapeDtypeStruct(shape, dtype) for sh...]
    another operation x3 -> x1, other arithmetic: 3.13 us -> 0.64 us  [on_device(): places = jnp.stack([rank, dp_rank // N_LOW, dp_rank % N_LOW, wanted[0]])]
  transfers between devices with their start and end apart: 12 -> 15, of which waited for: 6 -> 11; matrix products, arithmetic and copies ran while one was open for 3% -> 1% of each run, Pallas kernels for 5% -> 6%
where the time goes in v3:
time: 166 us; the launch traced here: 165 us
  starting transfers between devices  54.5 us (33%)
  waiting for transfers between devices  39.4 us (24%)
  blocking collectives  36.3 us (22%)
  Pallas kernels  16.6 us (10%)
  local copies, waits for them, and re-layouts  13.7 us (8%)
  matrix products  2.87 us (2%)
    all_to_all x6, starting transfers between devices, exchanged(): return lax.all_to_all(value, axis, 0, 0, axis_index_groups=groups)  38.9 us
    all_to_all x3, blocking collectives, exchanged(): return lax.all_to_all(value, axis, 0, 0, axis_index_groups=groups)  36.3 us
    all_to_all x6, waiting for transfers between devices, exchanged(): return lax.all_to_all(value, axis, 0, 0, axis_index_groups=groups)  23.6 us
    pallas_call x14, Pallas kernels, call(): pl.pallas_call(body, out_shape=[jax.ShapeDtypeStruct(shape, dtype) for sh...  16.6 us
    ppermute x6, waiting for transfers between devices, turned(): return lax.ppermute(value, 'dp', pairs)  15.9 us
    unnamed x47, local copies, waits for them, and re-layouts  12.7 us
    ppermute x2, starting transfers between devices, swapped_2(): lax.ppermute(value, axis, [(i, i ^ 1 << distance) for i in range(lax.axis...  8.89 us
    ppermute x6, starting transfers between devices, turned(): return lax.ppermute(value, 'dp', pairs)  5.15 us
  transfers between devices with their start and end apart: 15, of which 11 were waited for; matrix products, arithmetic and copies ran while one was open for 1% of the time, Pallas kernels for 6%

profile of v3, /device:TPU:1, one launch (start us, length us, event | category | flops | bytes accessed | tf_op | source)
XLA Modules:
  0.0 165.1 jit_solution(9736469507978122636)
XLA Ops:
  0.6 0.0 copy-start
  0.6 1.1 copy-done
  1.7 2.9 %convolution_convert_fusion.refs_0_ = bf16[768,768]{1,0:T(8,128)(2,1)} fusion(bf16[1,384,768]{2,1,0:T(8,128)(2,1)S(1)} %copy-done, bf16[1,768,384]{2,1,0:T(8,128)(2,1)} %param.16), kind=kOutput, calls=%fused_computation | convolution fusion | flops 453574656 | bytes 2359296 | tf_op jit(solution)/shard_map/dot_general | solution.py:67
  4.6 5.1 %all-to-all-start = ((bf16[4,192,768]{2,1,0:T(8,128)(2,1)}), bf16[4,192,768]{2,1,0:T(8,128)(2,1)S(1)}, u32[]{:S(2)}, u32[]{:S(2)}) async-start(bf16[4,192,768]{2,1,0:T(8,128)(2,1)} %bitcast.9), calls=%async_computation | async-start | bytes 2359296 | tf_op jit(solution)/shard_map/all_to_all | solution.py:29
  9.7 1.9 %collective-permute-start = (s32[1]{0:T(128)}, s32[1]{0:T(128)}, u32[]{:S(2)}, u32[]{:S(2)}) collective-permute-start(s32[1]{0:T(128)} %bitcast), channel_id=1, source_target_pairs={{0,8},{8,0},{1,9},{9,1},{2,10},{10,2},{3,11},{11,3},{4,12},{12,4},... | collective-permute-start | bytes 20 | tf_op jit(solution)/shard_map/ppermute | solution.py:25
  11.6 0.6 dynamic-slice_bitcast_fusion
  12.2 1.5 collective-permute-start.1
  13.8 0.6 pad_add_fusion.refs_1_.refs_0_
  14.4 1.4 copy-done.2
  15.8 1.3 shard_map.146
  17.2 0.7 copy-done.10
  17.9 0.8 copy-done.12
  18.7 0.8 copy-done.14
  19.4 0.7 copy-done.16
  20.1 4.4 %all-to-all-done.refs_2_ = bf16[4,192,768]{2,1,0:T(8,128)(2,1)S(1)} async-done(((bf16[4,192,768]{2,1,0:T(8,128)(2,1)}), bf16[4,192,768]{2,1,0:T(8,128)(2,1)S(1)}, u32[]{:S(2)}, u32[]{:S(2)}) %all-to-all-start) | async-done | bytes 1179680 | tf_op jit(solution)/shard_map/all_to_all | solution.py:29
  24.5 0.9 shard_map.147.refs_0_
  25.4 9.0 %all-to-all-start.1 = ((bf16[4,48,768]{2,1,0:T(8,128)(2,1)}), bf16[4,48,768]{2,1,0:T(8,128)(2,1)S(1)}, u32[]{:S(2)}, u32[]{:S(2)}) async-start(bf16[4,48,768]{2,1,0:T(8,128)(2,1)} %bitcast.15), calls=%async_computation.1 | async-start | bytes 589824 | tf_op jit(solution)/shard_map/all_to_all | solution.py:29
  34.4 0.1 copy.16
  34.5 0.1 broadcast_in_dim.21
  34.5 0.1 eq.22
  34.7 0.1 copy.17
  34.8 2.0 %shard_map.148 = (bf16[128,768]{1,0:T(8,128)(2,1)S(1)}, f32[6,128,128]{2,1,0:T(8,128)S(1)}) custom-call(bf16[192,768]{1,0:T(8,128)(2,1)} %shard_map.147.refs_0_, bf16[128,768]{1,0:T(8,128)(2,1)S(1)} %bitcast.39, bf16[128,768]{1,0:T(8,128)(2,1)S(1)} %bitcast.41, bf16[128,768]{1,0:T(8,128)(2,1)S(1)} %bitcast.43, f32[128,128]{1,0:T(8,128)S(1)} %fusion.3.refs_4_), custom_call_target="tpu_custom_call" | custom-call | flops 1 | bytes 4000000 | tf_op jit(solution)/shard_map/pallas_call | solution.py:89
  36.9 0.8 copy-done.8
  37.7 5.0 %all-to-all-done.1.refs_1_ = bf16[4,48,768]{2,1,0:T(8,128)(2,1)S(1)} async-done(((bf16[4,48,768]{2,1,0:T(8,128)(2,1)}), bf16[4,48,768]{2,1,0:T(8,128)(2,1)S(1)}, u32[]{:S(2)}, u32[]{:S(2)}) %all-to-all-start.1) | async-done | bytes 294944 | tf_op jit(solution)/shard_map/all_to_all | solution.py:29
  42.7 12.9 %all_to_all.45 = bf16[4,48,768]{2,1,0:T(8,128)(2,1)S(1)} all-to-all(bf16[4,48,768]{2,1,0:T(8,128)(2,1)S(1)} %shard_map.149), channel_id=1, replica_groups={{0,64,128,192},{16,80,144,208},{32,96,160,224},{48,112,176,240},{1,65,1..., dimensions={0} | all-to-all | bytes 589824 | tf_op jit(solution)/shard_map/all_to_all | solution.py:29
  55.6 1.1 shard_map.150
  56.7 5.1 %all-to-all-start.3 = ((bf16[4,192,768]{2,1,0:T(8,128)(2,1)}), bf16[4,192,768]{2,1,0:T(8,128)(2,1)S(1)}, u32[]{:S(2)}, u32[]{:S(2)}) async-start(bf16[4,192,768]{2,1,0:T(8,128)(2,1)} %get-tuple-element.29), calls=%async_computation.3 | async-start | bytes 2359296 | tf_op jit(solution)/shard_map/all_to_all | solution.py:29
  61.8 0.9 collective-permute-start.4
  62.7 1.9 %collective-permute-start.3 = (bf16[48,768]{1,0:T(8,128)(2,1)S(1)}, bf16[48,768]{1,0:T(8,128)(2,1)S(1)}, u32[]{:S(2)}, u32[]{:S(2)}) collective-permute-start(bf16[48,768]{1,0:T(8,128)(2,1)S(1)} %get-tuple-element.30.refs_1_), channel_id=1, source_target_pairs={{0,128},{16,144},{32,160},{48,176},{64,192},{80,208},{96,224},{112... | collective-permute-start | bytes 221192 | tf_op jit(solution)/shard_map/ppermute | solution.py:38
  64.6 0.6 collective-permute-start.2
  65.2 1.4 collective-permute-done.4.refs_4_
  66.6 4.7 %collective-permute-done.3.refs_3_ = bf16[48,768]{1,0:T(8,128)(2,1)S(1)} collective-permute-done((bf16[48,768]{1,0:T(8,128)(2,1)S(1)}, bf16[48,768]{1,0:T(8,128)(2,1)S(1)}, u32[]{:S(2)}, u32[]{:S(2)}) %collective-permute-start.3) | collective-permute-done | bytes 73760 | tf_op jit(solution)/shard_map/ppermute | solution.py:38
  71.3 0.1 collective-permute-done.2.refs_2_
  71.4 0.6 shard_map.151.refs_2_
  72.0 2.2 %all-to-all-done.3 = bf16[4,192,768]{2,1,0:T(8,128)(2,1)S(1)} async-done(((bf16[4,192,768]{2,1,0:T(8,128)(2,1)}), bf16[4,192,768]{2,1,0:T(8,128)(2,1)S(1)}, u32[]{:S(2)}, u32[]{:S(2)}) %all-to-all-start.3) | async-done | bytes 1179680 | tf_op jit(solution)/shard_map/all_to_all | solution.py:29
  74.2 1.0 shard_map.152
  75.2 5.4 %all-to-all-start.4 = ((bf16[8,16,768]{2,1,0:T(8,128)(2,1)}), bf16[8,16,768]{2,1,0:T(8,128)(2,1)S(1)}, u32[]{:S(2)}, u32[]{:S(2)}) async-start(bf16[8,16,768]{2,1,0:T(8,128)(2,1)} %bitcast.18), calls=%async_computation.4 | async-start | bytes 393216 | tf_op jit(solution)/shard_map/all_to_all | solution.py:29
  80.7 0.7 collective-permute-start.7
  81.4 1.1 collective-permute-start.6
  82.5 4.0 %collective-permute-done.7.refs_2_.refs_4_ = bf16[4,48,768]{2,1,0:T(8,128)(2,1)S(1)} collective-permute-done((bf16[4,48,768]{2,1,0:T(8,128)(2,1)}, bf16[4,48,768]{2,1,0:T(8,128)(2,1)S(1)}, u32[]{:S(2)}, u32[]{:S(2)}) %collective-permute-start.7) | collective-permute-done | bytes 294944 | tf_op jit(solution)/shard_map/ppermute | solution.py:38
  86.5 2.3 %collective-permute-done.6.refs_1_.refs_3_ = bf16[4,48,768]{2,1,0:T(8,128)(2,1)S(1)} collective-permute-done((bf16[4,48,768]{2,1,0:T(8,128)(2,1)}, bf16[4,48,768]{2,1,0:T(8,128)(2,1)S(1)}, u32[]{:S(2)}, u32[]{:S(2)}) %collective-permute-start.6) | collective-permute-done | bytes 294944 | tf_op jit(solution)/shard_map/ppermute | solution.py:38
  88.7 3.4 %collective-permute-done.5.refs_0_.refs_2_ = bf16[4,48,768]{2,1,0:T(8,128)(2,1)S(1)} collective-permute-done((bf16[4,48,768]{2,1,0:T(8,128)(2,1)}, bf16[4,48,768]{2,1,0:T(8,128)(2,1)S(1)}, u32[]{:S(2)}, u32[]{:S(2)}) %collective-permute-start.5) | collective-permute-done | bytes 294944 | tf_op jit(solution)/shard_map/ppermute | solution.py:38
  92.1 0.7 shard_map.153
  92.8 4.8 %all-to-all-start.5 = ((bf16[8,16,768]{2,1,0:T(8,128)(2,1)}), bf16[8,16,768]{2,1,0:T(8,128)(2,1)S(1)}, u32[]{:S(2)}, u32[]{:S(2)}) async-start(bf16[8,16,768]{2,1,0:T(8,128)(2,1)} %shard_map.153), calls=%async_computation.5 | async-start | bytes 393216 | tf_op jit(solution)/shard_map/all_to_all | solution.py:29
  97.7 0.9 copy-done.17
  98.6 1.8 %shard_map.154 = (bf16[16,48,768]{2,1,0:T(8,128)(2,1)S(1)}, bf16[128,768]{1,0:T(8,128)(2,1)S(1)}, bf16[16,384]{1,0:T(8,128)(2,1)S(1)}) custom-call(s32[4]{0:T(128)S(1)} %pad_add_fusion.refs_1_.refs_0_, bf16[4,48,768]{2,1,0:T(8,128)(2,1)} %get-tuple-element.31.refs_1_, bf16[4,48,768]{2,1,0:T(8,128)(2,1)S(1)} %collective-permute-done.5.refs_0_.refs_2_, ...), custom_call_target="tpu_custom_call" | custom-call | flops 1 | bytes 4000000 | tf_op jit(solution)/shard_map/pallas_call | solution.py:89
  100.4 1.0 copy-done.3
  101.5 0.7 copy-done.18
  102.1 1.3 all-to-all-done.5.refs_0_
  103.5 1.3 copy-done.4
  104.7 1.0 copy-done.11
  105.7 0.9 copy-done.19
  106.7 1.1 shard_map.155
  107.8 13.3 %all_to_all.46.refs_0_ = bf16[8,16,3456]{2,1,0:T(8,128)(2,1)S(1)} all-to-all(bf16[8,16,3456]{2,1,0:T(8,128)(2,1)S(1)} %shard_map.155), channel_id=1, replica_groups=mesh['dp'=16,'section'=2,'tensor'=8] {'tensor'}, dimensions={0} | all-to-all | bytes 1769472 | tf_op jit(solution)/shard_map/all_to_all | solution.py:29
  121.1 1.2 shard_map.156
  122.3 9.4 %all-to-all-start.7 = ((bf16[16,16,768]{2,1,0:T(8,128)(2,1)}), bf16[16,16,768]{2,1,0:T(8,128)(2,1)S(1)}, u32[]{:S(2)}, u32[]{:S(2)}) async-start(bf16[16,16,768]{2,1,0:T(8,128)(2,1)} %get-tuple-element.42), calls=%async_computation.7 | async-start | bytes 786432 | tf_op jit(solution)/shard_map/all_to_all | solution.py:29
  131.7 0.2 convert_reduce_fusion.refs_0_
  131.9 10.6 %all-to-all-done.7.refs_1_ = bf16[16,16,768]{2,1,0:T(8,128)(2,1)S(1)} async-done(((bf16[16,16,768]{2,1,0:T(8,128)(2,1)}), bf16[16,16,768]{2,1,0:T(8,128)(2,1)S(1)}, u32[]{:S(2)}, u32[]{:S(2)}) %all-to-all-start.7) | async-done | bytes 393248 | tf_op jit(solution)/shard_map/all_to_all | solution.py:29
  142.5 0.6 shard_map.157
  143.1 10.0 %all_to_all.47.refs_1_ = bf16[8,16,1536]{2,1,0:T(8,128)(2,1)S(1)} all-to-all(bf16[8,16,1536]{2,1,0:T(8,128)(2,1)S(1)} %shard_map.157), channel_id=1, replica_groups=mesh['dp'=16,'section'=2,'tensor'=8] {'tensor'}, dimensions={0} | all-to-all | bytes 786432 | tf_op jit(solution)/shard_map/all_to_all | solution.py:29
  153.1 0.6 shard_map.158.refs_0_
  153.7 7.0 %collective-permute-start.8 = (bf16[16,768]{1,0:T(8,128)(2,1)S(1)}, bf16[16,768]{1,0:T(8,128)(2,1)S(1)}, u32[]{:S(2)}, u32[]{:S(2)}) collective-permute-start(bf16[16,768]{1,0:T(8,128)(2,1)S(1)} %shard_map.158.refs_0_), channel_id=1, source_target_pairs={{0,8},{8,0},{1,9},{9,1},{2,10},{10,2},{3,11},{11,3},{4,12},{12,4},... | collective-permute-start | bytes 73736 | tf_op jit(solution)/shard_map/ppermute | solution.py:25
  160.8 3.7 %shard_map.159 = (bf16[128,768]{1,0:T(8,128)(2,1)}, bf16[128,768]{1,0:T(8,128)(2,1)}, bf16[128,768]{1,0:T(8,128)(2,1)}) custom-call(bf16[16,768]{1,0:T(8,128)(2,1)S(1)} %shard_map.158.refs_0_, bf16[8,16,1536]{2,1,0:T(8,128)(2,1)S(1)} %all_to_all.47.refs_1_, bf16[768,768]{1,0:T(8,128)(2,1)S(1)} %bitcast.34, bf16[128,768]{1,0:T(8,128)(2,1)S(1)} %bitcast.40, ...), custom_call_target="tpu_custom_call" | custom-call | flops 1 | bytes 4000000 | tf_op jit(solution)/shard_map/pallas_call | solution.py:89
  164.5 0.6 copy.19
  (41 shorter events, 0.2 us)
Async XLA Ops:
  0.6 1.1 copy-start
  4.6 9.8 %copy-start.1 = (bf16[1,1,128,6144]{3,2,1,0:T(8,128)(2,1)S(1)}, bf16[1,1,128,6144]{3,2,1,0:T(8,128)(2,1)}, u32[]{:S(2)}) copy-start(bf16[1,1,128,6144]{3,2,1,0:T(8,128)(2,1)} %param.11) | copy-start | bytes 4718596
  4.6 9.8 %copy-start.20 = (f32[1,6144]{1,0:T(1,128)S(1)}, f32[1,6144]{1,0:T(1,128)}, u32[]{:S(2)}) copy-start(f32[1,6144]{1,0:T(1,128)} %refs_4_.1) | copy-start | bytes 73732
  4.6 9.8 %copy-start.21 = (f32[1,6144]{1,0:T(1,128)S(1)}, f32[1,6144]{1,0:T(1,128)}, u32[]{:S(2)}) copy-start(f32[1,6144]{1,0:T(1,128)} %refs_5_.1) | copy-start | bytes 73732
  4.6 19.9 %all-to-all-start = ((bf16[4,192,768]{2,1,0:T(8,128)(2,1)}), bf16[4,192,768]{2,1,0:T(8,128)(2,1)S(1)}, u32[]{:S(2)}, u32[]{:S(2)}) async-start(bf16[4,192,768]{2,1,0:T(8,128)(2,1)} %bitcast.9), calls=%async_computation | async-start | bytes 2359296 | tf_op jit(solution)/shard_map/all_to_all | solution.py:29
  9.7 4.0 %collective-permute-start = (s32[1]{0:T(128)}, s32[1]{0:T(128)}, u32[]{:S(2)}, u32[]{:S(2)}) collective-permute-start(s32[1]{0:T(128)} %bitcast), channel_id=1, source_target_pairs={{0,8},{8,0},{1,9},{9,1},{2,10},{10,2},{3,11},{11,3},{4,12},{12,4},... | collective-permute-start | bytes 20 | tf_op jit(solution)/shard_map/ppermute | solution.py:25
  12.2 7.9 %collective-permute-start.1 = (bf16[48,768]{1,0:T(8,128)(2,1)}, bf16[48,768]{1,0:T(8,128)(2,1)S(1)}, u32[]{:S(2)}, u32[]{:S(2)}) collective-permute-start(bf16[48,768]{1,0:T(8,128)(2,1)} %dynamic-slice_bitcast_fusion), channel_id=1, source_target_pairs={{0,0},{1,16},{2,32},{3,48},{4,64},{5,80},{6,96},{7,112},{16,1},{17... | collective-permute-start | bytes 221192 | tf_op jit(solution)/shard_map/ppermute | solution.py:48
  14.4 1.4 copy-start.2
  17.1 0.7 copy-start.10
  17.9 0.8 copy-start.12
  18.7 0.8 copy-start.14
  19.4 0.7 copy-start.16
  20.1 14.3 %copy-start.22 = (s32[1,1,4,4]{3,2,1,0:T(4,128)S(1)}, s32[1,1,4,4]{3,2,1,0:T(4,128)}, u32[]{:S(2)}) copy-start(s32[1,1,4,4]{3,2,1,0:T(4,128)} %param.15) | copy-start | bytes 196
  20.1 14.7 %copy-start.5 = (bf16[1,1,128,768]{3,2,1,0:T(8,128)(2,1)S(1)}, bf16[1,1,128,768]{3,2,1,0:T(8,128)(2,1)}, u32[]{:S(2)}) copy-start(bf16[1,1,128,768]{3,2,1,0:T(8,128)(2,1)} %param.12) | copy-start | bytes 589828
  20.1 14.7 %copy-start.6 = (bf16[1,1,128,768]{3,2,1,0:T(8,128)(2,1)S(1)}, bf16[1,1,128,768]{3,2,1,0:T(8,128)(2,1)}, u32[]{:S(2)}) copy-start(bf16[1,1,128,768]{3,2,1,0:T(8,128)(2,1)} %param.13) | copy-start | bytes 589828
  20.1 14.7 %copy-start.7 = (bf16[1,1,128,768]{3,2,1,0:T(8,128)(2,1)S(1)}, bf16[1,1,128,768]{3,2,1,0:T(8,128)(2,1)}, u32[]{:S(2)}) copy-start(bf16[1,1,128,768]{3,2,1,0:T(8,128)(2,1)} %param.14) | copy-start | bytes 589828
  25.4 17.3 %all-to-all-start.1 = ((bf16[4,48,768]{2,1,0:T(8,128)(2,1)}), bf16[4,48,768]{2,1,0:T(8,128)(2,1)S(1)}, u32[]{:S(2)}, u32[]{:S(2)}) async-start(bf16[4,48,768]{2,1,0:T(8,128)(2,1)} %bitcast.15), calls=%async_computation.1 | async-start | bytes 589824 | tf_op jit(solution)/shard_map/all_to_all | solution.py:29
  36.9 0.8 copy-start.8
  56.7 17.5 %all-to-all-start.3 = ((bf16[4,192,768]{2,1,0:T(8,128)(2,1)}), bf16[4,192,768]{2,1,0:T(8,128)(2,1)S(1)}, u32[]{:S(2)}, u32[]{:S(2)}) async-start(bf16[4,192,768]{2,1,0:T(8,128)(2,1)} %get-tuple-element.29), calls=%async_computation.3 | async-start | bytes 2359296 | tf_op jit(solution)/shard_map/all_to_all | solution.py:29
  61.8 4.8 %collective-permute-start.4 = (bf16[48,768]{1,0:T(8,128)(2,1)S(1)}, bf16[48,768]{1,0:T(8,128)(2,1)S(1)}, u32[]{:S(2)}, u32[]{:S(2)}) collective-permute-start(bf16[48,768]{1,0:T(8,128)(2,1)S(1)} %get-tuple-element.30.refs_1_), channel_id=1, source_target_pairs={{0,192},{16,208},{32,224},{48,240},{64,0},{80,16},{96,32},{112,48}... | collective-permute-start | bytes 221192 | tf_op jit(solution)/shard_map/ppermute | solution.py:38
  62.7 8.6 %collective-permute-start.3 = (bf16[48,768]{1,0:T(8,128)(2,1)S(1)}, bf16[48,768]{1,0:T(8,128)(2,1)S(1)}, u32[]{:S(2)}, u32[]{:S(2)}) collective-permute-start(bf16[48,768]{1,0:T(8,128)(2,1)S(1)} %get-tuple-element.30.refs_1_), channel_id=1, source_target_pairs={{0,128},{16,144},{32,160},{48,176},{64,192},{80,208},{96,224},{112... | collective-permute-start | bytes 221192 | tf_op jit(solution)/shard_map/ppermute | solution.py:38
  64.6 6.8 %collective-permute-start.2 = (bf16[48,768]{1,0:T(8,128)(2,1)S(1)}, bf16[48,768]{1,0:T(8,128)(2,1)S(1)}, u32[]{:S(2)}, u32[]{:S(2)}) collective-permute-start(bf16[48,768]{1,0:T(8,128)(2,1)S(1)} %get-tuple-element.30.refs_1_), channel_id=1, source_target_pairs={{0,64},{16,80},{32,96},{48,112},{64,128},{80,144},{96,160},{112,17... | collective-permute-start | bytes 221192 | tf_op jit(solution)/shard_map/ppermute | solution.py:38
  75.2 16.9 %all-to-all-start.4 = ((bf16[8,16,768]{2,1,0:T(8,128)(2,1)}), bf16[8,16,768]{2,1,0:T(8,128)(2,1)S(1)}, u32[]{:S(2)}, u32[]{:S(2)}) async-start(bf16[8,16,768]{2,1,0:T(8,128)(2,1)} %bitcast.18), calls=%async_computation.4 | async-start | bytes 393216 | tf_op jit(solution)/shard_map/all_to_all | solution.py:29
  80.7 5.8 %collective-permute-start.7 = (bf16[4,48,768]{2,1,0:T(8,128)(2,1)}, bf16[4,48,768]{2,1,0:T(8,128)(2,1)S(1)}, u32[]{:S(2)}, u32[]{:S(2)}) collective-permute-start(bf16[4,48,768]{2,1,0:T(8,128)(2,1)} %get-tuple-element.31.refs_1_), channel_id=1, source_target_pairs={{0,48},{16,0},{32,16},{48,32},{64,112},{80,64},{96,80},{112,96},{1... | collective-permute-start | bytes 884744 | tf_op jit(solution)/shard_map/ppermute | solution.py:38
  81.4 7.4 %collective-permute-start.6 = (bf16[4,48,768]{2,1,0:T(8,128)(2,1)}, bf16[4,48,768]{2,1,0:T(8,128)(2,1)S(1)}, u32[]{:S(2)}, u32[]{:S(2)}) collective-permute-start(bf16[4,48,768]{2,1,0:T(8,128)(2,1)} %get-tuple-element.31.refs_1_), channel_id=1, source_target_pairs={{0,32},{16,48},{32,0},{48,16},{64,96},{80,112},{96,64},{112,80},{1... | collective-permute-start | bytes 884744 | tf_op jit(solution)/shard_map/ppermute | solution.py:38
  82.4 9.7 %collective-permute-start.5 = (bf16[4,48,768]{2,1,0:T(8,128)(2,1)}, bf16[4,48,768]{2,1,0:T(8,128)(2,1)S(1)}, u32[]{:S(2)}, u32[]{:S(2)}) collective-permute-start(bf16[4,48,768]{2,1,0:T(8,128)(2,1)} %get-tuple-element.31.refs_1_), channel_id=1, source_target_pairs={{0,16},{16,32},{32,48},{48,0},{64,80},{80,96},{96,112},{112,64},{1... | collective-permute-start | bytes 884744 | tf_op jit(solution)/shard_map/ppermute | solution.py:38
  92.8 10.7 %all-to-all-start.5 = ((bf16[8,16,768]{2,1,0:T(8,128)(2,1)}), bf16[8,16,768]{2,1,0:T(8,128)(2,1)S(1)}, u32[]{:S(2)}, u32[]{:S(2)}) async-start(bf16[8,16,768]{2,1,0:T(8,128)(2,1)} %shard_map.153), calls=%async_computation.5 | async-start | bytes 393216 | tf_op jit(solution)/shard_map/all_to_all | solution.py:29
  97.7 0.9 copy-start.17
  100.4 1.0 copy-start.3
  101.5 0.7 copy-start.18
  103.5 1.3 copy-start.4
  104.7 1.0 copy-start.11
  105.7 0.9 copy-start.19
  107.7 13.4 %copy-start.13 = (f32[16,6144]{1,0:T(8,128)S(1)}, f32[16,6144]{1,0:T(8,128)}, u32[]{:S(2)}) copy-start(f32[16,6144]{1,0:T(8,128)} %copy-done.12) | copy-start | bytes 1179652
  107.7 13.4 %copy-start.15 = (f32[16,6144]{1,0:T(8,128)S(1)}, f32[16,6144]{1,0:T(8,128)}, u32[]{:S(2)}) copy-start(f32[16,6144]{1,0:T(8,128)} %copy-done.14) | copy-start | bytes 1179652
  122.3 20.3 %all-to-all-start.7 = ((bf16[16,16,768]{2,1,0:T(8,128)(2,1)}), bf16[16,16,768]{2,1,0:T(8,128)(2,1)S(1)}, u32[]{:S(2)}, u32[]{:S(2)}) async-start(bf16[16,16,768]{2,1,0:T(8,128)(2,1)} %get-tuple-element.42), calls=%async_computation.7 | async-start | bytes 786432 | tf_op jit(solution)/shard_map/all_to_all | solution.py:29
  131.7 29.1 %copy-start.9 = (f32[6,128,128]{2,1,0:T(8,128)S(1)}, f32[6,128,128]{2,1,0:T(8,128)}, u32[]{:S(2)}) copy-start(f32[6,128,128]{2,1,0:T(8,128)} %copy-done.8) | copy-start | bytes 1179652
  153.7 10.7 %collective-permute-start.8 = (bf16[16,768]{1,0:T(8,128)(2,1)S(1)}, bf16[16,768]{1,0:T(8,128)(2,1)S(1)}, u32[]{:S(2)}, u32[]{:S(2)}) collective-permute-start(bf16[16,768]{1,0:T(8,128)(2,1)S(1)} %shard_map.158.refs_0_), channel_id=1, source_target_pairs={{0,8},{8,0},{1,9},{9,1},{2,10},{10,2},{3,11},{11,3},{4,12},{12,4},... | collective-permute-start | bytes 73736 | tf_op jit(solution)/shard_map/ppermute | solution.py:25

commit v4 on v3

--- a/solution.py
+++ b/solution.py
@@ -79,7 +79,7 @@
     )
 
 
-def call(kernel, shapes, *inputs, places=None, after=()):
+def call(kernel, shapes, *inputs, places=None, after=(), scratch=()):
     skipped = len(after)
 
     def body(*refs):
@@ -92,6 +92,7 @@
         in_specs=[pl.BlockSpec(memory_space=pl.ANY)] * skipped
         + [pl.BlockSpec(memory_space=pltpu.SMEM)] * len(scalars)
         + [pl.BlockSpec(memory_space=pltpu.VMEM)] * len(inputs),
+        scratch_shapes=list(scratch),
         cost_estimate=pl.CostEstimate(flops=1, bytes_accessed=4_000_000, transcendentals=0),
         compiler_params=pltpu.CompilerParams(vmem_limit_bytes=VMEM_BYTES),
     )(*after, *scalars, *inputs)
@@ -106,6 +107,7 @@
         raised = jnp.exp(scores - jnp.max(scores, axis=-1, keepdims=True))
         chances = raised / jnp.sum(raised, axis=-1, keepdims=True)
         chance_ref[head] = chances
+        chance_ref[chance_ref.shape[0] // 2 + head] = chances.T
         mixture = times(chances.astype(jnp.bfloat16), value_ref[:, columns])
         context_ref[:, columns] = mixture.astype(jnp.bfloat16)
 
@@ -151,14 +153,29 @@
         out_ref[copy] = total
 
 
-def weight_kernel(places_ref, *refs):
-    scaled_ref, gain_ref, bias_ref, book_ref, scaled_code_ref, extra_ref = refs[N_LOW:]
+def feature_kernel(places_ref, *refs):
+    parts_ref, scaled_ref, residual_ref, gain_ref, bias_ref, out_ref, book_ref = refs[N_LOW:]
     for high in range(N_HIGH):
         for step in range(N_LOW):
+            piece = refs[step][high]
             place = high * N_LOW + (places_ref[2] + N_LOW - step) % N_LOW
-            book_ref[place] = refs[step][high]
-    features, width = scaled_ref.shape[1], book_ref.shape[2]
-    book = book_ref[...].reshape(features, width)
+            start = pl.multiple_of(place * piece.shape[0], EXTRA_ROWS)
+            book_ref[pl.ds(start, piece.shape[0])] = piece
+    count, rows, _ = out_ref.shape
+    features, width = book_ref.shape
+    book = book_ref[...]
+    code = parts_ref[...].reshape(count * rows, width)
+
+    def put(start, value):
+        value = value.astype(jnp.bfloat16)
+        out_ref[:, :, start : start + value.shape[1]] = value.reshape(count, rows, -1)
+
+    decoded = times_transposed(code, book)
+    put(3 * width, decoded)
+    hidden = residual_ref[...] + decoded
+    put(0, times(hidden.astype(jnp.bfloat16), book))
+    put(width, times((hidden * gain_ref[...]).astype(jnp.bfloat16), book))
+    put(2 * width, times(scaled_ref[...], book))
     row = lax.broadcasted_iota(jnp.int32, (EXTRA_ROWS, features), 0)
     rest = jnp.where(row == 0, 1.0, jnp.where(row == 1, gain_ref[...], 0.0))
     rest = jnp.where(row == 2, bias_ref[...], rest)
@@ -174,29 +191,9 @@
     half = width // 2
     extra = both[:, :half] + pltpu.roll(both[:, half:], 6, 0)
     wanted = places_ref[3].astype(jnp.float32)
-    extra = jnp.where(row[:, :half] == ORDER_ROW, wanted, extra)
-    extra_ref[...] = extra.astype(jnp.bfloat16)
-    scaled_code_ref[...] = times(scaled_ref[...], book).astype(jnp.bfloat16)
-
-
-def feature_kernel(code_ref, book_ref, residual_ref, gain_ref, scaled_ref, extra_ref, out_ref):
-    count, rows, _ = out_ref.shape
-    features, width = book_ref.shape
-    book = book_ref[...]
-    code = code_ref[...].reshape(count * rows, width)
-
-    def put(start, value):
-        value = value.astype(jnp.bfloat16)
-        out_ref[:, :, start : start + value.shape[1]] = value.reshape(count, rows, -1)
-
-    decoded = times_transposed(code, book)
-    put(3 * width, decoded)
-    hidden = residual_ref[...] + decoded
-    put(0, times(hidden.astype(jnp.bfloat16), book))
-    put(width, times((hidden * gain_ref[...]).astype(jnp.bfloat16), book))
-    put(2 * width, scaled_ref[...])
+    extra = jnp.where(row[:, :half] == ORDER_ROW, wanted, extra).astype(jnp.bfloat16)
     for copy in range(count):
-        out_ref[copy, :, 3 * width + features :] = extra_ref[...]
+        out_ref[copy, :, 3 * width + features :] = extra
 
 
 def row_kernel(
@@ -246,7 +243,8 @@
 def slot_kernel(order_ref, blocks_ref, grad_code_ref, out_ref):
     width = grad_code_ref.shape[1]
     for slot in range(out_ref.shape[0]):
-        out_ref[slot, :, :width] = blocks_ref[order_ref[slot] // N_TENSOR]
+        wanted = jnp.max(order_ref[slot, ORDER_ROW : ORDER_ROW + 1]).astype(jnp.int32)
+        out_ref[slot, :, :width] = blocks_ref[wanted // N_TENSOR]
         out_ref[slot, :, width:] = grad_code_ref[...]
 
 
@@ -268,20 +266,26 @@
     length, width = query_ref.shape
     code_width = joined_ref.shape[1]
     grad_code = both_ref[:, :, code_width:].reshape(length, code_width)
-    for head in range(width // HEAD):
-        columns = slice(head * HEAD, (head + 1) * HEAD)
-        grad_context = times_transposed(grad_code, joined_ref[columns]).astype(jnp.bfloat16)
-        chances = chance_ref[head]
-        grad_value = transposed_times(chances.astype(jnp.bfloat16), grad_context)
+    grad_context = times_transposed(grad_code, joined_ref[...]).astype(jnp.bfloat16)
+    heads = [slice(start, start + HEAD) for start in range(0, width, HEAD)]
+    grads = [grad_context[:, columns] for columns in heads]
+    near = [times_transposed(grad, value_ref[:, columns]) for grad, columns in zip(grads, heads)]
+    far = [times_transposed(value_ref[:, columns], grad) for grad, columns in zip(grads, heads)]
+    for head, columns in enumerate(heads):
+        grad_value = times(chance_ref[len(heads) + head].astype(jnp.bfloat16), grads[head])
         grad_value_ref[:, columns] = grad_value.astype(jnp.bfloat16)
-        grad_chances = times_transposed(grad_context, value_ref[:, columns])
+
+    def scores(grad_chances, chances, axis):
         grad_chances = grad_chances.astype(jnp.bfloat16).astype(jnp.float32)
-        shift = jnp.sum(grad_chances * chances, axis=-1, keepdims=True)
-        grad_scores = chances * (grad_chances - shift) * HEAD ** (-0.5)
-        grad_scores = grad_scores.astype(jnp.bfloat16)
-        grad_query = times(grad_scores, key_ref[:, columns])
+        shift = jnp.sum(grad_chances * chances, axis=axis, keepdims=True)
+        return (chances * (grad_chances - shift) * HEAD ** (-0.5)).astype(jnp.bfloat16)
+
+    near = [scores(grad, chance_ref[head], 1) for head, grad in enumerate(near)]
+    far = [scores(grad, chance_ref[len(heads) + head], 0) for head, grad in enumerate(far)]
+    for head, columns in enumerate(heads):
+        grad_query = times(near[head], key_ref[:, columns])
         grad_query_ref[:, columns] = grad_query.astype(jnp.bfloat16)
-        grad_key = transposed_times(grad_scores, query_ref[:, columns])
+        grad_key = times(far[head], query_ref[:, columns])
         grad_key_ref[:, columns] = grad_key.astype(jnp.bfloat16)
 
 
@@ -392,7 +396,7 @@
     joined_parts = exchanged(joined_rows.reshape(N_HIGH, share, code_width), "dp", HIGH_GROUPS)
     context, chances = call(
         attend_kernel,
-        [((length, heads * HEAD), bf16), ((heads, length, length), f32)],
+        [((length, heads * HEAD), bf16), ((2 * heads, length, length), f32)],
         queries[0, 0],
         key_vectors[0, 0],
         value_vectors[0, 0],
@@ -431,28 +435,17 @@
         total_kernel, [((n_tensor, rows, code_width), bf16)], code_parts, after=columns[1:]
     )
     code = exchanged(code_copies, "tensor")
-    book_here, scaled_code, extra = call(
-        weight_kernel,
-        [
-            ((n_dp, piece, code_width), bf16),
-            ((length, code_width), bf16),
-            ((EXTRA_ROWS, code_width // 2), bf16),
-        ],
+    (sent,) = call(
+        feature_kernel,
+        [((n_tensor, rows, 3 * code_width + features + code_width // 2), bf16)],
         *columns,
+        code,
         scaled_here,
+        residual_here,
         gain_here,
         bias_here,
         places=places,
-    )
-    (sent,) = call(
-        feature_kernel,
-        [((n_tensor, rows, 3 * code_width + features + code_width // 2), bf16)],
-        code,
-        book_here.reshape(features, code_width),
-        residual_here,
-        gain_here,
-        scaled_code,
-        extra,
+        scratch=[pltpu.VMEM((features, code_width), bf16)],
     )
     arrived = exchanged(sent, "tensor")
     codes, grad_code, grad_residual, orders = call(
@@ -469,13 +462,12 @@
     )
 
     blocks = exchanged(codes, "dp")
-    order_here = orders[:, ORDER_ROW, 0].astype(jnp.int32)
     (both,) = call(
         slot_kernel,
         [((n_tensor, rows, 2 * code_width), bf16)],
+        orders,
         blocks,
         grad_code,
-        places=order_here,
     )
     both = exchanged(both, "tensor")
     (chosen,) = call(chosen_kernel, [((rows, code_width), bf16)], both, places=wanted)

time: 166 us -> 161 us (0.970)
  blocking collectives: 36.3 us -> 65 us
  starting transfers between devices: 54.5 us -> 41.7 us
  waiting for transfers between devices: 39.4 us -> 28.2 us
  local copies, waits for them, and re-layouts: 13.7 us -> 7.11 us
  Pallas kernels: 16.6 us -> 13.5 us
    all_to_all x3 -> x5, blocking collectives: 36.3 us -> 65 us  [exchanged(): return lax.all_to_all(value, axis, 0, 0, axis_index_groups=groups)]
    all_to_all x6 -> x4, starting transfers between devices: 38.9 us -> 24.6 us  [exchanged(): return lax.all_to_all(value, axis, 0, 0, axis_index_groups=groups)]
    all_to_all x6 -> x4, waiting for transfers between devices: 23.6 us -> 12.3 us  [exchanged(): return lax.all_to_all(value, axis, 0, 0, axis_index_groups=groups)]
    unnamed x47 -> x39, local copies, waits for them, and re-layouts: 12.7 us -> 6.06 us
    pallas_call x14 -> x13, Pallas kernels: 16.6 us -> 13.5 us  [call(): pl.pallas_call(body, out_shape=[jax.ShapeDtypeStruct(shape, dtype) for sh...]
  transfers between devices with their start and end apart: 15 -> 13, of which waited for: 11 -> 9; matrix products, arithmetic and copies ran while one was open for 1% -> 1% of each run, Pallas kernels for 6% -> 4%
where the time goes in v4:
time: 161 us; the launch traced here: 160 us
  blocking collectives  65 us (40%)
  starting transfers between devices  41.7 us (26%)
  waiting for transfers between devices  28.2 us (18%)
  Pallas kernels  13.5 us (8%)
  local copies, waits for them, and re-layouts  7.11 us (4%)
  matrix products  2.87 us (2%)
    all_to_all x5, blocking collectives, exchanged(): return lax.all_to_all(value, axis, 0, 0, axis_index_groups=groups)  65 us
    all_to_all x4, starting transfers between devices, exchanged(): return lax.all_to_all(value, axis, 0, 0, axis_index_groups=groups)  24.6 us
    ppermute x6, waiting for transfers between devices, turned(): return lax.ppermute(value, 'dp', pairs)  15.9 us
    pallas_call x13, Pallas kernels, call(): pl.pallas_call(body, out_shape=[jax.ShapeDtypeStruct(shape, dtype) for sh...  13.5 us
    all_to_all x4, waiting for transfers between devices, exchanged(): return lax.all_to_all(value, axis, 0, 0, axis_index_groups=groups)  12.3 us
    ppermute x2, starting transfers between devices, swapped_2(): lax.ppermute(value, axis, [(i, i ^ 1 << distance) for i in range(lax.axis...  10.4 us
    unnamed x39, local copies, waits for them, and re-layouts  6.06 us
    ppermute x6, starting transfers between devices, turned(): return lax.ppermute(value, 'dp', pairs)  5.15 us
  transfers between devices with their start and end apart: 13, of which 9 were waited for; matrix products, arithmetic and copies ran while one was open for 1% of the time, Pallas kernels for 4%

profile of v4, /device:TPU:1, one launch (start us, length us, event | category | flops | bytes accessed | tf_op | source)
XLA Modules:
  0.0 159.9 jit_solution(6076731889367916734)
XLA Ops:
  0.6 0.0 copy-start
  0.6 1.1 copy-done
  1.7 2.9 %convolution_convert_fusion.refs_0_ = bf16[768,768]{1,0:T(8,128)(2,1)} fusion(bf16[1,384,768]{2,1,0:T(8,128)(2,1)S(1)} %copy-done, bf16[1,768,384]{2,1,0:T(8,128)(2,1)} %param.16), kind=kOutput, calls=%fused_computation | convolution fusion | flops 453574656 | bytes 2359296 | tf_op jit(solution)/shard_map/dot_general | solution.py:67
  4.6 5.1 %all-to-all-start = ((bf16[4,192,768]{2,1,0:T(8,128)(2,1)}), bf16[4,192,768]{2,1,0:T(8,128)(2,1)S(1)}, u32[]{:S(2)}, u32[]{:S(2)}) async-start(bf16[4,192,768]{2,1,0:T(8,128)(2,1)} %bitcast.9), calls=%async_computation | async-start | bytes 2359296 | tf_op jit(solution)/shard_map/all_to_all | solution.py:29
  9.7 1.9 %collective-permute-start = (s32[1]{0:T(128)}, s32[1]{0:T(128)}, u32[]{:S(2)}, u32[]{:S(2)}) collective-permute-start(s32[1]{0:T(128)} %bitcast), channel_id=1, source_target_pairs={{0,8},{8,0},{1,9},{9,1},{2,10},{10,2},{3,11},{11,3},{4,12},{12,4},... | collective-permute-start | bytes 20 | tf_op jit(solution)/shard_map/ppermute | solution.py:25
  11.6 0.6 dynamic-slice_bitcast_fusion
  12.2 1.5 collective-permute-start.1
  13.7 0.0 collective-permute-done.refs_0_
  13.7 0.8 pad_add_fusion.refs_1_.refs_0_
  14.5 0.0 copy-done.1
  14.5 0.0 copy-done.16
  14.5 0.0 copy-done.17
  14.5 0.0 copy-start.2
  14.5 1.4 copy-done.2
  15.9 1.3 shard_map.146
  17.3 0.0 copy-start.8
  17.3 0.7 copy-done.8
  18.0 0.8 copy-done.10
  18.8 0.8 copy-done.12
  19.5 0.7 copy-done.14
  20.2 0.0 collective-permute-done.1.refs_0_.refs_1_
  20.2 4.3 %all-to-all-done.refs_2_ = bf16[4,192,768]{2,1,0:T(8,128)(2,1)S(1)} async-done(((bf16[4,192,768]{2,1,0:T(8,128)(2,1)}), bf16[4,192,768]{2,1,0:T(8,128)(2,1)S(1)}, u32[]{:S(2)}, u32[]{:S(2)}) %all-to-all-start) | async-done | bytes 1179680 | tf_op jit(solution)/shard_map/all_to_all | solution.py:29
  24.5 0.9 shard_map.147.refs_0_
  25.4 9.0 %all-to-all-start.1 = ((bf16[4,48,768]{2,1,0:T(8,128)(2,1)}), bf16[4,48,768]{2,1,0:T(8,128)(2,1)S(1)}, u32[]{:S(2)}, u32[]{:S(2)}) async-start(bf16[4,48,768]{2,1,0:T(8,128)(2,1)} %bitcast.15), calls=%async_computation.1 | async-start | bytes 589824 | tf_op jit(solution)/shard_map/all_to_all | solution.py:29
  34.4 0.1 copy.16
  34.5 0.1 broadcast_in_dim.21
  34.5 0.1 eq.22
  34.6 0.1 copy.17
  34.8 2.1 %shard_map.148 = (bf16[128,768]{1,0:T(8,128)(2,1)S(1)}, f32[12,128,128]{2,1,0:T(8,128)S(1)}) custom-call(bf16[192,768]{1,0:T(8,128)(2,1)} %shard_map.147.refs_0_, bf16[128,768]{1,0:T(8,128)(2,1)S(1)} %bitcast.37, bf16[128,768]{1,0:T(8,128)(2,1)S(1)} %bitcast.39, bf16[128,768]{1,0:T(8,128)(2,1)S(1)} %bitcast.41, f32[128,128]{1,0:T(8,128)S(1)} %fusion.3.refs_4_), custom_call_target="tpu_custom_call" | custom-call | flops 1 | bytes 4000000 | tf_op jit(solution)/shard_map/pallas_call | solution.py:89
  36.9 5.8 %all-to-all-done.1.refs_1_ = bf16[4,48,768]{2,1,0:T(8,128)(2,1)S(1)} async-done(((bf16[4,48,768]{2,1,0:T(8,128)(2,1)}), bf16[4,48,768]{2,1,0:T(8,128)(2,1)S(1)}, u32[]{:S(2)}, u32[]{:S(2)}) %all-to-all-start.1) | async-done | bytes 294944 | tf_op jit(solution)/shard_map/all_to_all | solution.py:29
  42.7 12.9 %all_to_all.45 = bf16[4,48,768]{2,1,0:T(8,128)(2,1)S(1)} all-to-all(bf16[4,48,768]{2,1,0:T(8,128)(2,1)S(1)} %shard_map.149), channel_id=1, replica_groups={{0,64,128,192},{16,80,144,208},{32,96,160,224},{48,112,176,240},{1,65,1..., dimensions={0} | all-to-all | bytes 589824 | tf_op jit(solution)/shard_map/all_to_all | solution.py:29
  55.6 1.1 shard_map.150
  56.7 5.1 %all-to-all-start.3 = ((bf16[4,192,768]{2,1,0:T(8,128)(2,1)}), bf16[4,192,768]{2,1,0:T(8,128)(2,1)S(1)}, u32[]{:S(2)}, u32[]{:S(2)}) async-start(bf16[4,192,768]{2,1,0:T(8,128)(2,1)} %get-tuple-element.26), calls=%async_computation.3 | async-start | bytes 2359296 | tf_op jit(solution)/shard_map/all_to_all | solution.py:29
  61.8 0.9 collective-permute-start.4
  62.7 1.9 %collective-permute-start.3 = (bf16[48,768]{1,0:T(8,128)(2,1)S(1)}, bf16[48,768]{1,0:T(8,128)(2,1)S(1)}, u32[]{:S(2)}, u32[]{:S(2)}) collective-permute-start(bf16[48,768]{1,0:T(8,128)(2,1)S(1)} %get-tuple-element.27.refs_1_), channel_id=1, source_target_pairs={{0,128},{16,144},{32,160},{48,176},{64,192},{80,208},{96,224},{112... | collective-permute-start | bytes 221192 | tf_op jit(solution)/shard_map/ppermute | solution.py:38
  64.6 0.6 collective-permute-start.2
  65.2 1.4 collective-permute-done.4.refs_4_
  66.6 4.7 %collective-permute-done.3.refs_3_ = bf16[48,768]{1,0:T(8,128)(2,1)S(1)} collective-permute-done((bf16[48,768]{1,0:T(8,128)(2,1)S(1)}, bf16[48,768]{1,0:T(8,128)(2,1)S(1)}, u32[]{:S(2)}, u32[]{:S(2)}) %collective-permute-start.3) | collective-permute-done | bytes 73760 | tf_op jit(solution)/shard_map/ppermute | solution.py:38
  71.3 0.1 collective-permute-done.2.refs_2_
  71.4 0.6 shard_map.151.refs_2_
  72.0 2.2 %all-to-all-done.3 = bf16[4,192,768]{2,1,0:T(8,128)(2,1)S(1)} async-done(((bf16[4,192,768]{2,1,0:T(8,128)(2,1)}), bf16[4,192,768]{2,1,0:T(8,128)(2,1)S(1)}, u32[]{:S(2)}, u32[]{:S(2)}) %all-to-all-start.3) | async-done | bytes 1179680 | tf_op jit(solution)/shard_map/all_to_all | solution.py:29
  74.2 1.0 shard_map.152
  75.2 5.4 %all-to-all-start.4 = ((bf16[8,16,768]{2,1,0:T(8,128)(2,1)}), bf16[8,16,768]{2,1,0:T(8,128)(2,1)S(1)}, u32[]{:S(2)}, u32[]{:S(2)}) async-start(bf16[8,16,768]{2,1,0:T(8,128)(2,1)} %bitcast.18), calls=%async_computation.4 | async-start | bytes 393216 | tf_op jit(solution)/shard_map/all_to_all | solution.py:29
  80.7 0.7 collective-permute-start.7
  81.4 1.1 collective-permute-start.6
  82.4 0.0 collective-permute-start.5
  82.5 4.0 %collective-permute-done.7.refs_2_.refs_4_ = bf16[4,48,768]{2,1,0:T(8,128)(2,1)S(1)} collective-permute-done((bf16[4,48,768]{2,1,0:T(8,128)(2,1)}, bf16[4,48,768]{2,1,0:T(8,128)(2,1)S(1)}, u32[]{:S(2)}, u32[]{:S(2)}) %collective-permute-start.7) | collective-permute-done | bytes 294944 | tf_op jit(solution)/shard_map/ppermute | solution.py:38
  86.5 2.3 %collective-permute-done.6.refs_1_.refs_3_ = bf16[4,48,768]{2,1,0:T(8,128)(2,1)S(1)} collective-permute-done((bf16[4,48,768]{2,1,0:T(8,128)(2,1)}, bf16[4,48,768]{2,1,0:T(8,128)(2,1)S(1)}, u32[]{:S(2)}, u32[]{:S(2)}) %collective-permute-start.6) | collective-permute-done | bytes 294944 | tf_op jit(solution)/shard_map/ppermute | solution.py:38
  88.7 3.4 %collective-permute-done.5.refs_0_.refs_2_ = bf16[4,48,768]{2,1,0:T(8,128)(2,1)S(1)} collective-permute-done((bf16[4,48,768]{2,1,0:T(8,128)(2,1)}, bf16[4,48,768]{2,1,0:T(8,128)(2,1)S(1)}, u32[]{:S(2)}, u32[]{:S(2)}) %collective-permute-start.5) | collective-permute-done | bytes 294944 | tf_op jit(solution)/shard_map/ppermute | solution.py:38
  92.1 0.0 all-to-all-done.4.refs_3_
  92.1 10.6 %all_to_all.46.refs_5_ = bf16[8,16,768]{2,1,0:T(8,128)(2,1)S(1)} all-to-all(bf16[8,16,768]{2,1,0:T(8,128)(2,1)S(1)} %shard_map.153), channel_id=1, replica_groups=mesh['dp'=16,'section'=2,'tensor'=8] {'tensor'}, dimensions={0} | all-to-all | bytes 393216 | tf_op jit(solution)/shard_map/all_to_all | solution.py:29
  102.7 2.8 %shard_map.154 = bf16[8,16,3456]{2,1,0:T(8,128)(2,1)S(1)} custom-call(s32[4]{0:T(128)S(1)} %pad_add_fusion.refs_1_.refs_0_, bf16[4,48,768]{2,1,0:T(8,128)(2,1)} %get-tuple-element.28.refs_1_, bf16[4,48,768]{2,1,0:T(8,128)(2,1)S(1)} %collective-permute-done.5.refs_0_.refs_2_, bf16[4,48,768]{2,1,0:T(8,128)(2,1)S(1)} %collective-permute-done.6.refs_1_.refs_3_, ...), custom_call_target="tpu_custom_call" | custom-call | flops 1 | bytes 4000000 | tf_op jit(solution)/shard_map/pallas_call | solution.py:89
  105.6 12.1 %all_to_all.47.refs_0_ = bf16[8,16,3456]{2,1,0:T(8,128)(2,1)S(1)} all-to-all(bf16[8,16,3456]{2,1,0:T(8,128)(2,1)S(1)} %shard_map.154), channel_id=1, replica_groups=mesh['dp'=16,'section'=2,'tensor'=8] {'tensor'}, dimensions={0} | all-to-all | bytes 1769472 | tf_op jit(solution)/shard_map/all_to_all | solution.py:29
  117.7 0.0 copy-done.9
  117.7 1.0 shard_map.155
  118.8 19.9 %all_to_all.48.refs_1_ = bf16[16,16,768]{2,1,0:T(8,128)(2,1)S(1)} all-to-all(bf16[16,16,768]{2,1,0:T(8,128)(2,1)S(1)} %get-tuple-element.36), channel_id=1, replica_groups=mesh['dp'=16,'section'=2,'tensor'=8] {'dp'}, dimensions={0} | all-to-all | bytes 786432 | tf_op jit(solution)/shard_map/all_to_all | solution.py:29
  138.7 0.2 shard_map.156
  138.9 9.5 %all_to_all.49.refs_1_ = bf16[8,16,1536]{2,1,0:T(8,128)(2,1)S(1)} all-to-all(bf16[8,16,1536]{2,1,0:T(8,128)(2,1)S(1)} %shard_map.156), channel_id=1, replica_groups=mesh['dp'=16,'section'=2,'tensor'=8] {'tensor'}, dimensions={0} | all-to-all | bytes 786432 | tf_op jit(solution)/shard_map/all_to_all | solution.py:29
  148.3 0.7 shard_map.157.refs_0_
  149.0 8.5 %collective-permute-start.8 = (bf16[16,768]{1,0:T(8,128)(2,1)S(1)}, bf16[16,768]{1,0:T(8,128)(2,1)S(1)}, u32[]{:S(2)}, u32[]{:S(2)}) collective-permute-start(bf16[16,768]{1,0:T(8,128)(2,1)S(1)} %shard_map.157.refs_0_), channel_id=1, source_target_pairs={{0,8},{8,0},{1,9},{9,1},{2,10},{10,2},{3,11},{11,3},{4,12},{12,4},... | collective-permute-start | bytes 73736 | tf_op jit(solution)/shard_map/ppermute | solution.py:25
  157.5 0.0 copy-done.4
  157.5 1.8 %shard_map.158 = (bf16[128,768]{1,0:T(8,128)(2,1)}, bf16[128,768]{1,0:T(8,128)(2,1)}, bf16[128,768]{1,0:T(8,128)(2,1)}) custom-call(bf16[16,768]{1,0:T(8,128)(2,1)S(1)} %shard_map.157.refs_0_, bf16[8,16,1536]{2,1,0:T(8,128)(2,1)S(1)} %all_to_all.49.refs_1_, bf16[768,768]{1,0:T(8,128)(2,1)S(1)} %bitcast.33, bf16[128,768]{1,0:T(8,128)(2,1)S(1)} %bitcast.38, ...), custom_call_target="tpu_custom_call" | custom-call | flops 1 | bytes 4000000 | tf_op jit(solution)/shard_map/pallas_call | solution.py:89
  159.3 0.0 collective-permute-done.8
  159.3 0.6 copy.19
  (29 shorter events, 0.2 us)
Async XLA Ops:
  0.6 1.1 copy-start
  4.6 9.9 %copy-start.1 = (bf16[1,1,128,6144]{3,2,1,0:T(8,128)(2,1)S(1)}, bf16[1,1,128,6144]{3,2,1,0:T(8,128)(2,1)}, u32[]{:S(2)}) copy-start(bf16[1,1,128,6144]{3,2,1,0:T(8,128)(2,1)} %param.11) | copy-start | bytes 4718596
  4.6 9.9 %copy-start.16 = (f32[1,6144]{1,0:T(1,128)S(1)}, f32[1,6144]{1,0:T(1,128)}, u32[]{:S(2)}) copy-start(f32[1,6144]{1,0:T(1,128)} %refs_4_.1) | copy-start | bytes 73732
  4.6 9.9 %copy-start.17 = (f32[1,6144]{1,0:T(1,128)S(1)}, f32[1,6144]{1,0:T(1,128)}, u32[]{:S(2)}) copy-start(f32[1,6144]{1,0:T(1,128)} %refs_5_.1) | copy-start | bytes 73732
  4.6 19.9 %all-to-all-start = ((bf16[4,192,768]{2,1,0:T(8,128)(2,1)}), bf16[4,192,768]{2,1,0:T(8,128)(2,1)S(1)}, u32[]{:S(2)}, u32[]{:S(2)}) async-start(bf16[4,192,768]{2,1,0:T(8,128)(2,1)} %bitcast.9), calls=%async_computation | async-start | bytes 2359296 | tf_op jit(solution)/shard_map/all_to_all | solution.py:29
  9.7 4.0 %collective-permute-start = (s32[1]{0:T(128)}, s32[1]{0:T(128)}, u32[]{:S(2)}, u32[]{:S(2)}) collective-permute-start(s32[1]{0:T(128)} %bitcast), channel_id=1, source_target_pairs={{0,8},{8,0},{1,9},{9,1},{2,10},{10,2},{3,11},{11,3},{4,12},{12,4},... | collective-permute-start | bytes 20 | tf_op jit(solution)/shard_map/ppermute | solution.py:25
  12.2 8.0 %collective-permute-start.1 = (bf16[48,768]{1,0:T(8,128)(2,1)}, bf16[48,768]{1,0:T(8,128)(2,1)S(1)}, u32[]{:S(2)}, u32[]{:S(2)}) collective-permute-start(bf16[48,768]{1,0:T(8,128)(2,1)} %dynamic-slice_bitcast_fusion), channel_id=1, source_target_pairs={{0,0},{1,16},{2,32},{3,48},{4,64},{5,80},{6,96},{7,112},{16,1},{17... | collective-permute-start | bytes 221192 | tf_op jit(solution)/shard_map/ppermute | solution.py:48
  14.5 1.4 copy-start.2
  17.3 0.8 copy-start.8
  18.0 0.8 copy-start.10
  18.8 0.8 copy-start.12
  19.5 0.7 copy-start.14
  20.2 14.1 %copy-start.18 = (s32[1,1,4,4]{3,2,1,0:T(4,128)S(1)}, s32[1,1,4,4]{3,2,1,0:T(4,128)}, u32[]{:S(2)}) copy-start(s32[1,1,4,4]{3,2,1,0:T(4,128)} %param.15) | copy-start | bytes 196
  20.2 14.6 %copy-start.5 = (bf16[1,1,128,768]{3,2,1,0:T(8,128)(2,1)S(1)}, bf16[1,1,128,768]{3,2,1,0:T(8,128)(2,1)}, u32[]{:S(2)}) copy-start(bf16[1,1,128,768]{3,2,1,0:T(8,128)(2,1)} %param.12) | copy-start | bytes 589828
  20.2 14.6 %copy-start.6 = (bf16[1,1,128,768]{3,2,1,0:T(8,128)(2,1)S(1)}, bf16[1,1,128,768]{3,2,1,0:T(8,128)(2,1)}, u32[]{:S(2)}) copy-start(bf16[1,1,128,768]{3,2,1,0:T(8,128)(2,1)} %param.13) | copy-start | bytes 589828
  20.2 14.6 %copy-start.7 = (bf16[1,1,128,768]{3,2,1,0:T(8,128)(2,1)S(1)}, bf16[1,1,128,768]{3,2,1,0:T(8,128)(2,1)}, u32[]{:S(2)}) copy-start(bf16[1,1,128,768]{3,2,1,0:T(8,128)(2,1)} %param.14) | copy-start | bytes 589828
  25.4 17.3 %all-to-all-start.1 = ((bf16[4,48,768]{2,1,0:T(8,128)(2,1)}), bf16[4,48,768]{2,1,0:T(8,128)(2,1)S(1)}, u32[]{:S(2)}, u32[]{:S(2)}) async-start(bf16[4,48,768]{2,1,0:T(8,128)(2,1)} %bitcast.15), calls=%async_computation.1 | async-start | bytes 589824 | tf_op jit(solution)/shard_map/all_to_all | solution.py:29
  36.9 19.8 %copy-start.3 = (f32[12,128,128]{2,1,0:T(8,128)}, f32[12,128,128]{2,1,0:T(8,128)S(1)}, u32[]{:S(2)}) copy-start(f32[12,128,128]{2,1,0:T(8,128)S(1)} %get-tuple-element.39.refs_6_) | copy-start | bytes 2359300
  56.7 17.5 %all-to-all-start.3 = ((bf16[4,192,768]{2,1,0:T(8,128)(2,1)}), bf16[4,192,768]{2,1,0:T(8,128)(2,1)S(1)}, u32[]{:S(2)}, u32[]{:S(2)}) async-start(bf16[4,192,768]{2,1,0:T(8,128)(2,1)} %get-tuple-element.26), calls=%async_computation.3 | async-start | bytes 2359296 | tf_op jit(solution)/shard_map/all_to_all | solution.py:29
  61.8 4.8 %collective-permute-start.4 = (bf16[48,768]{1,0:T(8,128)(2,1)S(1)}, bf16[48,768]{1,0:T(8,128)(2,1)S(1)}, u32[]{:S(2)}, u32[]{:S(2)}) collective-permute-start(bf16[48,768]{1,0:T(8,128)(2,1)S(1)} %get-tuple-element.27.refs_1_), channel_id=1, source_target_pairs={{0,192},{16,208},{32,224},{48,240},{64,0},{80,16},{96,32},{112,48}... | collective-permute-start | bytes 221192 | tf_op jit(solution)/shard_map/ppermute | solution.py:38
  62.7 8.6 %collective-permute-start.3 = (bf16[48,768]{1,0:T(8,128)(2,1)S(1)}, bf16[48,768]{1,0:T(8,128)(2,1)S(1)}, u32[]{:S(2)}, u32[]{:S(2)}) collective-permute-start(bf16[48,768]{1,0:T(8,128)(2,1)S(1)} %get-tuple-element.27.refs_1_), channel_id=1, source_target_pairs={{0,128},{16,144},{32,160},{48,176},{64,192},{80,208},{96,224},{112... | collective-permute-start | bytes 221192 | tf_op jit(solution)/shard_map/ppermute | solution.py:38
  64.6 6.8 %collective-permute-start.2 = (bf16[48,768]{1,0:T(8,128)(2,1)S(1)}, bf16[48,768]{1,0:T(8,128)(2,1)S(1)}, u32[]{:S(2)}, u32[]{:S(2)}) collective-permute-start(bf16[48,768]{1,0:T(8,128)(2,1)S(1)} %get-tuple-element.27.refs_1_), channel_id=1, source_target_pairs={{0,64},{16,80},{32,96},{48,112},{64,128},{80,144},{96,160},{112,17... | collective-permute-start | bytes 221192 | tf_op jit(solution)/shard_map/ppermute | solution.py:38
  75.2 16.9 %all-to-all-start.4 = ((bf16[8,16,768]{2,1,0:T(8,128)(2,1)}), bf16[8,16,768]{2,1,0:T(8,128)(2,1)S(1)}, u32[]{:S(2)}, u32[]{:S(2)}) async-start(bf16[8,16,768]{2,1,0:T(8,128)(2,1)} %bitcast.18), calls=%async_computation.4 | async-start | bytes 393216 | tf_op jit(solution)/shard_map/all_to_all | solution.py:29
  80.7 5.8 %collective-permute-start.7 = (bf16[4,48,768]{2,1,0:T(8,128)(2,1)}, bf16[4,48,768]{2,1,0:T(8,128)(2,1)S(1)}, u32[]{:S(2)}, u32[]{:S(2)}) collective-permute-start(bf16[4,48,768]{2,1,0:T(8,128)(2,1)} %get-tuple-element.28.refs_1_), channel_id=1, source_target_pairs={{0,48},{16,0},{32,16},{48,32},{64,112},{80,64},{96,80},{112,96},{1... | collective-permute-start | bytes 884744 | tf_op jit(solution)/shard_map/ppermute | solution.py:38
  81.4 7.4 %collective-permute-start.6 = (bf16[4,48,768]{2,1,0:T(8,128)(2,1)}, bf16[4,48,768]{2,1,0:T(8,128)(2,1)S(1)}, u32[]{:S(2)}, u32[]{:S(2)}) collective-permute-start(bf16[4,48,768]{2,1,0:T(8,128)(2,1)} %get-tuple-element.28.refs_1_), channel_id=1, source_target_pairs={{0,32},{16,48},{32,0},{48,16},{64,96},{80,112},{96,64},{112,80},{1... | collective-permute-start | bytes 884744 | tf_op jit(solution)/shard_map/ppermute | solution.py:38
  82.4 9.6 %collective-permute-start.5 = (bf16[4,48,768]{2,1,0:T(8,128)(2,1)}, bf16[4,48,768]{2,1,0:T(8,128)(2,1)S(1)}, u32[]{:S(2)}, u32[]{:S(2)}) collective-permute-start(bf16[4,48,768]{2,1,0:T(8,128)(2,1)} %get-tuple-element.28.refs_1_), channel_id=1, source_target_pairs={{0,16},{16,32},{32,48},{48,0},{64,80},{80,96},{96,112},{112,64},{1... | collective-permute-start | bytes 884744 | tf_op jit(solution)/shard_map/ppermute | solution.py:38
  92.1 10.6 %copy-start.13 = (f32[128,768]{1,0:T(8,128)S(1)}, f32[128,768]{1,0:T(8,128)}, u32[]{:S(2)}) copy-start(f32[128,768]{1,0:T(8,128)} %copy-done.12) | copy-start | bytes 1179652
  92.1 10.6 %copy-start.15 = (bf16[128,768]{1,0:T(8,128)(2,1)S(1)}, bf16[128,768]{1,0:T(8,128)(2,1)}, u32[]{:S(2)}) copy-start(bf16[128,768]{1,0:T(8,128)(2,1)} %copy-done.14) | copy-start | bytes 589828
  105.6 12.2 %copy-start.9 = (f32[16,6144]{1,0:T(8,128)S(1)}, f32[16,6144]{1,0:T(8,128)}, u32[]{:S(2)}) copy-start(f32[16,6144]{1,0:T(8,128)} %copy-done.8) | copy-start | bytes 1179652
  105.6 12.1 %copy-start.11 = (f32[16,6144]{1,0:T(8,128)S(1)}, f32[16,6144]{1,0:T(8,128)}, u32[]{:S(2)}) copy-start(f32[16,6144]{1,0:T(8,128)} %copy-done.10) | copy-start | bytes 1179652
  138.7 18.9 %copy-start.4 = (f32[12,128,128]{2,1,0:T(8,128)S(1)}, f32[12,128,128]{2,1,0:T(8,128)}, u32[]{:S(2)}) copy-start(f32[12,128,128]{2,1,0:T(8,128)} %copy-done.3) | copy-start | bytes 2359300
  149.0 10.3 %collective-permute-start.8 = (bf16[16,768]{1,0:T(8,128)(2,1)S(1)}, bf16[16,768]{1,0:T(8,128)(2,1)S(1)}, u32[]{:S(2)}, u32[]{:S(2)}) collective-permute-start(bf16[16,768]{1,0:T(8,128)(2,1)S(1)} %shard_map.157.refs_0_), channel_id=1, source_target_pairs={{0,8},{8,0},{1,9},{9,1},{2,10},{10,2},{3,11},{11,3},{4,12},{12,4},... | collective-permute-start | bytes 73736 | tf_op jit(solution)/shard_map/ppermute | solution.py:25

commit v5 on v4

--- a/solution.py
+++ b/solution.py
@@ -16,7 +16,7 @@
 N_TENSOR = 8
 EXTRA_ROWS = 16
 ORDER_ROW = 12
-VMEM_BYTES = 20 * 1024 * 1024
+VMEM_BYTES = 12 * 1024 * 1024
 HIGH_GROUPS = [[z * N_LOW + y for z in range(N_HIGH)] for y in range(N_LOW)]
 LOW_GROUPS = [[z * N_LOW + y for y in range(N_LOW)] for z in range(N_HIGH)]
 
@@ -141,7 +141,9 @@
 
 def code_kernel(context_ref, joined_ref, column_ref, code_ref, column_copy_ref):
     column_copy_ref[...] = column_ref[...]
-    code_ref[...] = times(context_ref[...], joined_ref[...]).astype(jnp.bfloat16)
+    code = times(context_ref[...], joined_ref[...]).astype(jnp.bfloat16)
+    for copy in range(code_ref.shape[0]):
+        code_ref[copy] = code
 
 
 def total_kernel(parts_ref, out_ref):
@@ -153,29 +155,20 @@
         out_ref[copy] = total
 
 
-def feature_kernel(places_ref, *refs):
-    parts_ref, scaled_ref, residual_ref, gain_ref, bias_ref, out_ref, book_ref = refs[N_LOW:]
+def pack_kernel(places_ref, *refs):
+    here_ref, gain_ref, bias_ref, pack_ref = refs[N_LOW:]
     for high in range(N_HIGH):
         for step in range(N_LOW):
             piece = refs[step][high]
             place = high * N_LOW + (places_ref[2] + N_LOW - step) % N_LOW
             start = pl.multiple_of(place * piece.shape[0], EXTRA_ROWS)
-            book_ref[pl.ds(start, piece.shape[0])] = piece
-    count, rows, _ = out_ref.shape
-    features, width = book_ref.shape
-    book = book_ref[...]
-    code = parts_ref[...].reshape(count * rows, width)
-
-    def put(start, value):
-        value = value.astype(jnp.bfloat16)
-        out_ref[:, :, start : start + value.shape[1]] = value.reshape(count, rows, -1)
-
-    decoded = times_transposed(code, book)
-    put(3 * width, decoded)
-    hidden = residual_ref[...] + decoded
-    put(0, times(hidden.astype(jnp.bfloat16), book))
-    put(width, times((hidden * gain_ref[...]).astype(jnp.bfloat16), book))
-    put(2 * width, times(scaled_ref[...], book))
+            pack_ref[pl.ds(start, piece.shape[0])] = piece
+    _, length, features = here_ref.shape
+    width = pack_ref.shape[1]
+    book = pack_ref[:features]
+    pack_ref[features : features + length] = times(here_ref[0], book).astype(jnp.bfloat16)
+    pack_ref[features + length : features + 2 * length] = here_ref[1]
+    pack_ref[features + 2 * length : features + 3 * length] = here_ref[2]
     row = lax.broadcasted_iota(jnp.int32, (EXTRA_ROWS, features), 0)
     rest = jnp.where(row == 0, 1.0, jnp.where(row == 1, gain_ref[...], 0.0))
     rest = jnp.where(row == 2, bias_ref[...], rest)
@@ -192,6 +185,34 @@
     extra = both[:, :half] + pltpu.roll(both[:, half:], 6, 0)
     wanted = places_ref[3].astype(jnp.float32)
     extra = jnp.where(row[:, :half] == ORDER_ROW, wanted, extra).astype(jnp.bfloat16)
+    pack_ref[features + 3 * length :, :half] = extra
+    pack_ref[features + 3 * length :, half:] = extra
+
+
+def feature_kernel(parts_ref, pack_ref, gain_ref, out_ref):
+    count, rows, _ = out_ref.shape
+    features = gain_ref.shape[1]
+    width = pack_ref.shape[1]
+    length = count * rows
+    book = pack_ref[:features]
+    total = parts_ref[0].astype(jnp.float32)
+    for part in range(1, count):
+        total += parts_ref[part].astype(jnp.float32)
+    code = total.astype(jnp.bfloat16)
+
+    def put(start, value):
+        value = value.astype(jnp.bfloat16)
+        out_ref[:, :, start : start + value.shape[1]] = value.reshape(count, rows, -1)
+
+    decoded = times_transposed(code, book)
+    put(3 * width, decoded)
+    upper = pack_ref[features + length : features + 2 * length].astype(jnp.float32)
+    lower = pack_ref[features + 2 * length : features + 3 * length].astype(jnp.float32)
+    hidden = upper + lower + decoded
+    put(0, times(hidden.astype(jnp.bfloat16), book))
+    put(width, times((hidden * gain_ref[...]).astype(jnp.bfloat16), book))
+    put(2 * width, pack_ref[features : features + length])
+    extra = pack_ref[features + 3 * length :, : width // 2]
     for copy in range(count):
         out_ref[copy, :, 3 * width + features :] = extra
 
@@ -295,8 +316,7 @@
     upstream_ref,
     gain_ref,
     bias_ref,
-    residual_here_ref,
-    scaled_here_ref,
+    here_ref,
     gain_here_ref,
     bias_here_ref,
     residual_rows_ref,
@@ -331,9 +351,12 @@
         scaled_mean = jnp.sum(wide, axis=-1, keepdims=True) / width
         for half in range(2):
             here, there = places(half)
-            residual_here_ref[block, here] = residual_ref[block, there].astype(jnp.float32) - mean
             scaled = upstream_ref[block, there].astype(jnp.float32) * gain_ref[:, there]
-            scaled_here_ref[block, here] = (scaled - scaled_mean).astype(jnp.bfloat16)
+            here_ref[0, block, here] = (scaled - scaled_mean).astype(jnp.bfloat16)
+            local = residual_ref[block, there].astype(jnp.float32) - mean
+            upper = local.astype(jnp.bfloat16)
+            here_ref[1, block, here] = upper
+            here_ref[2, block, here] = (local - upper.astype(jnp.float32)).astype(jnp.bfloat16)
     own = pl.multiple_of(rank * rows, rows)
     residual_rows_ref[...] = centered(residual_ref, own, None)
     scaled_rows_ref[...] = centered(upstream_ref, own, gain)
@@ -373,11 +396,10 @@
     joined_parts = exchanged(joined_part.reshape(N_LOW, -1, code_width), "dp", LOW_GROUPS)
     own_slice = lax.dynamic_slice_in_dim(code_book, rank * piece, piece, 0)
     own_slice = transposed_owner(own_slice, n_tensor)
-    residual_here, scaled_here, gain_here, bias_here, residual_rows, scaled_rows = call(
+    here, gain_here, bias_here, residual_rows, scaled_rows = call(
         prepare_kernel,
         [
-            ((length, features), f32),
-            ((length, features), bf16),
+            ((3, length, features), bf16),
             ((1, features), f32),
             ((1, features), f32),
             ((rows, width), f32),
@@ -422,30 +444,30 @@
         *[turned(own_slice, step, 0) for step in range(1, N_HIGH)],
         places=places,
     )
-    code_part, column = call(
+    sent, column = call(
         code_kernel,
-        [((length, code_width), bf16), ((N_HIGH, piece, code_width), bf16)],
+        [((n_tensor, length, code_width), bf16), ((N_HIGH, piece, code_width), bf16)],
         context,
         joined,
         column,
     )
     columns = [column] + [turned(column, 0, step) for step in range(1, N_LOW)]
-    code_parts = exchanged(code_part.reshape(n_tensor, rows, code_width), "tensor")
-    (code_copies,) = call(
-        total_kernel, [((n_tensor, rows, code_width), bf16)], code_parts, after=columns[1:]
-    )
-    code = exchanged(code_copies, "tensor")
+    code_parts = exchanged(sent, "tensor")
+    (pack,) = call(
+        pack_kernel,
+        [((features + 3 * length + EXTRA_ROWS, code_width), bf16)],
+        *columns,
+        here,
+        gain_here,
+        bias_here,
+        places=places,
+    )
     (sent,) = call(
         feature_kernel,
         [((n_tensor, rows, 3 * code_width + features + code_width // 2), bf16)],
-        *columns,
-        code,
-        scaled_here,
-        residual_here,
+        code_parts,
+        pack,
         gain_here,
-        bias_here,
-        places=places,
-        scratch=[pltpu.VMEM((features, code_width), bf16)],
     )
     arrived = exchanged(sent, "tensor")
     codes, grad_code, grad_residual, orders = call(

time: 161 us -> 160 us (level)
  local copies, waits for them, and re-layouts: 7.11 us -> 14 us
  blocking collectives: 65 us -> 59.5 us
    unnamed x39 -> x49, local copies, waits for them, and re-layouts: 6.06 us -> 12.9 us
    all_to_all x5 -> x4, blocking collectives: 65 us -> 59.5 us  [exchanged(): return lax.all_to_all(value, axis, 0, 0, axis_index_groups=groups)]
    ppermute x2, starting transfers between devices: 10.4 us -> 8.41 us  [swapped_2(): lax.ppermute(value, axis, [(i, i ^ 1 << distance) for i in range(lax.axis...]
  transfers between devices with their start and end apart: 13 -> 13, of which waited for: 9 -> 10; matrix products, arithmetic and copies ran while one was open for 1% -> 1% of each run, Pallas kernels for 4% -> 4%
where the time goes in v5:
time: 160 us; the launch traced here: 159 us
  blocking collectives  59.5 us (37%)
  starting transfers between devices  40.3 us (25%)
  waiting for transfers between devices  27.4 us (17%)
  local copies, waits for them, and re-layouts  14 us (9%)
  Pallas kernels  13.4 us (8%)
  matrix products  2.86 us (2%)
    all_to_all x4, blocking collectives, exchanged(): return lax.all_to_all(value, axis, 0, 0, axis_index_groups=groups)  59.5 us
    all_to_all x4, starting transfers between devices, exchanged(): return lax.all_to_all(value, axis, 0, 0, axis_index_groups=groups)  24.6 us
    ppermute x6, waiting for transfers between devices, turned(): return lax.ppermute(value, 'dp', pairs)  15.9 us
    pallas_call x13, Pallas kernels, call(): pl.pallas_call(body, out_shape=[jax.ShapeDtypeStruct(shape, dtype) for sh...  13.4 us
    unnamed x49, local copies, waits for them, and re-layouts  12.9 us
    all_to_all x4, waiting for transfers between devices, exchanged(): return lax.all_to_all(value, axis, 0, 0, axis_index_groups=groups)  11.6 us
    ppermute x2, starting transfers between devices, swapped_2(): lax.ppermute(value, axis, [(i, i ^ 1 << distance) for i in range(lax.axis...  8.41 us
    ppermute x6, starting transfers between devices, turned(): return lax.ppermute(value, 'dp', pairs)  5.15 us
  transfers between devices with their start and end apart: 13, of which 10 were waited for; matrix products, arithmetic and copies ran while one was open for 1% of the time, Pallas kernels for 4%

profile of v5, /device:TPU:1, one launch (start us, length us, event | category | flops | bytes accessed | tf_op | source)
XLA Modules:
  0.0 159.0 jit_solution(10925714219695711214)
XLA Ops:
  0.6 0.0 copy-start
  0.6 1.1 copy-done
  1.7 2.9 %convolution_convert_fusion.refs_0_ = bf16[768,768]{1,0:T(8,128)(2,1)} fusion(bf16[1,384,768]{2,1,0:T(8,128)(2,1)S(1)} %copy-done, bf16[1,768,384]{2,1,0:T(8,128)(2,1)} %param.16), kind=kOutput, calls=%fused_computation | convolution fusion | flops 453574656 | bytes 2359296 | tf_op jit(solution)/shard_map/dot_general | solution.py:67
  4.6 5.1 %all-to-all-start = ((bf16[4,192,768]{2,1,0:T(8,128)(2,1)}), bf16[4,192,768]{2,1,0:T(8,128)(2,1)S(1)}, u32[]{:S(2)}, u32[]{:S(2)}) async-start(bf16[4,192,768]{2,1,0:T(8,128)(2,1)} %bitcast.9), calls=%async_computation | async-start | bytes 2359296 | tf_op jit(solution)/shard_map/all_to_all | solution.py:29
  9.7 1.9 %collective-permute-start = (s32[1]{0:T(128)}, s32[1]{0:T(128)}, u32[]{:S(2)}, u32[]{:S(2)}) collective-permute-start(s32[1]{0:T(128)} %bitcast), channel_id=1, source_target_pairs={{0,8},{8,0},{1,9},{9,1},{2,10},{10,2},{3,11},{11,3},{4,12},{12,4},... | collective-permute-start | bytes 20 | tf_op jit(solution)/shard_map/ppermute | solution.py:25
  11.6 0.6 dynamic-slice_bitcast_fusion
  12.2 2.1 %collective-permute-start.1 = (bf16[48,768]{1,0:T(8,128)(2,1)}, bf16[48,768]{1,0:T(8,128)(2,1)}, u32[]{:S(2)}, u32[]{:S(2)}) collective-permute-start(bf16[48,768]{1,0:T(8,128)(2,1)} %dynamic-slice_bitcast_fusion), channel_id=1, source_target_pairs={{0,0},{1,16},{2,32},{3,48},{4,64},{5,80},{6,96},{7,112},{16,1},{17... | collective-permute-start | bytes 221192 | tf_op jit(solution)/shard_map/ppermute | solution.py:48
  14.3 0.0 collective-permute-done.refs_0_
  14.3 0.8 pad_add_fusion.refs_1_.refs_0_
  15.1 0.0 copy-start.4
  15.1 1.4 copy-done.4
  16.5 1.3 shard_map.146
  17.9 0.8 copy-done.13
  18.7 0.8 copy-done.15
  19.4 0.8 copy-done.17
  20.2 0.0 collective-permute-done.1.refs_0_.refs_1_
  20.2 4.3 %all-to-all-done.refs_2_ = bf16[4,192,768]{2,1,0:T(8,128)(2,1)S(1)} async-done(((bf16[4,192,768]{2,1,0:T(8,128)(2,1)}), bf16[4,192,768]{2,1,0:T(8,128)(2,1)S(1)}, u32[]{:S(2)}, u32[]{:S(2)}) %all-to-all-start) | async-done | bytes 1179680 | tf_op jit(solution)/shard_map/all_to_all | solution.py:29
  24.5 0.9 shard_map.147.refs_0_
  25.4 9.0 %all-to-all-start.1 = ((bf16[4,48,768]{2,1,0:T(8,128)(2,1)}), bf16[4,48,768]{2,1,0:T(8,128)(2,1)S(1)}, u32[]{:S(2)}, u32[]{:S(2)}) async-start(bf16[4,48,768]{2,1,0:T(8,128)(2,1)} %bitcast.15), calls=%async_computation.1 | async-start | bytes 589824 | tf_op jit(solution)/shard_map/all_to_all | solution.py:29
  34.4 0.1 copy.16
  34.5 0.1 broadcast_in_dim.21
  34.5 0.1 eq.22
  34.6 0.1 copy.17
  34.8 2.1 %shard_map.148 = (bf16[128,768]{1,0:T(8,128)(2,1)S(1)}, f32[12,128,128]{2,1,0:T(8,128)S(1)}) custom-call(bf16[192,768]{1,0:T(8,128)(2,1)} %shard_map.147.refs_0_, bf16[128,768]{1,0:T(8,128)(2,1)S(1)} %bitcast.36, bf16[128,768]{1,0:T(8,128)(2,1)S(1)} %bitcast.38, bf16[128,768]{1,0:T(8,128)(2,1)S(1)} %bitcast.40, f32[128,128]{1,0:T(8,128)S(1)} %fusion.3.refs_4_), custom_call_target="tpu_custom_call" | custom-call | flops 1 | bytes 4000000 | tf_op jit(solution)/shard_map/pallas_call | solution.py:89
  36.9 0.9 copy-done.6
  37.8 4.9 %all-to-all-done.1.refs_1_ = bf16[4,48,768]{2,1,0:T(8,128)(2,1)S(1)} async-done(((bf16[4,48,768]{2,1,0:T(8,128)(2,1)}), bf16[4,48,768]{2,1,0:T(8,128)(2,1)S(1)}, u32[]{:S(2)}, u32[]{:S(2)}) %all-to-all-start.1) | async-done | bytes 294944 | tf_op jit(solution)/shard_map/all_to_all | solution.py:29
  42.7 12.9 %all_to_all.40 = bf16[4,48,768]{2,1,0:T(8,128)(2,1)S(1)} all-to-all(bf16[4,48,768]{2,1,0:T(8,128)(2,1)S(1)} %shard_map.149), channel_id=1, replica_groups={{0,64,128,192},{16,80,144,208},{32,96,160,224},{48,112,176,240},{1,65,1..., dimensions={0} | all-to-all | bytes 589824 | tf_op jit(solution)/shard_map/all_to_all | solution.py:29
  55.6 2.0 %shard_map.150 = (bf16[4,192,768]{2,1,0:T(8,128)(2,1)}, bf16[48,768]{1,0:T(8,128)(2,1)S(1)}) custom-call(bf16[192,768]{1,0:T(8,128)(2,1)S(1)} %bitcast.35, bf16[48,768]{1,0:T(8,128)(2,1)} %collective-permute-done.1.refs_0_.refs_1_), custom_call_target="tpu_custom_call" | custom-call | flops 1 | bytes 4000000 | tf_op jit(solution)/shard_map/pallas_call | solution.py:89
  57.6 5.1 %all-to-all-start.3 = ((bf16[4,192,768]{2,1,0:T(8,128)(2,1)}), bf16[4,192,768]{2,1,0:T(8,128)(2,1)S(1)}, u32[]{:S(2)}, u32[]{:S(2)}) async-start(bf16[4,192,768]{2,1,0:T(8,128)(2,1)} %get-tuple-element.25), calls=%async_computation.3 | async-start | bytes 2359296 | tf_op jit(solution)/shard_map/all_to_all | solution.py:29
  62.7 0.9 collective-permute-start.4
  63.6 1.9 %collective-permute-start.3 = (bf16[48,768]{1,0:T(8,128)(2,1)S(1)}, bf16[48,768]{1,0:T(8,128)(2,1)S(1)}, u32[]{:S(2)}, u32[]{:S(2)}) collective-permute-start(bf16[48,768]{1,0:T(8,128)(2,1)S(1)} %get-tuple-element.26.refs_1_), channel_id=1, source_target_pairs={{0,128},{16,144},{32,160},{48,176},{64,192},{80,208},{96,224},{112... | collective-permute-start | bytes 221192 | tf_op jit(solution)/shard_map/ppermute | solution.py:38
  65.5 0.6 collective-permute-start.2
  66.0 1.4 collective-permute-done.4.refs_4_
  67.5 4.7 %collective-permute-done.3.refs_3_ = bf16[48,768]{1,0:T(8,128)(2,1)S(1)} collective-permute-done((bf16[48,768]{1,0:T(8,128)(2,1)S(1)}, bf16[48,768]{1,0:T(8,128)(2,1)S(1)}, u32[]{:S(2)}, u32[]{:S(2)}) %collective-permute-start.3) | collective-permute-done | bytes 73760 | tf_op jit(solution)/shard_map/ppermute | solution.py:38
  72.2 0.1 collective-permute-done.2.refs_2_
  72.3 0.6 shard_map.151.refs_2_
  72.8 2.2 %all-to-all-done.3 = bf16[4,192,768]{2,1,0:T(8,128)(2,1)S(1)} async-done(((bf16[4,192,768]{2,1,0:T(8,128)(2,1)}), bf16[4,192,768]{2,1,0:T(8,128)(2,1)S(1)}, u32[]{:S(2)}, u32[]{:S(2)}) %all-to-all-start.3) | async-done | bytes 1179680 | tf_op jit(solution)/shard_map/all_to_all | solution.py:29
  75.1 0.4 shard_map.152
  75.5 1.1 copy-done.5
  76.6 0.7 copy-done.19
  77.3 5.4 %all-to-all-start.4 = ((bf16[8,128,768]{2,1,0:T(8,128)(2,1)}), bf16[8,128,768]{2,1,0:T(8,128)(2,1)S(1)}, u32[]{:S(2)}, u32[]{:S(2)}) async-start(bf16[8,128,768]{2,1,0:T(8,128)(2,1)} %copy-done.5), calls=%async_computation.4 | async-start | bytes 3145728 | tf_op jit(solution)/shard_map/all_to_all | solution.py:29
  82.8 0.7 collective-permute-start.7
  83.4 1.1 collective-permute-start.6
  84.5 0.0 collective-permute-start.5
  84.5 4.0 %collective-permute-done.7.refs_4_ = bf16[4,48,768]{2,1,0:T(8,128)(2,1)S(1)} collective-permute-done((bf16[4,48,768]{2,1,0:T(8,128)(2,1)}, bf16[4,48,768]{2,1,0:T(8,128)(2,1)S(1)}, u32[]{:S(2)}, u32[]{:S(2)}) %collective-permute-start.7) | collective-permute-done | bytes 294944 | tf_op jit(solution)/shard_map/ppermute | solution.py:38
  88.5 2.3 %collective-permute-done.6.refs_3_ = bf16[4,48,768]{2,1,0:T(8,128)(2,1)S(1)} collective-permute-done((bf16[4,48,768]{2,1,0:T(8,128)(2,1)}, bf16[4,48,768]{2,1,0:T(8,128)(2,1)S(1)}, u32[]{:S(2)}, u32[]{:S(2)}) %collective-permute-start.6) | collective-permute-done | bytes 294944 | tf_op jit(solution)/shard_map/ppermute | solution.py:38
  90.8 3.4 %collective-permute-done.5.refs_2_ = bf16[4,48,768]{2,1,0:T(8,128)(2,1)S(1)} collective-permute-done((bf16[4,48,768]{2,1,0:T(8,128)(2,1)}, bf16[4,48,768]{2,1,0:T(8,128)(2,1)S(1)}, u32[]{:S(2)}, u32[]{:S(2)}) %collective-permute-start.5) | collective-permute-done | bytes 294944 | tf_op jit(solution)/shard_map/ppermute | solution.py:38
  94.2 1.1 copy-done.14
  95.2 1.0 copy-done.20
  96.2 1.4 shard_map.153.refs_1_
  97.6 1.2 copy-done.1
  98.8 0.1 all-to-all-done.4.refs_0_
  99.0 1.5 copy-done.2
  100.5 1.1 shard_map.154
  101.5 14.4 %all_to_all.41.refs_0_ = bf16[8,16,3456]{2,1,0:T(8,128)(2,1)S(1)} all-to-all(bf16[8,16,3456]{2,1,0:T(8,128)(2,1)S(1)} %shard_map.154), channel_id=1, replica_groups=mesh['dp'=16,'section'=2,'tensor'=8] {'tensor'}, dimensions={0} | all-to-all | bytes 1769472 | tf_op jit(solution)/shard_map/all_to_all | solution.py:29
  115.9 1.0 shard_map.155
  117.0 22.3 %all_to_all.42.refs_1_ = bf16[16,16,768]{2,1,0:T(8,128)(2,1)S(1)} all-to-all(bf16[16,16,768]{2,1,0:T(8,128)(2,1)S(1)} %get-tuple-element.34), channel_id=1, replica_groups=mesh['dp'=16,'section'=2,'tensor'=8] {'dp'}, dimensions={0} | all-to-all | bytes 786432 | tf_op jit(solution)/shard_map/all_to_all | solution.py:29
  139.2 0.2 shard_map.156
  139.4 10.0 %all_to_all.43.refs_1_ = bf16[8,16,1536]{2,1,0:T(8,128)(2,1)S(1)} all-to-all(bf16[8,16,1536]{2,1,0:T(8,128)(2,1)S(1)} %shard_map.156), channel_id=1, replica_groups=mesh['dp'=16,'section'=2,'tensor'=8] {'tensor'}, dimensions={0} | all-to-all | bytes 786432 | tf_op jit(solution)/shard_map/all_to_all | solution.py:29
  149.4 0.7 shard_map.157.refs_0_
  150.1 6.6 %collective-permute-start.8 = (bf16[16,768]{1,0:T(8,128)(2,1)S(1)}, bf16[16,768]{1,0:T(8,128)(2,1)S(1)}, u32[]{:S(2)}, u32[]{:S(2)}) collective-permute-start(bf16[16,768]{1,0:T(8,128)(2,1)S(1)} %shard_map.157.refs_0_), channel_id=1, source_target_pairs={{0,8},{8,0},{1,9},{9,1},{2,10},{10,2},{3,11},{11,3},{4,12},{12,4},... | collective-permute-start | bytes 73736 | tf_op jit(solution)/shard_map/ppermute | solution.py:25
  156.6 1.8 %shard_map.158 = (bf16[128,768]{1,0:T(8,128)(2,1)}, bf16[128,768]{1,0:T(8,128)(2,1)}, bf16[128,768]{1,0:T(8,128)(2,1)}) custom-call(bf16[16,768]{1,0:T(8,128)(2,1)S(1)} %shard_map.157.refs_0_, bf16[8,16,1536]{2,1,0:T(8,128)(2,1)S(1)} %all_to_all.43.refs_1_, bf16[768,768]{1,0:T(8,128)(2,1)S(1)} %bitcast.32, bf16[128,768]{1,0:T(8,128)(2,1)S(1)} %bitcast.37, ...), custom_call_target="tpu_custom_call" | custom-call | flops 1 | bytes 4000000 | tf_op jit(solution)/shard_map/pallas_call | solution.py:89
  158.4 0.0 collective-permute-done.8
  158.4 0.6 copy.19
  (38 shorter events, 0.1 us)
Async XLA Ops:
  0.6 1.1 copy-start
  4.6 10.5 %copy-start.3 = (bf16[1,1,128,6144]{3,2,1,0:T(8,128)(2,1)S(1)}, bf16[1,1,128,6144]{3,2,1,0:T(8,128)(2,1)}, u32[]{:S(2)}) copy-start(bf16[1,1,128,6144]{3,2,1,0:T(8,128)(2,1)} %param.11) | copy-start | bytes 4718596
  4.6 10.5 %copy-start.21 = (f32[1,6144]{1,0:T(1,128)S(1)}, f32[1,6144]{1,0:T(1,128)}, u32[]{:S(2)}) copy-start(f32[1,6144]{1,0:T(1,128)} %refs_4_.1) | copy-start | bytes 73732
  4.6 10.5 %copy-start.22 = (f32[1,6144]{1,0:T(1,128)S(1)}, f32[1,6144]{1,0:T(1,128)}, u32[]{:S(2)}) copy-start(f32[1,6144]{1,0:T(1,128)} %refs_5_.1) | copy-start | bytes 73732
  4.6 19.9 %all-to-all-start = ((bf16[4,192,768]{2,1,0:T(8,128)(2,1)}), bf16[4,192,768]{2,1,0:T(8,128)(2,1)S(1)}, u32[]{:S(2)}, u32[]{:S(2)}) async-start(bf16[4,192,768]{2,1,0:T(8,128)(2,1)} %bitcast.9), calls=%async_computation | async-start | bytes 2359296 | tf_op jit(solution)/shard_map/all_to_all | solution.py:29
  9.7 4.6 %collective-permute-start = (s32[1]{0:T(128)}, s32[1]{0:T(128)}, u32[]{:S(2)}, u32[]{:S(2)}) collective-permute-start(s32[1]{0:T(128)} %bitcast), channel_id=1, source_target_pairs={{0,8},{8,0},{1,9},{9,1},{2,10},{10,2},{3,11},{11,3},{4,12},{12,4},... | collective-permute-start | bytes 20 | tf_op jit(solution)/shard_map/ppermute | solution.py:25
  12.2 8.0 %collective-permute-start.1 = (bf16[48,768]{1,0:T(8,128)(2,1)}, bf16[48,768]{1,0:T(8,128)(2,1)}, u32[]{:S(2)}, u32[]{:S(2)}) collective-permute-start(bf16[48,768]{1,0:T(8,128)(2,1)} %dynamic-slice_bitcast_fusion), channel_id=1, source_target_pairs={{0,0},{1,16},{2,32},{3,48},{4,64},{5,80},{6,96},{7,112},{16,1},{17... | collective-permute-start | bytes 221192 | tf_op jit(solution)/shard_map/ppermute | solution.py:48
  15.1 1.4 copy-start.4
  17.9 0.8 copy-start.13
  18.7 0.8 copy-start.15
  19.4 0.8 copy-start.17
  20.2 14.2 %copy-start.23 = (s32[1,1,4,4]{3,2,1,0:T(4,128)S(1)}, s32[1,1,4,4]{3,2,1,0:T(4,128)}, u32[]{:S(2)}) copy-start(s32[1,1,4,4]{3,2,1,0:T(4,128)} %param.15) | copy-start | bytes 196
  20.2 14.6 %copy-start.8 = (bf16[1,1,128,768]{3,2,1,0:T(8,128)(2,1)S(1)}, bf16[1,1,128,768]{3,2,1,0:T(8,128)(2,1)}, u32[]{:S(2)}) copy-start(bf16[1,1,128,768]{3,2,1,0:T(8,128)(2,1)} %param.12) | copy-start | bytes 589828
  20.2 14.6 %copy-start.9 = (bf16[1,1,128,768]{3,2,1,0:T(8,128)(2,1)S(1)}, bf16[1,1,128,768]{3,2,1,0:T(8,128)(2,1)}, u32[]{:S(2)}) copy-start(bf16[1,1,128,768]{3,2,1,0:T(8,128)(2,1)} %param.13) | copy-start | bytes 589828
  20.2 14.6 %copy-start.11 = (bf16[1,1,128,768]{3,2,1,0:T(8,128)(2,1)S(1)}, bf16[1,1,128,768]{3,2,1,0:T(8,128)(2,1)}, u32[]{:S(2)}) copy-start(bf16[1,1,128,768]{3,2,1,0:T(8,128)(2,1)} %param.14) | copy-start | bytes 589828
  25.4 17.3 %all-to-all-start.1 = ((bf16[4,48,768]{2,1,0:T(8,128)(2,1)}), bf16[4,48,768]{2,1,0:T(8,128)(2,1)S(1)}, u32[]{:S(2)}, u32[]{:S(2)}) async-start(bf16[4,48,768]{2,1,0:T(8,128)(2,1)} %bitcast.15), calls=%async_computation.1 | async-start | bytes 589824 | tf_op jit(solution)/shard_map/all_to_all | solution.py:29
  36.9 0.9 copy-start.6
  57.6 17.5 %all-to-all-start.3 = ((bf16[4,192,768]{2,1,0:T(8,128)(2,1)}), bf16[4,192,768]{2,1,0:T(8,128)(2,1)S(1)}, u32[]{:S(2)}, u32[]{:S(2)}) async-start(bf16[4,192,768]{2,1,0:T(8,128)(2,1)} %get-tuple-element.25), calls=%async_computation.3 | async-start | bytes 2359296 | tf_op jit(solution)/shard_map/all_to_all | solution.py:29
  62.7 4.8 %collective-permute-start.4 = (bf16[48,768]{1,0:T(8,128)(2,1)S(1)}, bf16[48,768]{1,0:T(8,128)(2,1)S(1)}, u32[]{:S(2)}, u32[]{:S(2)}) collective-permute-start(bf16[48,768]{1,0:T(8,128)(2,1)S(1)} %get-tuple-element.26.refs_1_), channel_id=1, source_target_pairs={{0,192},{16,208},{32,224},{48,240},{64,0},{80,16},{96,32},{112,48}... | collective-permute-start | bytes 221192 | tf_op jit(solution)/shard_map/ppermute | solution.py:38
  63.6 8.6 %collective-permute-start.3 = (bf16[48,768]{1,0:T(8,128)(2,1)S(1)}, bf16[48,768]{1,0:T(8,128)(2,1)S(1)}, u32[]{:S(2)}, u32[]{:S(2)}) collective-permute-start(bf16[48,768]{1,0:T(8,128)(2,1)S(1)} %get-tuple-element.26.refs_1_), channel_id=1, source_target_pairs={{0,128},{16,144},{32,160},{48,176},{64,192},{80,208},{96,224},{112... | collective-permute-start | bytes 221192 | tf_op jit(solution)/shard_map/ppermute | solution.py:38
  65.5 6.8 %collective-permute-start.2 = (bf16[48,768]{1,0:T(8,128)(2,1)S(1)}, bf16[48,768]{1,0:T(8,128)(2,1)S(1)}, u32[]{:S(2)}, u32[]{:S(2)}) collective-permute-start(bf16[48,768]{1,0:T(8,128)(2,1)S(1)} %get-tuple-element.26.refs_1_), channel_id=1, source_target_pairs={{0,64},{16,80},{32,96},{48,112},{64,128},{80,144},{96,160},{112,17... | collective-permute-start | bytes 221192 | tf_op jit(solution)/shard_map/ppermute | solution.py:38
  75.5 1.1 copy-start.5
  76.6 0.7 copy-start.19
  77.3 21.7 %all-to-all-start.4 = ((bf16[8,128,768]{2,1,0:T(8,128)(2,1)}), bf16[8,128,768]{2,1,0:T(8,128)(2,1)S(1)}, u32[]{:S(2)}, u32[]{:S(2)}) async-start(bf16[8,128,768]{2,1,0:T(8,128)(2,1)} %copy-done.5), calls=%async_computation.4 | async-start | bytes 3145728 | tf_op jit(solution)/shard_map/all_to_all | solution.py:29
  82.8 5.8 %collective-permute-start.7 = (bf16[4,48,768]{2,1,0:T(8,128)(2,1)}, bf16[4,48,768]{2,1,0:T(8,128)(2,1)S(1)}, u32[]{:S(2)}, u32[]{:S(2)}) collective-permute-start(bf16[4,48,768]{2,1,0:T(8,128)(2,1)} %copy-done.19), channel_id=1, source_target_pairs={{0,48},{16,0},{32,16},{48,32},{64,112},{80,64},{96,80},{112,96},{1... | collective-permute-start | bytes 884744 | tf_op jit(solution)/shard_map/ppermute | solution.py:38
  83.4 7.4 %collective-permute-start.6 = (bf16[4,48,768]{2,1,0:T(8,128)(2,1)}, bf16[4,48,768]{2,1,0:T(8,128)(2,1)S(1)}, u32[]{:S(2)}, u32[]{:S(2)}) collective-permute-start(bf16[4,48,768]{2,1,0:T(8,128)(2,1)} %copy-done.19), channel_id=1, source_target_pairs={{0,32},{16,48},{32,0},{48,16},{64,96},{80,112},{96,64},{112,80},{1... | collective-permute-start | bytes 884744 | tf_op jit(solution)/shard_map/ppermute | solution.py:38
  84.5 9.6 %collective-permute-start.5 = (bf16[4,48,768]{2,1,0:T(8,128)(2,1)}, bf16[4,48,768]{2,1,0:T(8,128)(2,1)S(1)}, u32[]{:S(2)}, u32[]{:S(2)}) collective-permute-start(bf16[4,48,768]{2,1,0:T(8,128)(2,1)} %copy-done.19), channel_id=1, source_target_pairs={{0,16},{16,32},{32,48},{48,0},{64,80},{80,96},{96,112},{112,64},{1... | collective-permute-start | bytes 884744 | tf_op jit(solution)/shard_map/ppermute | solution.py:38
  94.2 1.1 copy-start.14
  95.2 1.0 copy-start.20
  97.6 1.2 copy-start.1
  99.0 1.5 copy-start.2
  101.5 14.4 %copy-start.16 = (f32[16,6144]{1,0:T(8,128)S(1)}, f32[16,6144]{1,0:T(8,128)}, u32[]{:S(2)}) copy-start(f32[16,6144]{1,0:T(8,128)} %copy-done.15) | copy-start | bytes 1179652
  101.5 14.4 %copy-start.18 = (f32[16,6144]{1,0:T(8,128)S(1)}, f32[16,6144]{1,0:T(8,128)}, u32[]{:S(2)}) copy-start(f32[16,6144]{1,0:T(8,128)} %copy-done.17) | copy-start | bytes 1179652
  117.0 39.7 %copy-start.7 = (f32[12,128,128]{2,1,0:T(8,128)S(1)}, f32[12,128,128]{2,1,0:T(8,128)}, u32[]{:S(2)}) copy-start(f32[12,128,128]{2,1,0:T(8,128)} %copy-done.6) | copy-start | bytes 2359300
  117.0 39.7 %copy-start.10 = (bf16[1,1,128,768]{3,2,1,0:T(8,128)(2,1)S(1)}, bf16[1,1,128,768]{3,2,1,0:T(8,128)(2,1)}, u32[]{:S(2)}) copy-start(bf16[1,1,128,768]{3,2,1,0:T(8,128)(2,1)} %param.13) | copy-start | bytes 589828
  117.0 39.7 %copy-start.12 = (bf16[1,1,128,768]{3,2,1,0:T(8,128)(2,1)S(1)}, bf16[1,1,128,768]{3,2,1,0:T(8,128)(2,1)}, u32[]{:S(2)}) copy-start(bf16[1,1,128,768]{3,2,1,0:T(8,128)(2,1)} %param.14) | copy-start | bytes 589828
  150.1 8.4 %collective-permute-start.8 = (bf16[16,768]{1,0:T(8,128)(2,1)S(1)}, bf16[16,768]{1,0:T(8,128)(2,1)S(1)}, u32[]{:S(2)}, u32[]{:S(2)}) collective-permute-start(bf16[16,768]{1,0:T(8,128)(2,1)S(1)} %shard_map.157.refs_0_), channel_id=1, source_target_pairs={{0,8},{8,0},{1,9},{9,1},{2,10},{10,2},{3,11},{11,3},{4,12},{12,4},... | collective-permute-start | bytes 73736 | tf_op jit(solution)/shard_map/ppermute | solution.py:25

commit v6 on v5

--- a/solution.py
+++ b/solution.py
@@ -79,20 +79,27 @@
     )
 
 
-def call(kernel, shapes, *inputs, places=None, after=(), scratch=()):
+def call(kernel, shapes, *inputs, places=None, after=(), far=(), far_out=()):
     skipped = len(after)
 
     def body(*refs):
         kernel(*refs[skipped:])
 
     scalars = [] if places is None else [places]
+    inputs = [
+        pltpu.with_memory_space_constraint(array, pltpu.HBM) if place in far else array
+        for place, array in enumerate(inputs)
+    ]
     return pl.pallas_call(
         body,
-        out_shape=[jax.ShapeDtypeStruct(shape, dtype) for shape, dtype in shapes],
+        out_shape=[
+            pltpu.HBM(shape, dtype) if place in far_out else jax.ShapeDtypeStruct(shape, dtype)
+            for place, (shape, dtype) in enumerate(shapes)
+        ],
         in_specs=[pl.BlockSpec(memory_space=pl.ANY)] * skipped
         + [pl.BlockSpec(memory_space=pltpu.SMEM)] * len(scalars)
         + [pl.BlockSpec(memory_space=pltpu.VMEM)] * len(inputs),
-        scratch_shapes=list(scratch),
+        out_specs=[pl.BlockSpec(memory_space=pltpu.VMEM)] * len(shapes),
         cost_estimate=pl.CostEstimate(flops=1, bytes_accessed=4_000_000, transcendentals=0),
         compiler_params=pltpu.CompilerParams(vmem_limit_bytes=VMEM_BYTES),
     )(*after, *scalars, *inputs)
@@ -411,6 +418,7 @@
         norm_bias,
         places=places,
         after=(joined_part,),
+        far_out=(0, 3, 4),
     )
     (joined_rows,) = call(
         first_kernel, [((N_HIGH * share, code_width), bf16)], joined_parts, after=(own_slice, gain_here)
@@ -450,6 +458,7 @@
         context,
         joined,
         column,
+        far_out=(0, 1),
     )
     columns = [column] + [turned(column, 0, step) for step in range(1, N_LOW)]
     code_parts = exchanged(sent, "tensor")
@@ -461,6 +470,8 @@
         gain_here,
         bias_here,
         places=places,
+        far=(0, N_LOW),
+        far_out=(0,),
     )
     (sent,) = call(
         feature_kernel,
@@ -468,6 +479,7 @@
         code_parts,
         pack,
         gain_here,
+        far=(1,),
     )
     arrived = exchanged(sent, "tensor")
     codes, grad_code, grad_residual, orders = call(

time: 160 us -> 158 us (0.988)
  local copies, waits for them, and re-layouts: 14 us -> 4.17 us
  Pallas kernels: 13.4 us -> 18.9 us
  waiting for transfers between devices: 27.4 us -> 31.1 us
    unnamed x49 -> x31, local copies, waits for them, and re-layouts: 12.9 us -> 3.12 us
    pallas_call x13, Pallas kernels: 13.4 us -> 18.9 us  [call(): pl.pallas_call(body, out_shape=[pltpu.HBM(shape, dtype) if place in far_o...]
    all_to_all x4, waiting for transfers between devices: 11.6 us -> 15.2 us  [exchanged(): return lax.all_to_all(value, axis, 0, 0, axis_index_groups=groups)]
  transfers between devices with their start and end apart: 13 -> 13, of which waited for: 10 -> 10; matrix products, arithmetic and copies ran while one was open for 1% -> 1% of each run, Pallas kernels for 4% -> 6%
where the time goes in v6:
time: 158 us; the launch traced here: 157 us
  blocking collectives  58.2 us (37%)
  starting transfers between devices  40.2 us (25%)
  waiting for transfers between devices  31.1 us (20%)
  Pallas kernels  18.9 us (12%)
  local copies, waits for them, and re-layouts  4.17 us (3%)
  matrix products  2.87 us (2%)
    all_to_all x4, blocking collectives, exchanged(): return lax.all_to_all(value, axis, 0, 0, axis_index_groups=groups)  58.2 us
    all_to_all x4, starting transfers between devices, exchanged(): return lax.all_to_all(value, axis, 0, 0, axis_index_groups=groups)  24.6 us
    pallas_call x13, Pallas kernels, call(): pl.pallas_call(body, out_shape=[pltpu.HBM(shape, dtype) if place in far_o...  18.9 us
    ppermute x6, waiting for transfers between devices, turned(): return lax.ppermute(value, 'dp', pairs)  15.9 us
    all_to_all x4, waiting for transfers between devices, exchanged(): return lax.all_to_all(value, axis, 0, 0, axis_index_groups=groups)  15.2 us
    ppermute x2, starting transfers between devices, swapped_2(): lax.ppermute(value, axis, [(i, i ^ 1 << distance) for i in range(lax.axis...  8.32 us
    ppermute x6, starting transfers between devices, turned(): return lax.ppermute(value, 'dp', pairs)  5.15 us
  transfers between devices with their start and end apart: 13, of which 10 were waited for; matrix products, arithmetic and copies ran while one was open for 1% of the time, Pallas kernels for 6%

profile of v6, /device:TPU:1, one launch (start us, length us, event | category | flops | bytes accessed | tf_op | source)
XLA Modules:
  0.0 157.0 jit_solution(8822785779471712302)
XLA Ops:
  0.6 0.0 copy-start
  0.6 1.1 copy-done
  1.7 2.9 %convolution_convert_fusion.refs_0_ = bf16[768,768]{1,0:T(8,128)(2,1)} fusion(bf16[1,384,768]{2,1,0:T(8,128)(2,1)S(1)} %copy-done, bf16[1,768,384]{2,1,0:T(8,128)(2,1)} %param.16), kind=kOutput, calls=%fused_computation | convolution fusion | flops 453574656 | bytes 2359296 | tf_op jit(solution)/shard_map/dot_general | solution.py:67
  4.6 5.1 %all-to-all-start = ((bf16[4,192,768]{2,1,0:T(8,128)(2,1)}), bf16[4,192,768]{2,1,0:T(8,128)(2,1)S(1)}, u32[]{:S(2)}, u32[]{:S(2)}) async-start(bf16[4,192,768]{2,1,0:T(8,128)(2,1)} %bitcast.9), calls=%async_computation | async-start | bytes 2359296 | tf_op jit(solution)/shard_map/all_to_all | solution.py:29
  9.7 1.9 %collective-permute-start = (s32[1]{0:T(128)}, s32[1]{0:T(128)}, u32[]{:S(2)}, u32[]{:S(2)}) collective-permute-start(s32[1]{0:T(128)} %bitcast), channel_id=1, source_target_pairs={{0,8},{8,0},{1,9},{9,1},{2,10},{10,2},{3,11},{11,3},{4,12},{12,4},... | collective-permute-start | bytes 20 | tf_op jit(solution)/shard_map/ppermute | solution.py:25
  11.6 0.6 dynamic-slice_bitcast_fusion
  12.2 2.1 %collective-permute-start.1 = (bf16[48,768]{1,0:T(8,128)(2,1)}, bf16[48,768]{1,0:T(8,128)(2,1)}, u32[]{:S(2)}, u32[]{:S(2)}) collective-permute-start(bf16[48,768]{1,0:T(8,128)(2,1)} %dynamic-slice_bitcast_fusion), channel_id=1, source_target_pairs={{0,0},{1,16},{2,32},{3,48},{4,64},{5,80},{6,96},{7,112},{16,1},{17... | collective-permute-start | bytes 221192 | tf_op jit(solution)/shard_map/ppermute | solution.py:48
  14.3 0.0 collective-permute-done.refs_0_
  14.3 0.7 pad_add_fusion.refs_1_.refs_0_
  15.1 0.0 copy-done.1
  15.1 0.0 copy-done.12
  15.1 0.0 copy-done.13
  15.1 0.0 copy-start.2
  15.1 1.4 copy-done.2
  16.5 2.4 %shard_map.146 = (bf16[3,128,768]{2,1,0:T(8,128)(2,1)}, f32[1,768]{1,0:T(1,128)S(1)}, f32[1,768]{1,0:T(1,128)S(1)}, f32[16,6144]{1,0:T(8,128)}, f32[16,6144]{1,0:T(8,128)}) custom-call(bf16[768,768]{1,0:T(8,128)(2,1)} %convolution_convert_fusion.refs_0_, s32[4]{0:T(128)S(1)} %pad_add_fusion.refs_1_.refs_0_, bf16[128,6144]{1,0:T(8,128)(2,1)S(1)} %bitcast.33, ...), custom_call_target="tpu_custom_call" | custom-call | flops 1 | bytes 4000000 | tf_op jit(solution)/shard_map/pallas_call | solution.py:93
  18.9 0.0 collective-permute-done.1.refs_0_.refs_1_
  18.9 5.7 %all-to-all-done.refs_2_ = bf16[4,192,768]{2,1,0:T(8,128)(2,1)S(1)} async-done(((bf16[4,192,768]{2,1,0:T(8,128)(2,1)}), bf16[4,192,768]{2,1,0:T(8,128)(2,1)S(1)}, u32[]{:S(2)}, u32[]{:S(2)}) %all-to-all-start) | async-done | bytes 1179680 | tf_op jit(solution)/shard_map/all_to_all | solution.py:29
  24.5 0.9 shard_map.147.refs_0_
  25.4 9.0 %all-to-all-start.1 = ((bf16[4,48,768]{2,1,0:T(8,128)(2,1)}), bf16[4,48,768]{2,1,0:T(8,128)(2,1)S(1)}, u32[]{:S(2)}, u32[]{:S(2)}) async-start(bf16[4,48,768]{2,1,0:T(8,128)(2,1)} %bitcast.15), calls=%async_computation.1 | async-start | bytes 589824 | tf_op jit(solution)/shard_map/all_to_all | solution.py:29
  34.3 0.0 copy-done.14
  34.4 0.1 copy.16
  34.5 0.1 broadcast_in_dim.21
  34.5 0.1 eq.22
  34.6 0.1 copy.17
  34.8 0.0 copy-done.5
  34.8 0.0 copy-done.6
  34.8 2.1 %shard_map.148 = (bf16[128,768]{1,0:T(8,128)(2,1)S(1)}, f32[12,128,128]{2,1,0:T(8,128)S(1)}) custom-call(bf16[192,768]{1,0:T(8,128)(2,1)} %shard_map.147.refs_0_, bf16[128,768]{1,0:T(8,128)(2,1)S(1)} %bitcast.36, bf16[128,768]{1,0:T(8,128)(2,1)S(1)} %bitcast.38, bf16[128,768]{1,0:T(8,128)(2,1)S(1)} %bitcast.40, f32[128,128]{1,0:T(8,128)S(1)} %fusion.3.refs_4_), custom_call_target="tpu_custom_call" | custom-call | flops 1 | bytes 4000000 | tf_op jit(solution)/shard_map/pallas_call | solution.py:93
  36.9 5.8 %all-to-all-done.1.refs_1_ = bf16[4,48,768]{2,1,0:T(8,128)(2,1)S(1)} async-done(((bf16[4,48,768]{2,1,0:T(8,128)(2,1)}), bf16[4,48,768]{2,1,0:T(8,128)(2,1)S(1)}, u32[]{:S(2)}, u32[]{:S(2)}) %all-to-all-start.1) | async-done | bytes 294944 | tf_op jit(solution)/shard_map/all_to_all | solution.py:29
  42.7 12.9 %all_to_all.40 = bf16[4,48,768]{2,1,0:T(8,128)(2,1)S(1)} all-to-all(bf16[4,48,768]{2,1,0:T(8,128)(2,1)S(1)} %shard_map.149), channel_id=1, replica_groups={{0,64,128,192},{16,80,144,208},{32,96,160,224},{48,112,176,240},{1,65,1..., dimensions={0} | all-to-all | bytes 589824 | tf_op jit(solution)/shard_map/all_to_all | solution.py:29
  55.6 2.0 %shard_map.150 = (bf16[4,192,768]{2,1,0:T(8,128)(2,1)}, bf16[48,768]{1,0:T(8,128)(2,1)S(1)}) custom-call(bf16[192,768]{1,0:T(8,128)(2,1)S(1)} %bitcast.35, bf16[48,768]{1,0:T(8,128)(2,1)} %collective-permute-done.1.refs_0_.refs_1_), custom_call_target="tpu_custom_call" | custom-call | flops 1 | bytes 4000000 | tf_op jit(solution)/shard_map/pallas_call | solution.py:93
  57.6 5.1 %all-to-all-start.3 = ((bf16[4,192,768]{2,1,0:T(8,128)(2,1)}), bf16[4,192,768]{2,1,0:T(8,128)(2,1)S(1)}, u32[]{:S(2)}, u32[]{:S(2)}) async-start(bf16[4,192,768]{2,1,0:T(8,128)(2,1)} %get-tuple-element.25), calls=%async_computation.3 | async-start | bytes 2359296 | tf_op jit(solution)/shard_map/all_to_all | solution.py:29
  62.7 0.9 collective-permute-start.4
  63.6 1.9 %collective-permute-start.3 = (bf16[48,768]{1,0:T(8,128)(2,1)S(1)}, bf16[48,768]{1,0:T(8,128)(2,1)S(1)}, u32[]{:S(2)}, u32[]{:S(2)}) collective-permute-start(bf16[48,768]{1,0:T(8,128)(2,1)S(1)} %get-tuple-element.26.refs_1_), channel_id=1, source_target_pairs={{0,128},{16,144},{32,160},{48,176},{64,192},{80,208},{96,224},{112... | collective-permute-start | bytes 221192 | tf_op jit(solution)/shard_map/ppermute | solution.py:38
  65.5 0.6 collective-permute-start.2
  66.1 1.4 collective-permute-done.4.refs_4_
  67.5 4.7 %collective-permute-done.3.refs_3_ = bf16[48,768]{1,0:T(8,128)(2,1)S(1)} collective-permute-done((bf16[48,768]{1,0:T(8,128)(2,1)S(1)}, bf16[48,768]{1,0:T(8,128)(2,1)S(1)}, u32[]{:S(2)}, u32[]{:S(2)}) %collective-permute-start.3) | collective-permute-done | bytes 73760 | tf_op jit(solution)/shard_map/ppermute | solution.py:38
  72.2 0.1 collective-permute-done.2.refs_2_
  72.3 0.6 shard_map.151.refs_2_
  72.9 2.2 %all-to-all-done.3 = bf16[4,192,768]{2,1,0:T(8,128)(2,1)S(1)} async-done(((bf16[4,192,768]{2,1,0:T(8,128)(2,1)}), bf16[4,192,768]{2,1,0:T(8,128)(2,1)S(1)}, u32[]{:S(2)}, u32[]{:S(2)}) %all-to-all-start.3) | async-done | bytes 1179680 | tf_op jit(solution)/shard_map/all_to_all | solution.py:29
  75.1 1.5 shard_map.152
  76.6 5.4 %all-to-all-start.4 = ((bf16[8,128,768]{2,1,0:T(8,128)(2,1)}), bf16[8,128,768]{2,1,0:T(8,128)(2,1)S(1)}, u32[]{:S(2)}, u32[]{:S(2)}) async-start(bf16[8,128,768]{2,1,0:T(8,128)(2,1)} %get-tuple-element.27), calls=%async_computation.4 | async-start | bytes 3145728 | tf_op jit(solution)/shard_map/all_to_all | solution.py:29
  82.0 0.7 collective-permute-start.7
  82.7 1.1 collective-permute-start.6
  83.8 0.0 collective-permute-start.5
  83.8 4.0 %collective-permute-done.7.refs_4_ = bf16[4,48,768]{2,1,0:T(8,128)(2,1)S(1)} collective-permute-done((bf16[4,48,768]{2,1,0:T(8,128)(2,1)}, bf16[4,48,768]{2,1,0:T(8,128)(2,1)S(1)}, u32[]{:S(2)}, u32[]{:S(2)}) %collective-permute-start.7) | collective-permute-done | bytes 294944 | tf_op jit(solution)/shard_map/ppermute | solution.py:38
  87.8 2.3 %collective-permute-done.6.refs_3_ = bf16[4,48,768]{2,1,0:T(8,128)(2,1)S(1)} collective-permute-done((bf16[4,48,768]{2,1,0:T(8,128)(2,1)}, bf16[4,48,768]{2,1,0:T(8,128)(2,1)S(1)}, u32[]{:S(2)}, u32[]{:S(2)}) %collective-permute-start.6) | collective-permute-done | bytes 294944 | tf_op jit(solution)/shard_map/ppermute | solution.py:38
  90.1 3.4 %collective-permute-done.5.refs_2_ = bf16[4,48,768]{2,1,0:T(8,128)(2,1)S(1)} collective-permute-done((bf16[4,48,768]{2,1,0:T(8,128)(2,1)}, bf16[4,48,768]{2,1,0:T(8,128)(2,1)S(1)}, u32[]{:S(2)}, u32[]{:S(2)}) %collective-permute-start.5) | collective-permute-done | bytes 294944 | tf_op jit(solution)/shard_map/ppermute | solution.py:38
  93.5 3.2 %shard_map.153.refs_1_ = bf16[1168,768]{1,0:T(8,128)(2,1)} custom-call(s32[4]{0:T(128)S(1)} %pad_add_fusion.refs_1_.refs_0_, bf16[4,48,768]{2,1,0:T(8,128)(2,1)} %get-tuple-element.28.refs_1_, bf16[4,48,768]{2,1,0:T(8,128)(2,1)S(1)} %collective-permute-done.5.refs_2_, bf16[4,48,768]{2,1,0:T(8,128)(2,1)S(1)} %collective-permute-done.6.refs_3_, ...), custom_call_target="tpu_custom_call" | custom-call | flops 1 | bytes 4000000 | tf_op jit(solution)/shard_map/pallas_call | solution.py:93
  96.7 1.5 all-to-all-done.4.refs_0_
  98.3 2.6 %shard_map.154 = bf16[8,16,3456]{2,1,0:T(8,128)(2,1)S(1)} custom-call(bf16[8,128,768]{2,1,0:T(8,128)(2,1)S(1)} %all-to-all-done.4.refs_0_, bf16[1168,768]{1,0:T(8,128)(2,1)} %shard_map.153.refs_1_, f32[1,768]{1,0:T(1,128)S(1)} %get-tuple-element.23.refs_1_.refs_6_.refs_2_), custom_call_target="tpu_custom_call" | custom-call | flops 1 | bytes 4000000 | tf_op jit(solution)/shard_map/pallas_call | solution.py:93
  100.8 0.0 copy-start.10
  100.9 0.0 copy-start.11
  100.9 13.4 %all_to_all.41.refs_0_ = bf16[8,16,3456]{2,1,0:T(8,128)(2,1)S(1)} all-to-all(bf16[8,16,3456]{2,1,0:T(8,128)(2,1)S(1)} %shard_map.154), channel_id=1, replica_groups=mesh['dp'=16,'section'=2,'tensor'=8] {'tensor'}, dimensions={0} | all-to-all | bytes 1769472 | tf_op jit(solution)/shard_map/all_to_all | solution.py:29
  114.3 0.0 copy-done.10
  114.3 1.1 shard_map.155
  115.4 21.8 %all_to_all.42.refs_1_ = bf16[16,16,768]{2,1,0:T(8,128)(2,1)S(1)} all-to-all(bf16[16,16,768]{2,1,0:T(8,128)(2,1)S(1)} %get-tuple-element.34), channel_id=1, replica_groups=mesh['dp'=16,'section'=2,'tensor'=8] {'dp'}, dimensions={0} | all-to-all | bytes 786432 | tf_op jit(solution)/shard_map/all_to_all | solution.py:29
  137.2 0.2 shard_map.156
  137.4 10.0 %all_to_all.43.refs_1_ = bf16[8,16,1536]{2,1,0:T(8,128)(2,1)S(1)} all-to-all(bf16[8,16,1536]{2,1,0:T(8,128)(2,1)S(1)} %shard_map.156), channel_id=1, replica_groups=mesh['dp'=16,'section'=2,'tensor'=8] {'tensor'}, dimensions={0} | all-to-all | bytes 786432 | tf_op jit(solution)/shard_map/all_to_all | solution.py:29
  147.4 0.6 shard_map.157.refs_0_
  148.1 6.5 %collective-permute-start.8 = (bf16[16,768]{1,0:T(8,128)(2,1)S(1)}, bf16[16,768]{1,0:T(8,128)(2,1)S(1)}, u32[]{:S(2)}, u32[]{:S(2)}) collective-permute-start(bf16[16,768]{1,0:T(8,128)(2,1)S(1)} %shard_map.157.refs_0_), channel_id=1, source_target_pairs={{0,8},{8,0},{1,9},{9,1},{2,10},{10,2},{3,11},{11,3},{4,12},{12,4},... | collective-permute-start | bytes 73736 | tf_op jit(solution)/shard_map/ppermute | solution.py:25
  154.5 0.0 copy-done.9
  154.5 1.8 %shard_map.158 = (bf16[128,768]{1,0:T(8,128)(2,1)}, bf16[128,768]{1,0:T(8,128)(2,1)}, bf16[128,768]{1,0:T(8,128)(2,1)}) custom-call(bf16[16,768]{1,0:T(8,128)(2,1)S(1)} %shard_map.157.refs_0_, bf16[8,16,1536]{2,1,0:T(8,128)(2,1)S(1)} %all_to_all.43.refs_1_, bf16[768,768]{1,0:T(8,128)(2,1)S(1)} %bitcast.32, bf16[128,768]{1,0:T(8,128)(2,1)S(1)} %bitcast.37, ...), custom_call_target="tpu_custom_call" | custom-call | flops 1 | bytes 4000000 | tf_op jit(solution)/shard_map/pallas_call | solution.py:93
  156.3 0.0 collective-permute-done.8
  156.3 0.6 copy.19
  (20 shorter events, 0.1 us)
Async XLA Ops:
  0.6 1.1 copy-start
  4.6 10.5 %copy-start.1 = (bf16[1,1,128,6144]{3,2,1,0:T(8,128)(2,1)S(1)}, bf16[1,1,128,6144]{3,2,1,0:T(8,128)(2,1)}, u32[]{:S(2)}) copy-start(bf16[1,1,128,6144]{3,2,1,0:T(8,128)(2,1)} %param.11) | copy-start | bytes 4718596
  4.6 10.5 %copy-start.12 = (f32[1,6144]{1,0:T(1,128)S(1)}, f32[1,6144]{1,0:T(1,128)}, u32[]{:S(2)}) copy-start(f32[1,6144]{1,0:T(1,128)} %refs_4_.1) | copy-start | bytes 73732
  4.6 10.5 %copy-start.13 = (f32[1,6144]{1,0:T(1,128)S(1)}, f32[1,6144]{1,0:T(1,128)}, u32[]{:S(2)}) copy-start(f32[1,6144]{1,0:T(1,128)} %refs_5_.1) | copy-start | bytes 73732
  4.6 19.9 %all-to-all-start = ((bf16[4,192,768]{2,1,0:T(8,128)(2,1)}), bf16[4,192,768]{2,1,0:T(8,128)(2,1)S(1)}, u32[]{:S(2)}, u32[]{:S(2)}) async-start(bf16[4,192,768]{2,1,0:T(8,128)(2,1)} %bitcast.9), calls=%async_computation | async-start | bytes 2359296 | tf_op jit(solution)/shard_map/all_to_all | solution.py:29
  9.7 4.6 %collective-permute-start = (s32[1]{0:T(128)}, s32[1]{0:T(128)}, u32[]{:S(2)}, u32[]{:S(2)}) collective-permute-start(s32[1]{0:T(128)} %bitcast), channel_id=1, source_target_pairs={{0,8},{8,0},{1,9},{9,1},{2,10},{10,2},{3,11},{11,3},{4,12},{12,4},... | collective-permute-start | bytes 20 | tf_op jit(solution)/shard_map/ppermute | solution.py:25
  12.2 6.7 %collective-permute-start.1 = (bf16[48,768]{1,0:T(8,128)(2,1)}, bf16[48,768]{1,0:T(8,128)(2,1)}, u32[]{:S(2)}, u32[]{:S(2)}) collective-permute-start(bf16[48,768]{1,0:T(8,128)(2,1)} %dynamic-slice_bitcast_fusion), channel_id=1, source_target_pairs={{0,0},{1,16},{2,32},{3,48},{4,64},{5,80},{6,96},{7,112},{16,1},{17... | collective-permute-start | bytes 221192 | tf_op jit(solution)/shard_map/ppermute | solution.py:48
  15.1 1.4 copy-start.2
  18.9 15.5 %copy-start.14 = (s32[1,1,4,4]{3,2,1,0:T(4,128)S(1)}, s32[1,1,4,4]{3,2,1,0:T(4,128)}, u32[]{:S(2)}) copy-start(s32[1,1,4,4]{3,2,1,0:T(4,128)} %param.15) | copy-start | bytes 196
  18.9 16.0 %copy-start.5 = (bf16[1,1,128,768]{3,2,1,0:T(8,128)(2,1)S(1)}, bf16[1,1,128,768]{3,2,1,0:T(8,128)(2,1)}, u32[]{:S(2)}) copy-start(bf16[1,1,128,768]{3,2,1,0:T(8,128)(2,1)} %param.12) | copy-start | bytes 589828
  18.9 16.0 %copy-start.6 = (bf16[1,1,128,768]{3,2,1,0:T(8,128)(2,1)S(1)}, bf16[1,1,128,768]{3,2,1,0:T(8,128)(2,1)}, u32[]{:S(2)}) copy-start(bf16[1,1,128,768]{3,2,1,0:T(8,128)(2,1)} %param.13) | copy-start | bytes 589828
  18.9 16.0 %copy-start.8 = (bf16[1,1,128,768]{3,2,1,0:T(8,128)(2,1)S(1)}, bf16[1,1,128,768]{3,2,1,0:T(8,128)(2,1)}, u32[]{:S(2)}) copy-start(bf16[1,1,128,768]{3,2,1,0:T(8,128)(2,1)} %param.14) | copy-start | bytes 589828
  25.4 17.3 %all-to-all-start.1 = ((bf16[4,48,768]{2,1,0:T(8,128)(2,1)}), bf16[4,48,768]{2,1,0:T(8,128)(2,1)S(1)}, u32[]{:S(2)}, u32[]{:S(2)}) async-start(bf16[4,48,768]{2,1,0:T(8,128)(2,1)} %bitcast.15), calls=%async_computation.1 | async-start | bytes 589824 | tf_op jit(solution)/shard_map/all_to_all | solution.py:29
  36.9 20.7 %copy-start.3 = (f32[12,128,128]{2,1,0:T(8,128)}, f32[12,128,128]{2,1,0:T(8,128)S(1)}, u32[]{:S(2)}) copy-start(f32[12,128,128]{2,1,0:T(8,128)S(1)} %get-tuple-element.37.refs_6_) | copy-start | bytes 2359300
  57.6 17.5 %all-to-all-start.3 = ((bf16[4,192,768]{2,1,0:T(8,128)(2,1)}), bf16[4,192,768]{2,1,0:T(8,128)(2,1)S(1)}, u32[]{:S(2)}, u32[]{:S(2)}) async-start(bf16[4,192,768]{2,1,0:T(8,128)(2,1)} %get-tuple-element.25), calls=%async_computation.3 | async-start | bytes 2359296 | tf_op jit(solution)/shard_map/all_to_all | solution.py:29
  62.7 4.8 %collective-permute-start.4 = (bf16[48,768]{1,0:T(8,128)(2,1)S(1)}, bf16[48,768]{1,0:T(8,128)(2,1)S(1)}, u32[]{:S(2)}, u32[]{:S(2)}) collective-permute-start(bf16[48,768]{1,0:T(8,128)(2,1)S(1)} %get-tuple-element.26.refs_1_), channel_id=1, source_target_pairs={{0,192},{16,208},{32,224},{48,240},{64,0},{80,16},{96,32},{112,48}... | collective-permute-start | bytes 221192 | tf_op jit(solution)/shard_map/ppermute | solution.py:38
  63.6 8.6 %collective-permute-start.3 = (bf16[48,768]{1,0:T(8,128)(2,1)S(1)}, bf16[48,768]{1,0:T(8,128)(2,1)S(1)}, u32[]{:S(2)}, u32[]{:S(2)}) collective-permute-start(bf16[48,768]{1,0:T(8,128)(2,1)S(1)} %get-tuple-element.26.refs_1_), channel_id=1, source_target_pairs={{0,128},{16,144},{32,160},{48,176},{64,192},{80,208},{96,224},{112... | collective-permute-start | bytes 221192 | tf_op jit(solution)/shard_map/ppermute | solution.py:38
  65.5 6.8 %collective-permute-start.2 = (bf16[48,768]{1,0:T(8,128)(2,1)S(1)}, bf16[48,768]{1,0:T(8,128)(2,1)S(1)}, u32[]{:S(2)}, u32[]{:S(2)}) collective-permute-start(bf16[48,768]{1,0:T(8,128)(2,1)S(1)} %get-tuple-element.26.refs_1_), channel_id=1, source_target_pairs={{0,64},{16,80},{32,96},{48,112},{64,128},{80,144},{96,160},{112,17... | collective-permute-start | bytes 221192 | tf_op jit(solution)/shard_map/ppermute | solution.py:38
  76.6 21.6 %all-to-all-start.4 = ((bf16[8,128,768]{2,1,0:T(8,128)(2,1)}), bf16[8,128,768]{2,1,0:T(8,128)(2,1)S(1)}, u32[]{:S(2)}, u32[]{:S(2)}) async-start(bf16[8,128,768]{2,1,0:T(8,128)(2,1)} %get-tuple-element.27), calls=%async_computation.4 | async-start | bytes 3145728 | tf_op jit(solution)/shard_map/all_to_all | solution.py:29
  82.0 5.8 %collective-permute-start.7 = (bf16[4,48,768]{2,1,0:T(8,128)(2,1)}, bf16[4,48,768]{2,1,0:T(8,128)(2,1)S(1)}, u32[]{:S(2)}, u32[]{:S(2)}) collective-permute-start(bf16[4,48,768]{2,1,0:T(8,128)(2,1)} %get-tuple-element.28.refs_1_), channel_id=1, source_target_pairs={{0,48},{16,0},{32,16},{48,32},{64,112},{80,64},{96,80},{112,96},{1... | collective-permute-start | bytes 884744 | tf_op jit(solution)/shard_map/ppermute | solution.py:38
  82.7 7.4 %collective-permute-start.6 = (bf16[4,48,768]{2,1,0:T(8,128)(2,1)}, bf16[4,48,768]{2,1,0:T(8,128)(2,1)S(1)}, u32[]{:S(2)}, u32[]{:S(2)}) collective-permute-start(bf16[4,48,768]{2,1,0:T(8,128)(2,1)} %get-tuple-element.28.refs_1_), channel_id=1, source_target_pairs={{0,32},{16,48},{32,0},{48,16},{64,96},{80,112},{96,64},{112,80},{1... | collective-permute-start | bytes 884744 | tf_op jit(solution)/shard_map/ppermute | solution.py:38
  83.8 9.7 %collective-permute-start.5 = (bf16[4,48,768]{2,1,0:T(8,128)(2,1)}, bf16[4,48,768]{2,1,0:T(8,128)(2,1)S(1)}, u32[]{:S(2)}, u32[]{:S(2)}) collective-permute-start(bf16[4,48,768]{2,1,0:T(8,128)(2,1)} %get-tuple-element.28.refs_1_), channel_id=1, source_target_pairs={{0,16},{16,32},{32,48},{48,0},{64,80},{80,96},{96,112},{112,64},{1... | collective-permute-start | bytes 884744 | tf_op jit(solution)/shard_map/ppermute | solution.py:38
  100.8 13.5 %copy-start.10 = (f32[16,6144]{1,0:T(8,128)S(1)}, f32[16,6144]{1,0:T(8,128)}, u32[]{:S(2)}) copy-start(f32[16,6144]{1,0:T(8,128)} %get-tuple-element.31.refs_1_) | copy-start | bytes 1179652
  100.9 13.5 %copy-start.11 = (f32[16,6144]{1,0:T(8,128)S(1)}, f32[16,6144]{1,0:T(8,128)}, u32[]{:S(2)}) copy-start(f32[16,6144]{1,0:T(8,128)} %get-tuple-element.32.refs_2_) | copy-start | bytes 1179652
  115.4 39.2 %copy-start.4 = (f32[12,128,128]{2,1,0:T(8,128)S(1)}, f32[12,128,128]{2,1,0:T(8,128)}, u32[]{:S(2)}) copy-start(f32[12,128,128]{2,1,0:T(8,128)} %copy-done.3) | copy-start | bytes 2359300
  115.4 39.2 %copy-start.7 = (bf16[1,1,128,768]{3,2,1,0:T(8,128)(2,1)S(1)}, bf16[1,1,128,768]{3,2,1,0:T(8,128)(2,1)}, u32[]{:S(2)}) copy-start(bf16[1,1,128,768]{3,2,1,0:T(8,128)(2,1)} %param.13) | copy-start | bytes 589828
  115.4 39.2 %copy-start.9 = (bf16[1,1,128,768]{3,2,1,0:T(8,128)(2,1)S(1)}, bf16[1,1,128,768]{3,2,1,0:T(8,128)(2,1)}, u32[]{:S(2)}) copy-start(bf16[1,1,128,768]{3,2,1,0:T(8,128)(2,1)} %param.14) | copy-start | bytes 589828
  148.1 8.3 %collective-permute-start.8 = (bf16[16,768]{1,0:T(8,128)(2,1)S(1)}, bf16[16,768]{1,0:T(8,128)(2,1)S(1)}, u32[]{:S(2)}, u32[]{:S(2)}) collective-permute-start(bf16[16,768]{1,0:T(8,128)(2,1)S(1)} %shard_map.157.refs_0_), channel_id=1, source_target_pairs={{0,8},{8,0},{1,9},{9,1},{2,10},{10,2},{3,11},{11,3},{4,12},{12,4},... | collective-permute-start | bytes 73736 | tf_op jit(solution)/shard_map/ppermute | solution.py:25

commit v7 on v6

--- a/solution.py
+++ b/solution.py
@@ -38,13 +38,31 @@
     return lax.ppermute(value, "dp", pairs)
 
 
+def slice_at(place, rank):
+    count = N_TENSOR
+    owner = place // count * count + rank
+    near = [(ring(owner // N_LOW, e // N_LOW) * 2 + ring(owner, e), e) for e in octet_of(place)]
+    far = [(-ring(p // 2, rank // 2) - abs(p % 2 - rank % 2), p) for p in range(count)]
+    pairs = {e: p for (_, e), (_, p) in zip(sorted(near), sorted(far))}
+    return pairs[place]
+
+
+def octet_of(place):
+    start = place // N_TENSOR * N_TENSOR
+    return range(start, start + N_TENSOR)
+
+
+def ring(one, other):
+    away = (one - other) % N_LOW
+    return min(away, N_LOW - away)
+
+
 def transposed_owner(value, count):
-    pairs = [
-        ((half * count + d) * count + t, (half * count + t) * count + d)
-        for half in range(2)
-        for d in range(count)
-        for t in range(count)
-    ]
+    pairs = []
+    for place in range(2 * count):
+        for rank in range(count):
+            owner = place // count * count + rank
+            pairs.append((owner * count + slice_at(place, rank), place * count + rank))
     return lax.ppermute(value, ("dp", "tensor"), pairs)
 
 
@@ -79,7 +97,9 @@
     )
 
 
-def call(kernel, shapes, *inputs, places=None, after=(), far=(), far_out=()):
+def call(
+    kernel, shapes, *inputs, places=None, after=(), far=(), far_out=(), raw=(), scratch=()
+):
     skipped = len(after)
 
     def body(*refs):
@@ -98,8 +118,15 @@
         ],
         in_specs=[pl.BlockSpec(memory_space=pl.ANY)] * skipped
         + [pl.BlockSpec(memory_space=pltpu.SMEM)] * len(scalars)
-        + [pl.BlockSpec(memory_space=pltpu.VMEM)] * len(inputs),
-        out_specs=[pl.BlockSpec(memory_space=pltpu.VMEM)] * len(shapes),
+        + [
+            pl.BlockSpec(memory_space=pl.ANY if place in raw else pltpu.VMEM)
+            for place in range(len(inputs))
+        ],
+        out_specs=[
+            pl.BlockSpec(memory_space=pl.ANY if raw and place in far_out else pltpu.VMEM)
+            for place in range(len(shapes))
+        ],
+        scratch_shapes=list(scratch),
         cost_estimate=pl.CostEstimate(flops=1, bytes_accessed=4_000_000, transcendentals=0),
         compiler_params=pltpu.CompilerParams(vmem_limit_bytes=VMEM_BYTES),
     )(*after, *scalars, *inputs)
@@ -168,7 +195,8 @@
         for step in range(N_LOW):
             piece = refs[step][high]
             place = high * N_LOW + (places_ref[2] + N_LOW - step) % N_LOW
-            start = pl.multiple_of(place * piece.shape[0], EXTRA_ROWS)
+            part = place // N_TENSOR * N_TENSOR + places_ref[4 + place]
+            start = pl.multiple_of(part * piece.shape[0], EXTRA_ROWS)
             pack_ref[pl.ds(start, piece.shape[0])] = piece
     _, length, features = here_ref.shape
     width = pack_ref.shape[1]
@@ -196,16 +224,24 @@
     pack_ref[features + 3 * length :, half:] = extra
 
 
-def feature_kernel(parts_ref, pack_ref, gain_ref, out_ref):
+def feature_kernel(parts_ref, pack_hbm, gain_ref, out_ref, pack_ref, semaphores):
     count, rows, _ = out_ref.shape
     features = gain_ref.shape[1]
     width = pack_ref.shape[1]
     length = count * rows
-    book = pack_ref[:features]
+    rest = pl.ds(features, pack_ref.shape[0] - features)
+    copies = [
+        pltpu.make_async_copy(pack_hbm.at[there], pack_ref.at[there], semaphores.at[place])
+        for place, there in enumerate((pl.ds(0, features), rest))
+    ]
+    for copy in copies:
+        copy.start()
     total = parts_ref[0].astype(jnp.float32)
     for part in range(1, count):
         total += parts_ref[part].astype(jnp.float32)
     code = total.astype(jnp.bfloat16)
+    copies[0].wait()
+    book = pack_ref[:features]
 
     def put(start, value):
         value = value.astype(jnp.bfloat16)
@@ -213,6 +249,7 @@
 
     decoded = times_transposed(code, book)
     put(3 * width, decoded)
+    copies[1].wait()
     upper = pack_ref[features + length : features + 2 * length].astype(jnp.float32)
     lower = pack_ref[features + 2 * length : features + 3 * length].astype(jnp.float32)
     hidden = upper + lower + decoded
@@ -397,6 +434,9 @@
     dp_rank = lax.axis_index("dp")
     wanted = swapped_2(receiver_order[0], "section", 0)
     places = jnp.stack([rank, dp_rank // N_LOW, dp_rank % N_LOW, wanted[0]])
+    slices = [[slice_at(place, t) for place in range(n_dp)] for t in range(n_tensor)]
+    slices = lax.dynamic_index_in_dim(jnp.array(slices, jnp.int32), rank, 0, keepdims=False)
+    places = jnp.concatenate([places, slices])
     allowed = allowed_pairs(block_mask[0, 0]).astype(f32)
 
     joined_part = times(out_weight[0], code_book).astype(bf16)
@@ -480,6 +520,8 @@
         pack,
         gain_here,
         far=(1,),
+        raw=(1,),
+        scratch=[pltpu.VMEM(pack.shape, bf16), pltpu.SemaphoreType.DMA((2,))],
     )
     arrived = exchanged(sent, "tensor")
     codes, grad_code, grad_residual, orders = call(

time: 158 us -> 157 us (level)
  starting transfers between devices: 40.2 us -> 47.8 us
  blocking collectives: 58.2 us -> 52.1 us
  waiting for transfers between devices: 31.1 us -> 28.3 us
    ppermute x2, starting transfers between devices: 8.32 us -> 14.7 us  [swapped_2(): lax.ppermute(value, axis, [(i, i ^ 1 << distance) for i in range(lax.axis...]
    all_to_all x4, blocking collectives: 58.2 us -> 52.1 us  [exchanged(): return lax.all_to_all(value, axis, 0, 0, axis_index_groups=groups)]
    all_to_all x4, waiting for transfers between devices: 15.2 us -> 12.1 us  [exchanged(): return lax.all_to_all(value, axis, 0, 0, axis_index_groups=groups)]
    ppermute x1, starting transfers between devices: 2.13 us -> 5.06 us  [transposed_owner(): return lax.ppermute(value, ('dp', 'tensor'), pairs)]
  transfers between devices with their start and end apart: 13 -> 13, of which waited for: 10 -> 10; matrix products, arithmetic and copies ran while one was open for 1% -> 2% of each run, Pallas kernels for 6% -> 6%
where the time goes in v7:
time: 157 us; the launch traced here: 156 us
  blocking collectives  52.1 us (33%)
  starting transfers between devices  47.8 us (30%)
  waiting for transfers between devices  28.3 us (18%)
  Pallas kernels  18.8 us (12%)
  local copies, waits for them, and re-layouts  5.58 us (4%)
  matrix products  2.87 us (2%)
    all_to_all x4, blocking collectives, exchanged(): return lax.all_to_all(value, axis, 0, 0, axis_index_groups=groups)  52.1 us
    all_to_all x4, starting transfers between devices, exchanged(): return lax.all_to_all(value, axis, 0, 0, axis_index_groups=groups)  23.2 us
    pallas_call x13, Pallas kernels, call(): pl.pallas_call(body, out_shape=[pltpu.HBM(shape, dtype) if place in far_o...  18.8 us
    ppermute x6, waiting for transfers between devices, turned(): return lax.ppermute(value, 'dp', pairs)  16.1 us
    ppermute x2, starting transfers between devices, swapped_2(): lax.ppermute(value, axis, [(i, i ^ 1 << distance) for i in range(lax.axis...  14.7 us
    all_to_all x4, waiting for transfers between devices, exchanged(): return lax.all_to_all(value, axis, 0, 0, axis_index_groups=groups)  12.1 us
    ppermute x1, starting transfers between devices, transposed_owner(): return lax.ppermute(value, ('dp', 'tensor'), pairs)  5.06 us
    ppermute x6, starting transfers between devices, turned(): return lax.ppermute(value, 'dp', pairs)  4.79 us
  transfers between devices with their start and end apart: 13, of which 10 were waited for; matrix products, arithmetic and copies ran while one was open for 2% of the time, Pallas kernels for 6%

profile of v7, /device:TPU:1, one launch (start us, length us, event | category | flops | bytes accessed | tf_op | source)
XLA Modules:
  0.0 156.2 jit_solution(10880431968712161346)
XLA Ops:
  0.6 0.0 copy-start
  0.6 1.1 copy-done
  1.7 2.9 %convolution_convert_fusion.refs_0_ = bf16[768,768]{1,0:T(8,128)(2,1)} fusion(bf16[1,384,768]{2,1,0:T(8,128)(2,1)S(1)} %copy-done, bf16[1,768,384]{2,1,0:T(8,128)(2,1)} %param.17), kind=kOutput, calls=%fused_computation | convolution fusion | flops 453574656 | bytes 2359296 | tf_op jit(solution)/shard_map/dot_general | solution.py:85
  4.6 5.1 %all-to-all-start = ((bf16[4,192,768]{2,1,0:T(8,128)(2,1)}), bf16[4,192,768]{2,1,0:T(8,128)(2,1)S(1)}, u32[]{:S(2)}, u32[]{:S(2)}) async-start(bf16[4,192,768]{2,1,0:T(8,128)(2,1)} %bitcast.10), calls=%async_computation | async-start | bytes 2359296 | tf_op jit(solution)/shard_map/all_to_all | solution.py:29
  9.7 1.9 %collective-permute-start = (s32[1]{0:T(128)}, s32[1]{0:T(128)}, u32[]{:S(2)}, u32[]{:S(2)}) collective-permute-start(s32[1]{0:T(128)} %bitcast), channel_id=1, source_target_pairs={{0,8},{8,0},{1,9},{9,1},{2,10},{10,2},{3,11},{11,3},{4,12},{12,4},... | collective-permute-start | bytes 20 | tf_op jit(solution)/shard_map/ppermute | solution.py:25
  11.6 0.6 dynamic-slice_bitcast_fusion
  12.2 5.1 %collective-permute-start.1 = (bf16[48,768]{1,0:T(8,128)(2,1)}, bf16[48,768]{1,0:T(8,128)(2,1)}, u32[]{:S(2)}, u32[]{:S(2)}) collective-permute-start(bf16[48,768]{1,0:T(8,128)(2,1)} %dynamic-slice_bitcast_fusion), channel_id=1, source_target_pairs={{5,0},{18,1},{38,2},{48,3},{71,4},{84,5},{102,6},{117,7},{3,16},{2... | collective-permute-start | bytes 221192 | tf_op jit(solution)/shard_map/ppermute | solution.py:66
  17.3 0.7 dynamic-slice_bitcast_fusion.1
  18.0 0.0 collective-permute-done.refs_0_
  18.0 0.7 concatenate.3.refs_1_.refs_0_
  18.7 0.0 copy-done.1
  18.7 0.0 copy-done.12
  18.7 0.0 copy-done.13
  18.7 0.0 copy-start.2
  18.7 1.4 copy-done.2
  20.1 2.4 %shard_map.155 = (bf16[3,128,768]{2,1,0:T(8,128)(2,1)}, f32[1,768]{1,0:T(1,128)S(1)}, f32[1,768]{1,0:T(1,128)S(1)}, f32[16,6144]{1,0:T(8,128)}, f32[16,6144]{1,0:T(8,128)}) custom-call(bf16[768,768]{1,0:T(8,128)(2,1)} %convolution_convert_fusion.refs_0_, s32[20]{0:T(128)S(1)} %concatenate.3.refs_1_.refs_0_, bf16[128,6144]{1,0:T(8,128)(2,1)S(1)} %bitcast.35, ...), custom_call_target="tpu_custom_call" | custom-call | flops 1 | bytes 4000000 | tf_op jit(solution)/shard_map/pallas_call | solution.py:113
  22.5 0.0 collective-permute-done.1.refs_0_.refs_1_
  22.5 2.0 %all-to-all-done.refs_2_ = bf16[4,192,768]{2,1,0:T(8,128)(2,1)S(1)} async-done(((bf16[4,192,768]{2,1,0:T(8,128)(2,1)}), bf16[4,192,768]{2,1,0:T(8,128)(2,1)S(1)}, u32[]{:S(2)}, u32[]{:S(2)}) %all-to-all-start) | async-done | bytes 1179680 | tf_op jit(solution)/shard_map/all_to_all | solution.py:29
  24.5 0.9 shard_map.156.refs_0_
  25.4 9.0 %all-to-all-start.1 = ((bf16[4,48,768]{2,1,0:T(8,128)(2,1)}), bf16[4,48,768]{2,1,0:T(8,128)(2,1)S(1)}, u32[]{:S(2)}, u32[]{:S(2)}) async-start(bf16[4,48,768]{2,1,0:T(8,128)(2,1)} %bitcast.16), calls=%async_computation.1 | async-start | bytes 589824 | tf_op jit(solution)/shard_map/all_to_all | solution.py:29
  34.3 0.0 copy-done.14
  34.4 0.1 copy.17
  34.5 0.1 broadcast_in_dim.21
  34.5 0.1 eq.22
  34.6 0.1 copy.18
  34.8 0.0 copy-done.5
  34.8 0.0 copy-done.6
  34.8 0.0 copy-done.8
  34.8 2.1 %shard_map.157 = (bf16[128,768]{1,0:T(8,128)(2,1)S(1)}, f32[12,128,128]{2,1,0:T(8,128)S(1)}) custom-call(bf16[192,768]{1,0:T(8,128)(2,1)} %shard_map.156.refs_0_, bf16[128,768]{1,0:T(8,128)(2,1)S(1)} %bitcast.38, bf16[128,768]{1,0:T(8,128)(2,1)S(1)} %bitcast.40, bf16[128,768]{1,0:T(8,128)(2,1)S(1)} %bitcast.42, f32[128,128]{1,0:T(8,128)S(1)} %fusion.3.refs_4_), custom_call_target="tpu_custom_call" | custom-call | flops 1 | bytes 4000000 | tf_op jit(solution)/shard_map/pallas_call | solution.py:113
  36.9 5.8 %all-to-all-done.1.refs_1_ = bf16[4,48,768]{2,1,0:T(8,128)(2,1)S(1)} async-done(((bf16[4,48,768]{2,1,0:T(8,128)(2,1)}), bf16[4,48,768]{2,1,0:T(8,128)(2,1)S(1)}, u32[]{:S(2)}, u32[]{:S(2)}) %all-to-all-start.1) | async-done | bytes 294944 | tf_op jit(solution)/shard_map/all_to_all | solution.py:29
  42.7 12.9 %all_to_all.40 = bf16[4,48,768]{2,1,0:T(8,128)(2,1)S(1)} all-to-all(bf16[4,48,768]{2,1,0:T(8,128)(2,1)S(1)} %shard_map.158), channel_id=1, replica_groups={{0,64,128,192},{16,80,144,208},{32,96,160,224},{48,112,176,240},{1,65,1..., dimensions={0} | all-to-all | bytes 589824 | tf_op jit(solution)/shard_map/all_to_all | solution.py:29
  55.6 2.0 %shard_map.159 = (bf16[4,192,768]{2,1,0:T(8,128)(2,1)}, bf16[48,768]{1,0:T(8,128)(2,1)S(1)}) custom-call(bf16[192,768]{1,0:T(8,128)(2,1)S(1)} %bitcast.37, bf16[48,768]{1,0:T(8,128)(2,1)} %collective-permute-done.1.refs_0_.refs_1_), custom_call_target="tpu_custom_call" | custom-call | flops 1 | bytes 4000000 | tf_op jit(solution)/shard_map/pallas_call | solution.py:113
  57.6 5.1 %all-to-all-start.3 = ((bf16[4,192,768]{2,1,0:T(8,128)(2,1)}), bf16[4,192,768]{2,1,0:T(8,128)(2,1)S(1)}, u32[]{:S(2)}, u32[]{:S(2)}) async-start(bf16[4,192,768]{2,1,0:T(8,128)(2,1)} %get-tuple-element.25), calls=%async_computation.3 | async-start | bytes 2359296 | tf_op jit(solution)/shard_map/all_to_all | solution.py:29
  62.8 0.3 collective-permute-start.4
  63.1 2.4 %collective-permute-start.3 = (bf16[48,768]{1,0:T(8,128)(2,1)S(1)}, bf16[48,768]{1,0:T(8,128)(2,1)S(1)}, u32[]{:S(2)}, u32[]{:S(2)}) collective-permute-start(bf16[48,768]{1,0:T(8,128)(2,1)S(1)} %get-tuple-element.26.refs_1_), channel_id=1, source_target_pairs={{0,128},{16,144},{32,160},{48,176},{64,192},{80,208},{96,224},{112... | collective-permute-start | bytes 221192 | tf_op jit(solution)/shard_map/ppermute | solution.py:38
  65.5 0.2 collective-permute-start.2
  65.7 1.5 collective-permute-done.4.refs_4_
  67.3 3.9 %collective-permute-done.3.refs_3_ = bf16[48,768]{1,0:T(8,128)(2,1)S(1)} collective-permute-done((bf16[48,768]{1,0:T(8,128)(2,1)S(1)}, bf16[48,768]{1,0:T(8,128)(2,1)S(1)}, u32[]{:S(2)}, u32[]{:S(2)}) %collective-permute-start.3) | collective-permute-done | bytes 73760 | tf_op jit(solution)/shard_map/ppermute | solution.py:38
  71.2 1.1 collective-permute-done.2.refs_2_
  72.3 0.6 shard_map.160.refs_2_
  72.8 3.0 %all-to-all-done.3 = bf16[4,192,768]{2,1,0:T(8,128)(2,1)S(1)} async-done(((bf16[4,192,768]{2,1,0:T(8,128)(2,1)}), bf16[4,192,768]{2,1,0:T(8,128)(2,1)S(1)}, u32[]{:S(2)}, u32[]{:S(2)}) %all-to-all-start.3) | async-done | bytes 1179680 | tf_op jit(solution)/shard_map/all_to_all | solution.py:29
  75.9 1.5 shard_map.161
  77.4 4.0 %all-to-all-start.4 = ((bf16[8,128,768]{2,1,0:T(8,128)(2,1)}), bf16[8,128,768]{2,1,0:T(8,128)(2,1)S(1)}, u32[]{:S(2)}, u32[]{:S(2)}) async-start(bf16[8,128,768]{2,1,0:T(8,128)(2,1)} %get-tuple-element.27), calls=%async_computation.4 | async-start | bytes 3145728 | tf_op jit(solution)/shard_map/all_to_all | solution.py:29
  81.4 0.7 collective-permute-start.7
  82.0 1.1 collective-permute-start.6
  83.2 0.0 collective-permute-start.5
  83.2 4.0 %collective-permute-done.7.refs_4_ = bf16[4,48,768]{2,1,0:T(8,128)(2,1)S(1)} collective-permute-done((bf16[4,48,768]{2,1,0:T(8,128)(2,1)}, bf16[4,48,768]{2,1,0:T(8,128)(2,1)S(1)}, u32[]{:S(2)}, u32[]{:S(2)}) %collective-permute-start.7) | collective-permute-done | bytes 294944 | tf_op jit(solution)/shard_map/ppermute | solution.py:38
  87.2 2.3 %collective-permute-done.6.refs_3_ = bf16[4,48,768]{2,1,0:T(8,128)(2,1)S(1)} collective-permute-done((bf16[4,48,768]{2,1,0:T(8,128)(2,1)}, bf16[4,48,768]{2,1,0:T(8,128)(2,1)S(1)}, u32[]{:S(2)}, u32[]{:S(2)}) %collective-permute-start.6) | collective-permute-done | bytes 294944 | tf_op jit(solution)/shard_map/ppermute | solution.py:38
  89.4 3.4 %collective-permute-done.5.refs_2_ = bf16[4,48,768]{2,1,0:T(8,128)(2,1)S(1)} collective-permute-done((bf16[4,48,768]{2,1,0:T(8,128)(2,1)}, bf16[4,48,768]{2,1,0:T(8,128)(2,1)S(1)}, u32[]{:S(2)}, u32[]{:S(2)}) %collective-permute-start.5) | collective-permute-done | bytes 294944 | tf_op jit(solution)/shard_map/ppermute | solution.py:38
  92.8 3.3 %shard_map.162.refs_1_ = bf16[1168,768]{1,0:T(8,128)(2,1)} custom-call(s32[20]{0:T(128)S(1)} %concatenate.3.refs_1_.refs_0_, bf16[4,48,768]{2,1,0:T(8,128)(2,1)} %get-tuple-element.28.refs_1_, bf16[4,48,768]{2,1,0:T(8,128)(2,1)S(1)} %collective-permute-done.5.refs_2_, bf16[4,48,768]{2,1,0:T(8,128)(2,1)S(1)} %collective-permute-done.6.refs_3_, ...), custom_call_target="tpu_custom_call" | custom-call | flops 1 | bytes 4000000 | tf_op jit(solution)/shard_map/pallas_call | solution.py:113
  96.1 1.3 all-to-all-done.4.refs_0_
  97.4 2.5 %shard_map.163 = bf16[8,16,3456]{2,1,0:T(8,128)(2,1)S(1)} custom-call(bf16[8,128,768]{2,1,0:T(8,128)(2,1)S(1)} %all-to-all-done.4.refs_0_, bf16[1168,768]{1,0:T(8,128)(2,1)} %shard_map.162.refs_1_, f32[1,768]{1,0:T(1,128)S(1)} %get-tuple-element.23.refs_1_.refs_6_.refs_2_), custom_call_target="tpu_custom_call" | custom-call | flops 1 | bytes 4000000 | tf_op jit(solution)/shard_map/pallas_call | solution.py:113
  99.9 13.7 %all_to_all.41.refs_0_ = bf16[8,16,3456]{2,1,0:T(8,128)(2,1)S(1)} all-to-all(bf16[8,16,3456]{2,1,0:T(8,128)(2,1)S(1)} %shard_map.163), channel_id=1, replica_groups=mesh['dp'=16,'section'=2,'tensor'=8] {'tensor'}, dimensions={0} | all-to-all | bytes 1769472 | tf_op jit(solution)/shard_map/all_to_all | solution.py:29
  113.6 0.0 copy-done.11
  113.6 1.1 shard_map.164
  114.6 15.8 %all_to_all.42.refs_1_ = bf16[16,16,768]{2,1,0:T(8,128)(2,1)S(1)} all-to-all(bf16[16,16,768]{2,1,0:T(8,128)(2,1)S(1)} %get-tuple-element.34), channel_id=1, replica_groups=mesh['dp'=16,'section'=2,'tensor'=8] {'dp'}, dimensions={0} | all-to-all | bytes 786432 | tf_op jit(solution)/shard_map/all_to_all | solution.py:29
  130.4 0.2 shard_map.165
  130.6 9.7 %all_to_all.43.refs_1_ = bf16[8,16,1536]{2,1,0:T(8,128)(2,1)S(1)} all-to-all(bf16[8,16,1536]{2,1,0:T(8,128)(2,1)S(1)} %shard_map.165), channel_id=1, replica_groups=mesh['dp'=16,'section'=2,'tensor'=8] {'tensor'}, dimensions={0} | all-to-all | bytes 786432 | tf_op jit(solution)/shard_map/all_to_all | solution.py:29
  140.3 0.6 shard_map.166.refs_0_
  140.9 12.8 %collective-permute-start.8 = (bf16[16,768]{1,0:T(8,128)(2,1)S(1)}, bf16[16,768]{1,0:T(8,128)(2,1)S(1)}, u32[]{:S(2)}, u32[]{:S(2)}) collective-permute-start(bf16[16,768]{1,0:T(8,128)(2,1)S(1)} %shard_map.166.refs_0_), channel_id=1, source_target_pairs={{0,8},{8,0},{1,9},{9,1},{2,10},{10,2},{3,11},{11,3},{4,12},{12,4},... | collective-permute-start | bytes 73736 | tf_op jit(solution)/shard_map/ppermute | solution.py:25
  153.8 0.0 copy-done.4
  153.8 1.8 %shard_map.167 = (bf16[128,768]{1,0:T(8,128)(2,1)}, bf16[128,768]{1,0:T(8,128)(2,1)}, bf16[128,768]{1,0:T(8,128)(2,1)}) custom-call(bf16[16,768]{1,0:T(8,128)(2,1)S(1)} %shard_map.166.refs_0_, bf16[8,16,1536]{2,1,0:T(8,128)(2,1)S(1)} %all_to_all.43.refs_1_, bf16[768,768]{1,0:T(8,128)(2,1)S(1)} %bitcast.34, bf16[128,768]{1,0:T(8,128)(2,1)S(1)} %bitcast.39, ...), custom_call_target="tpu_custom_call" | custom-call | flops 1 | bytes 4000000 | tf_op jit(solution)/shard_map/pallas_call | solution.py:113
  155.6 0.0 collective-permute-done.8
  155.6 0.6 copy.20
  (21 shorter events, 0.1 us)
Async XLA Ops:
  0.6 1.1 copy-start
  4.6 14.1 %copy-start.1 = (bf16[1,1,128,6144]{3,2,1,0:T(8,128)(2,1)S(1)}, bf16[1,1,128,6144]{3,2,1,0:T(8,128)(2,1)}, u32[]{:S(2)}) copy-start(bf16[1,1,128,6144]{3,2,1,0:T(8,128)(2,1)} %param.12) | copy-start | bytes 4718596
  4.6 14.1 %copy-start.12 = (f32[1,6144]{1,0:T(1,128)S(1)}, f32[1,6144]{1,0:T(1,128)}, u32[]{:S(2)}) copy-start(f32[1,6144]{1,0:T(1,128)} %refs_4_.1) | copy-start | bytes 73732
  4.6 14.1 %copy-start.13 = (f32[1,6144]{1,0:T(1,128)S(1)}, f32[1,6144]{1,0:T(1,128)}, u32[]{:S(2)}) copy-start(f32[1,6144]{1,0:T(1,128)} %refs_5_.1) | copy-start | bytes 73732
  4.6 19.9 %all-to-all-start = ((bf16[4,192,768]{2,1,0:T(8,128)(2,1)}), bf16[4,192,768]{2,1,0:T(8,128)(2,1)S(1)}, u32[]{:S(2)}, u32[]{:S(2)}) async-start(bf16[4,192,768]{2,1,0:T(8,128)(2,1)} %bitcast.10), calls=%async_computation | async-start | bytes 2359296 | tf_op jit(solution)/shard_map/all_to_all | solution.py:29
  9.7 8.2 %collective-permute-start = (s32[1]{0:T(128)}, s32[1]{0:T(128)}, u32[]{:S(2)}, u32[]{:S(2)}) collective-permute-start(s32[1]{0:T(128)} %bitcast), channel_id=1, source_target_pairs={{0,8},{8,0},{1,9},{9,1},{2,10},{10,2},{3,11},{11,3},{4,12},{12,4},... | collective-permute-start | bytes 20 | tf_op jit(solution)/shard_map/ppermute | solution.py:25
  12.2 10.3 %collective-permute-start.1 = (bf16[48,768]{1,0:T(8,128)(2,1)}, bf16[48,768]{1,0:T(8,128)(2,1)}, u32[]{:S(2)}, u32[]{:S(2)}) collective-permute-start(bf16[48,768]{1,0:T(8,128)(2,1)} %dynamic-slice_bitcast_fusion), channel_id=1, source_target_pairs={{5,0},{18,1},{38,2},{48,3},{71,4},{84,5},{102,6},{117,7},{3,16},{2... | collective-permute-start | bytes 221192 | tf_op jit(solution)/shard_map/ppermute | solution.py:66
  18.7 1.4 copy-start.2
  22.5 11.9 %copy-start.14 = (s32[1,1,4,4]{3,2,1,0:T(4,128)S(1)}, s32[1,1,4,4]{3,2,1,0:T(4,128)}, u32[]{:S(2)}) copy-start(s32[1,1,4,4]{3,2,1,0:T(4,128)} %param.16) | copy-start | bytes 196
  22.5 12.3 %copy-start.5 = (bf16[1,1,128,768]{3,2,1,0:T(8,128)(2,1)S(1)}, bf16[1,1,128,768]{3,2,1,0:T(8,128)(2,1)}, u32[]{:S(2)}) copy-start(bf16[1,1,128,768]{3,2,1,0:T(8,128)(2,1)} %param.13) | copy-start | bytes 589828
  22.5 12.3 %copy-start.6 = (bf16[1,1,128,768]{3,2,1,0:T(8,128)(2,1)S(1)}, bf16[1,1,128,768]{3,2,1,0:T(8,128)(2,1)}, u32[]{:S(2)}) copy-start(bf16[1,1,128,768]{3,2,1,0:T(8,128)(2,1)} %param.14) | copy-start | bytes 589828
  22.5 12.3 %copy-start.8 = (bf16[1,1,128,768]{3,2,1,0:T(8,128)(2,1)S(1)}, bf16[1,1,128,768]{3,2,1,0:T(8,128)(2,1)}, u32[]{:S(2)}) copy-start(bf16[1,1,128,768]{3,2,1,0:T(8,128)(2,1)} %param.15) | copy-start | bytes 589828
  25.4 17.3 %all-to-all-start.1 = ((bf16[4,48,768]{2,1,0:T(8,128)(2,1)}), bf16[4,48,768]{2,1,0:T(8,128)(2,1)S(1)}, u32[]{:S(2)}, u32[]{:S(2)}) async-start(bf16[4,48,768]{2,1,0:T(8,128)(2,1)} %bitcast.16), calls=%async_computation.1 | async-start | bytes 589824 | tf_op jit(solution)/shard_map/all_to_all | solution.py:29
  36.9 20.7 %copy-start.3 = (f32[12,128,128]{2,1,0:T(8,128)}, f32[12,128,128]{2,1,0:T(8,128)S(1)}, u32[]{:S(2)}) copy-start(f32[12,128,128]{2,1,0:T(8,128)S(1)} %get-tuple-element.37.refs_6_) | copy-start | bytes 2359300
  57.6 18.3 %all-to-all-start.3 = ((bf16[4,192,768]{2,1,0:T(8,128)(2,1)}), bf16[4,192,768]{2,1,0:T(8,128)(2,1)S(1)}, u32[]{:S(2)}, u32[]{:S(2)}) async-start(bf16[4,192,768]{2,1,0:T(8,128)(2,1)} %get-tuple-element.25), calls=%async_computation.3 | async-start | bytes 2359296 | tf_op jit(solution)/shard_map/all_to_all | solution.py:29
  62.8 4.5 %collective-permute-start.4 = (bf16[48,768]{1,0:T(8,128)(2,1)S(1)}, bf16[48,768]{1,0:T(8,128)(2,1)S(1)}, u32[]{:S(2)}, u32[]{:S(2)}) collective-permute-start(bf16[48,768]{1,0:T(8,128)(2,1)S(1)} %get-tuple-element.26.refs_1_), channel_id=1, source_target_pairs={{0,192},{16,208},{32,224},{48,240},{64,0},{80,16},{96,32},{112,48}... | collective-permute-start | bytes 221192 | tf_op jit(solution)/shard_map/ppermute | solution.py:38
  63.1 8.1 %collective-permute-start.3 = (bf16[48,768]{1,0:T(8,128)(2,1)S(1)}, bf16[48,768]{1,0:T(8,128)(2,1)S(1)}, u32[]{:S(2)}, u32[]{:S(2)}) collective-permute-start(bf16[48,768]{1,0:T(8,128)(2,1)S(1)} %get-tuple-element.26.refs_1_), channel_id=1, source_target_pairs={{0,128},{16,144},{32,160},{48,176},{64,192},{80,208},{96,224},{112... | collective-permute-start | bytes 221192 | tf_op jit(solution)/shard_map/ppermute | solution.py:38
  65.5 6.8 %collective-permute-start.2 = (bf16[48,768]{1,0:T(8,128)(2,1)S(1)}, bf16[48,768]{1,0:T(8,128)(2,1)S(1)}, u32[]{:S(2)}, u32[]{:S(2)}) collective-permute-start(bf16[48,768]{1,0:T(8,128)(2,1)S(1)} %get-tuple-element.26.refs_1_), channel_id=1, source_target_pairs={{0,64},{16,80},{32,96},{48,112},{64,128},{80,144},{96,160},{112,17... | collective-permute-start | bytes 221192 | tf_op jit(solution)/shard_map/ppermute | solution.py:38
  77.4 20.0 %all-to-all-start.4 = ((bf16[8,128,768]{2,1,0:T(8,128)(2,1)}), bf16[8,128,768]{2,1,0:T(8,128)(2,1)S(1)}, u32[]{:S(2)}, u32[]{:S(2)}) async-start(bf16[8,128,768]{2,1,0:T(8,128)(2,1)} %get-tuple-element.27), calls=%async_computation.4 | async-start | bytes 3145728 | tf_op jit(solution)/shard_map/all_to_all | solution.py:29
  81.4 5.8 %collective-permute-start.7 = (bf16[4,48,768]{2,1,0:T(8,128)(2,1)}, bf16[4,48,768]{2,1,0:T(8,128)(2,1)S(1)}, u32[]{:S(2)}, u32[]{:S(2)}) collective-permute-start(bf16[4,48,768]{2,1,0:T(8,128)(2,1)} %get-tuple-element.28.refs_1_), channel_id=1, source_target_pairs={{0,48},{16,0},{32,16},{48,32},{64,112},{80,64},{96,80},{112,96},{1... | collective-permute-start | bytes 884744 | tf_op jit(solution)/shard_map/ppermute | solution.py:38
  82.0 7.4 %collective-permute-start.6 = (bf16[4,48,768]{2,1,0:T(8,128)(2,1)}, bf16[4,48,768]{2,1,0:T(8,128)(2,1)S(1)}, u32[]{:S(2)}, u32[]{:S(2)}) collective-permute-start(bf16[4,48,768]{2,1,0:T(8,128)(2,1)} %get-tuple-element.28.refs_1_), channel_id=1, source_target_pairs={{0,32},{16,48},{32,0},{48,16},{64,96},{80,112},{96,64},{112,80},{1... | collective-permute-start | bytes 884744 | tf_op jit(solution)/shard_map/ppermute | solution.py:38
  83.2 9.6 %collective-permute-start.5 = (bf16[4,48,768]{2,1,0:T(8,128)(2,1)}, bf16[4,48,768]{2,1,0:T(8,128)(2,1)S(1)}, u32[]{:S(2)}, u32[]{:S(2)}) collective-permute-start(bf16[4,48,768]{2,1,0:T(8,128)(2,1)} %get-tuple-element.28.refs_1_), channel_id=1, source_target_pairs={{0,16},{16,32},{32,48},{48,0},{64,80},{80,96},{96,112},{112,64},{1... | collective-permute-start | bytes 884744 | tf_op jit(solution)/shard_map/ppermute | solution.py:38
  99.8 13.7 %copy-start.10 = (f32[16,6144]{1,0:T(8,128)S(1)}, f32[16,6144]{1,0:T(8,128)}, u32[]{:S(2)}) copy-start(f32[16,6144]{1,0:T(8,128)} %get-tuple-element.31.refs_1_) | copy-start | bytes 1179652
  99.9 13.7 %copy-start.11 = (f32[16,6144]{1,0:T(8,128)S(1)}, f32[16,6144]{1,0:T(8,128)}, u32[]{:S(2)}) copy-start(f32[16,6144]{1,0:T(8,128)} %get-tuple-element.32.refs_2_) | copy-start | bytes 1179652
  114.6 39.1 %copy-start.4 = (f32[12,128,128]{2,1,0:T(8,128)S(1)}, f32[12,128,128]{2,1,0:T(8,128)}, u32[]{:S(2)}) copy-start(f32[12,128,128]{2,1,0:T(8,128)} %copy-done.3) | copy-start | bytes 2359300
  114.6 39.1 %copy-start.7 = (bf16[1,1,128,768]{3,2,1,0:T(8,128)(2,1)S(1)}, bf16[1,1,128,768]{3,2,1,0:T(8,128)(2,1)}, u32[]{:S(2)}) copy-start(bf16[1,1,128,768]{3,2,1,0:T(8,128)(2,1)} %param.14) | copy-start | bytes 589828
  114.6 39.1 %copy-start.9 = (bf16[1,1,128,768]{3,2,1,0:T(8,128)(2,1)S(1)}, bf16[1,1,128,768]{3,2,1,0:T(8,128)(2,1)}, u32[]{:S(2)}) copy-start(bf16[1,1,128,768]{3,2,1,0:T(8,128)(2,1)} %param.15) | copy-start | bytes 589828
  140.9 14.6 %collective-permute-start.8 = (bf16[16,768]{1,0:T(8,128)(2,1)S(1)}, bf16[16,768]{1,0:T(8,128)(2,1)S(1)}, u32[]{:S(2)}, u32[]{:S(2)}) collective-permute-start(bf16[16,768]{1,0:T(8,128)(2,1)S(1)} %shard_map.166.refs_0_), channel_id=1, source_target_pairs={{0,8},{8,0},{1,9},{9,1},{2,10},{10,2},{3,11},{11,3},{4,12},{12,4},... | collective-permute-start | bytes 73736 | tf_op jit(solution)/shard_map/ppermute | solution.py:25

commit v8 on v7

--- a/solution.py
+++ b/solution.py
@@ -189,59 +189,31 @@
         out_ref[copy] = total
 
 
-def pack_kernel(places_ref, *refs):
-    here_ref, gain_ref, bias_ref, pack_ref = refs[N_LOW:]
-    for high in range(N_HIGH):
-        for step in range(N_LOW):
-            piece = refs[step][high]
-            place = high * N_LOW + (places_ref[2] + N_LOW - step) % N_LOW
-            part = place // N_TENSOR * N_TENSOR + places_ref[4 + place]
-            start = pl.multiple_of(part * piece.shape[0], EXTRA_ROWS)
-            pack_ref[pl.ds(start, piece.shape[0])] = piece
-    _, length, features = here_ref.shape
-    width = pack_ref.shape[1]
-    book = pack_ref[:features]
-    pack_ref[features : features + length] = times(here_ref[0], book).astype(jnp.bfloat16)
-    pack_ref[features + length : features + 2 * length] = here_ref[1]
-    pack_ref[features + 2 * length : features + 3 * length] = here_ref[2]
-    row = lax.broadcasted_iota(jnp.int32, (EXTRA_ROWS, features), 0)
-    rest = jnp.where(row == 0, 1.0, jnp.where(row == 1, gain_ref[...], 0.0))
-    rest = jnp.where(row == 2, bias_ref[...], rest)
-    total = jnp.zeros((EXTRA_ROWS, width), jnp.float32)
-    for _ in range(3):
-        top = rest.astype(jnp.bfloat16)
-        rest = rest - top.astype(jnp.float32)
-        total += times(top, book)
-    upper = total.astype(jnp.bfloat16).astype(jnp.float32)
-    lower = pltpu.roll(total - upper, 3, 0)
-    row = lax.broadcasted_iota(jnp.int32, total.shape, 0)
-    both = jnp.where(row < 3, upper, jnp.where(row < 6, lower, 0.0))
-    half = width // 2
-    extra = both[:, :half] + pltpu.roll(both[:, half:], 6, 0)
-    wanted = places_ref[3].astype(jnp.float32)
-    extra = jnp.where(row[:, :half] == ORDER_ROW, wanted, extra).astype(jnp.bfloat16)
-    pack_ref[features + 3 * length :, :half] = extra
-    pack_ref[features + 3 * length :, half:] = extra
-
-
-def feature_kernel(parts_ref, pack_hbm, gain_ref, out_ref, pack_ref, semaphores):
+def feature_kernel(places_ref, parts_ref, *refs):
+    columns_hbm, (here_hbm, gain_ref, bias_ref, out_ref) = refs[:N_LOW], refs[N_LOW : N_LOW + 4]
+    columns_ref, here_ref, book_ref, semaphores = refs[N_LOW + 4 :]
     count, rows, _ = out_ref.shape
-    features = gain_ref.shape[1]
-    width = pack_ref.shape[1]
-    length = count * rows
-    rest = pl.ds(features, pack_ref.shape[0] - features)
+    features, width = book_ref.shape
     copies = [
-        pltpu.make_async_copy(pack_hbm.at[there], pack_ref.at[there], semaphores.at[place])
-        for place, there in enumerate((pl.ds(0, features), rest))
+        pltpu.make_async_copy(column, columns_ref.at[step], semaphores.at[step])
+        for step, column in enumerate(columns_hbm)
     ]
+    copies.append(pltpu.make_async_copy(here_hbm, here_ref, semaphores.at[N_LOW]))
     for copy in copies:
         copy.start()
     total = parts_ref[0].astype(jnp.float32)
     for part in range(1, count):
         total += parts_ref[part].astype(jnp.float32)
     code = total.astype(jnp.bfloat16)
-    copies[0].wait()
-    book = pack_ref[:features]
+    for step in range(N_LOW):
+        copies[step].wait()
+        for high in range(N_HIGH):
+            piece = columns_ref[step, high]
+            place = high * N_LOW + (places_ref[2] + N_LOW - step) % N_LOW
+            part = place // N_TENSOR * N_TENSOR + places_ref[4 + place]
+            start = pl.multiple_of(part * piece.shape[0], EXTRA_ROWS)
+            book_ref[pl.ds(start, piece.shape[0])] = piece
+    book = book_ref[...]
 
     def put(start, value):
         value = value.astype(jnp.bfloat16)
@@ -249,14 +221,27 @@
 
     decoded = times_transposed(code, book)
     put(3 * width, decoded)
-    copies[1].wait()
-    upper = pack_ref[features + length : features + 2 * length].astype(jnp.float32)
-    lower = pack_ref[features + 2 * length : features + 3 * length].astype(jnp.float32)
-    hidden = upper + lower + decoded
+    copies[N_LOW].wait()
+    put(2 * width, times(here_ref[0], book))
+    hidden = here_ref[1].astype(jnp.float32) + here_ref[2].astype(jnp.float32) + decoded
     put(0, times(hidden.astype(jnp.bfloat16), book))
     put(width, times((hidden * gain_ref[...]).astype(jnp.bfloat16), book))
-    put(2 * width, pack_ref[features : features + length])
-    extra = pack_ref[features + 3 * length :, : width // 2]
+    row = lax.broadcasted_iota(jnp.int32, (EXTRA_ROWS, features), 0)
+    rest = jnp.where(row == 0, 1.0, jnp.where(row == 1, gain_ref[...], 0.0))
+    rest = jnp.where(row == 2, bias_ref[...], rest)
+    sums = jnp.zeros((EXTRA_ROWS, width), jnp.float32)
+    for _ in range(3):
+        top = rest.astype(jnp.bfloat16)
+        rest = rest - top.astype(jnp.float32)
+        sums += times(top, book)
+    upper = sums.astype(jnp.bfloat16).astype(jnp.float32)
+    lower = pltpu.roll(sums - upper, 3, 0)
+    row = lax.broadcasted_iota(jnp.int32, sums.shape, 0)
+    both = jnp.where(row < 3, upper, jnp.where(row < 6, lower, 0.0))
+    half = width // 2
+    extra = both[:, :half] + pltpu.roll(both[:, half:], 6, 0)
+    wanted = places_ref[3].astype(jnp.float32)
+    extra = jnp.where(row[:, :half] == ORDER_ROW, wanted, extra).astype(jnp.bfloat16)
     for copy in range(count):
         out_ref[copy, :, 3 * width + features :] = extra
 
@@ -502,26 +487,23 @@
     )
     columns = [column] + [turned(column, 0, step) for step in range(1, N_LOW)]
     code_parts = exchanged(sent, "tensor")
-    (pack,) = call(
-        pack_kernel,
-        [((features + 3 * length + EXTRA_ROWS, code_width), bf16)],
+    (sent,) = call(
+        feature_kernel,
+        [((n_tensor, rows, 3 * code_width + features + code_width // 2), bf16)],
+        code_parts,
         *columns,
         here,
         gain_here,
         bias_here,
         places=places,
-        far=(0, N_LOW),
-        far_out=(0,),
-    )
-    (sent,) = call(
-        feature_kernel,
-        [((n_tensor, rows, 3 * code_width + features + code_width // 2), bf16)],
-        code_parts,
-        pack,
-        gain_here,
-        far=(1,),
-        raw=(1,),
-        scratch=[pltpu.VMEM(pack.shape, bf16), pltpu.SemaphoreType.DMA((2,))],
+        far=range(1, N_LOW + 2),
+        raw=range(1, N_LOW + 2),
+        scratch=[
+            pltpu.VMEM((N_LOW,) + column.shape, bf16),
+            pltpu.VMEM(here.shape, bf16),
+            pltpu.VMEM((features, code_width), bf16),
+            pltpu.SemaphoreType.DMA((N_LOW + 1,)),
+        ],
     )
     arrived = exchanged(sent, "tensor")
     codes, grad_code, grad_residual, orders = call(

time: 157 us -> 153 us (0.975)
  starting transfers between devices: 47.8 us -> 41.1 us
  waiting for transfers between devices: 28.3 us -> 30.8 us
  Pallas kernels: 18.8 us -> 16.9 us
  blocking collectives: 52.1 us -> 53.8 us
    ppermute x2, starting transfers between devices: 14.7 us -> 8.01 us  [swapped_2(): lax.ppermute(value, axis, [(i, i ^ 1 << distance) for i in range(lax.axis...]
    all_to_all x4, waiting for transfers between devices: 12.1 us -> 15.4 us  [exchanged(): return lax.all_to_all(value, axis, 0, 0, axis_index_groups=groups)]
    pallas_call x13 -> x12, Pallas kernels: 18.8 us -> 16.9 us  [call(): pl.pallas_call(body, out_shape=[pltpu.HBM(shape, dtype) if place in far_o...]
    all_to_all x4, blocking collectives: 52.1 us -> 53.8 us  [exchanged(): return lax.all_to_all(value, axis, 0, 0, axis_index_groups=groups)]
    unnamed x31 -> x35, local copies, waits for them, and re-layouts: 3.12 us -> 3.85 us
  transfers between devices with their start and end apart: 13 -> 13, of which waited for: 10 -> 10; matrix products, arithmetic and copies ran while one was open for 2% -> 2% of each run, Pallas kernels for 6% -> 4%
where the time goes in v8:
time: 153 us
  blocking collectives  53.8 us (35%)
  starting transfers between devices  41.1 us (27%)
  waiting for transfers between devices  30.8 us (20%)
  Pallas kernels  16.9 us (11%)
  local copies, waits for them, and re-layouts  6.36 us (4%)
  matrix products  2.88 us (2%)
    all_to_all x4, blocking collectives, exchanged(): return lax.all_to_all(value, axis, 0, 0, axis_index_groups=groups)  53.8 us
    all_to_all x4, starting transfers between devices, exchanged(): return lax.all_to_all(value, axis, 0, 0, axis_index_groups=groups)  23.2 us
    pallas_call x12, Pallas kernels, call(): pl.pallas_call(body, out_shape=[pltpu.HBM(shape, dtype) if place in far_o...  16.9 us
    ppermute x6, waiting for transfers between devices, turned(): return lax.ppermute(value, 'dp', pairs)  15.4 us
    all_to_all x4, waiting for transfers between devices, exchanged(): return lax.all_to_all(value, axis, 0, 0, axis_index_groups=groups)  15.4 us
    ppermute x2, starting transfers between devices, swapped_2(): lax.ppermute(value, axis, [(i, i ^ 1 << distance) for i in range(lax.axis...  8.01 us
    ppermute x1, starting transfers between devices, transposed_owner(): return lax.ppermute(value, ('dp', 'tensor'), pairs)  5.06 us
    ppermute x6, starting transfers between devices, turned(): return lax.ppermute(value, 'dp', pairs)  4.8 us
  transfers between devices with their start and end apart: 13, of which 10 were waited for; matrix products, arithmetic and copies ran while one was open for 2% of the time, Pallas kernels for 4%

profile of v8, /device:TPU:1, one launch (start us, length us, event | category | flops | bytes accessed | tf_op | source)
XLA Modules:
  0.0 152.6 jit_solution(1900191463834496201)
XLA Ops:
  0.6 0.0 copy-start
  0.6 1.1 copy-done
  1.7 2.9 %convolution_convert_fusion.refs_0_ = bf16[768,768]{1,0:T(8,128)(2,1)} fusion(bf16[1,384,768]{2,1,0:T(8,128)(2,1)S(1)} %copy-done, bf16[1,768,384]{2,1,0:T(8,128)(2,1)} %param.17), kind=kOutput, calls=%fused_computation | convolution fusion | flops 453574656 | bytes 2359296 | tf_op jit(solution)/shard_map/dot_general | solution.py:85
  4.6 5.1 %all-to-all-start = ((bf16[4,192,768]{2,1,0:T(8,128)(2,1)}), bf16[4,192,768]{2,1,0:T(8,128)(2,1)S(1)}, u32[]{:S(2)}, u32[]{:S(2)}) async-start(bf16[4,192,768]{2,1,0:T(8,128)(2,1)} %bitcast.10), calls=%async_computation | async-start | bytes 2359296 | tf_op jit(solution)/shard_map/all_to_all | solution.py:29
  9.7 1.9 %collective-permute-start = (s32[1]{0:T(128)}, s32[1]{0:T(128)}, u32[]{:S(2)}, u32[]{:S(2)}) collective-permute-start(s32[1]{0:T(128)} %bitcast), channel_id=1, source_target_pairs={{0,8},{8,0},{1,9},{9,1},{2,10},{10,2},{3,11},{11,3},{4,12},{12,4},... | collective-permute-start | bytes 20 | tf_op jit(solution)/shard_map/ppermute | solution.py:25
  11.6 0.6 dynamic-slice_bitcast_fusion
  12.2 5.1 %collective-permute-start.1 = (bf16[48,768]{1,0:T(8,128)(2,1)}, bf16[48,768]{1,0:T(8,128)(2,1)}, u32[]{:S(2)}, u32[]{:S(2)}) collective-permute-start(bf16[48,768]{1,0:T(8,128)(2,1)} %dynamic-slice_bitcast_fusion), channel_id=1, source_target_pairs={{5,0},{18,1},{38,2},{48,3},{71,4},{84,5},{102,6},{117,7},{3,16},{2... | collective-permute-start | bytes 221192 | tf_op jit(solution)/shard_map/ppermute | solution.py:66
  17.3 0.7 dynamic-slice_bitcast_fusion.1
  18.0 0.0 collective-permute-done.refs_0_
  18.0 0.8 concatenate.3.refs_1_.refs_0_
  18.7 0.0 copy-done.1
  18.8 0.0 copy-done.12
  18.8 0.0 copy-done.13
  18.8 0.0 copy-start.2
  18.8 1.4 copy-done.2
  20.2 2.3 %shard_map.155 = (bf16[3,128,768]{2,1,0:T(8,128)(2,1)}, f32[1,768]{1,0:T(1,128)S(1)}, f32[1,768]{1,0:T(1,128)S(1)}, f32[16,6144]{1,0:T(8,128)}, f32[16,6144]{1,0:T(8,128)}) custom-call(bf16[768,768]{1,0:T(8,128)(2,1)} %convolution_convert_fusion.refs_0_, s32[20]{0:T(128)S(1)} %concatenate.3.refs_1_.refs_0_, bf16[128,6144]{1,0:T(8,128)(2,1)S(1)} %bitcast.35, ...), custom_call_target="tpu_custom_call" | custom-call | flops 1 | bytes 4000000 | tf_op jit(solution)/shard_map/pallas_call | solution.py:113
  22.5 0.0 collective-permute-done.1.refs_0_.refs_1_
  22.5 2.0 %all-to-all-done.refs_2_ = bf16[4,192,768]{2,1,0:T(8,128)(2,1)S(1)} async-done(((bf16[4,192,768]{2,1,0:T(8,128)(2,1)}), bf16[4,192,768]{2,1,0:T(8,128)(2,1)S(1)}, u32[]{:S(2)}, u32[]{:S(2)}) %all-to-all-start) | async-done | bytes 1179680 | tf_op jit(solution)/shard_map/all_to_all | solution.py:29
  24.5 0.9 shard_map.156.refs_0_
  25.4 9.0 %all-to-all-start.1 = ((bf16[4,48,768]{2,1,0:T(8,128)(2,1)}), bf16[4,48,768]{2,1,0:T(8,128)(2,1)S(1)}, u32[]{:S(2)}, u32[]{:S(2)}) async-start(bf16[4,48,768]{2,1,0:T(8,128)(2,1)} %bitcast.16), calls=%async_computation.1 | async-start | bytes 589824 | tf_op jit(solution)/shard_map/all_to_all | solution.py:29
  34.4 0.0 copy-done.16
  34.4 0.1 copy.17
  34.5 0.1 broadcast_in_dim.21
  34.6 0.1 eq.22
  34.7 0.1 copy.18
  34.8 0.0 copy-done.5
  34.8 0.0 copy-done.6
  34.8 0.0 copy-done.8
  34.8 2.1 %shard_map.157 = (bf16[128,768]{1,0:T(8,128)(2,1)S(1)}, f32[12,128,128]{2,1,0:T(8,128)S(1)}) custom-call(bf16[192,768]{1,0:T(8,128)(2,1)} %shard_map.156.refs_0_, bf16[128,768]{1,0:T(8,128)(2,1)S(1)} %bitcast.38, bf16[128,768]{1,0:T(8,128)(2,1)S(1)} %bitcast.40, bf16[128,768]{1,0:T(8,128)(2,1)S(1)} %bitcast.42, f32[128,128]{1,0:T(8,128)S(1)} %fusion.3.refs_4_), custom_call_target="tpu_custom_call" | custom-call | flops 1 | bytes 4000000 | tf_op jit(solution)/shard_map/pallas_call | solution.py:113
  36.9 5.8 %all-to-all-done.1.refs_1_ = bf16[4,48,768]{2,1,0:T(8,128)(2,1)S(1)} async-done(((bf16[4,48,768]{2,1,0:T(8,128)(2,1)}), bf16[4,48,768]{2,1,0:T(8,128)(2,1)S(1)}, u32[]{:S(2)}, u32[]{:S(2)}) %all-to-all-start.1) | async-done | bytes 294944 | tf_op jit(solution)/shard_map/all_to_all | solution.py:29
  42.7 12.9 %all_to_all.40 = bf16[4,48,768]{2,1,0:T(8,128)(2,1)S(1)} all-to-all(bf16[4,48,768]{2,1,0:T(8,128)(2,1)S(1)} %shard_map.158), channel_id=1, replica_groups={{0,64,128,192},{16,80,144,208},{32,96,160,224},{48,112,176,240},{1,65,1..., dimensions={0} | all-to-all | bytes 589824 | tf_op jit(solution)/shard_map/all_to_all | solution.py:29
  55.6 2.0 %shard_map.159 = (bf16[4,192,768]{2,1,0:T(8,128)(2,1)}, bf16[48,768]{1,0:T(8,128)(2,1)S(1)}) custom-call(bf16[192,768]{1,0:T(8,128)(2,1)S(1)} %bitcast.37, bf16[48,768]{1,0:T(8,128)(2,1)} %collective-permute-done.1.refs_0_.refs_1_), custom_call_target="tpu_custom_call" | custom-call | flops 1 | bytes 4000000 | tf_op jit(solution)/shard_map/pallas_call | solution.py:113
  57.6 5.1 %all-to-all-start.3 = ((bf16[4,192,768]{2,1,0:T(8,128)(2,1)}), bf16[4,192,768]{2,1,0:T(8,128)(2,1)S(1)}, u32[]{:S(2)}, u32[]{:S(2)}) async-start(bf16[4,192,768]{2,1,0:T(8,128)(2,1)} %get-tuple-element.25), calls=%async_computation.3 | async-start | bytes 2359296 | tf_op jit(solution)/shard_map/all_to_all | solution.py:29
  62.8 0.3 collective-permute-start.4
  63.1 2.4 %collective-permute-start.3 = (bf16[48,768]{1,0:T(8,128)(2,1)S(1)}, bf16[48,768]{1,0:T(8,128)(2,1)S(1)}, u32[]{:S(2)}, u32[]{:S(2)}) collective-permute-start(bf16[48,768]{1,0:T(8,128)(2,1)S(1)} %get-tuple-element.26.refs_1_), channel_id=1, source_target_pairs={{0,128},{16,144},{32,160},{48,176},{64,192},{80,208},{96,224},{112... | collective-permute-start | bytes 221192 | tf_op jit(solution)/shard_map/ppermute | solution.py:38
  65.5 0.2 collective-permute-start.2
  65.7 1.5 %collective-permute-done.4.refs_4_ = bf16[48,768]{1,0:T(8,128)(2,1)S(1)} collective-permute-done((bf16[48,768]{1,0:T(8,128)(2,1)S(1)}, bf16[48,768]{1,0:T(8,128)(2,1)S(1)}, u32[]{:S(2)}, u32[]{:S(2)}) %collective-permute-start.4) | collective-permute-done | bytes 73760 | tf_op jit(solution)/shard_map/ppermute | solution.py:38
  67.3 3.9 %collective-permute-done.3.refs_3_ = bf16[48,768]{1,0:T(8,128)(2,1)S(1)} collective-permute-done((bf16[48,768]{1,0:T(8,128)(2,1)S(1)}, bf16[48,768]{1,0:T(8,128)(2,1)S(1)}, u32[]{:S(2)}, u32[]{:S(2)}) %collective-permute-start.3) | collective-permute-done | bytes 73760 | tf_op jit(solution)/shard_map/ppermute | solution.py:38
  71.2 1.1 collective-permute-done.2.refs_2_
  72.3 0.6 shard_map.160.refs_2_
  72.9 3.0 %all-to-all-done.3 = bf16[4,192,768]{2,1,0:T(8,128)(2,1)S(1)} async-done(((bf16[4,192,768]{2,1,0:T(8,128)(2,1)}), bf16[4,192,768]{2,1,0:T(8,128)(2,1)S(1)}, u32[]{:S(2)}, u32[]{:S(2)}) %all-to-all-start.3) | async-done | bytes 1179680 | tf_op jit(solution)/shard_map/all_to_all | solution.py:29
  75.9 1.6 %shard_map.161 = (bf16[8,128,768]{2,1,0:T(8,128)(2,1)}, bf16[4,48,768]{2,1,0:T(8,128)(2,1)}) custom-call(bf16[128,768]{1,0:T(8,128)(2,1)S(1)} %get-tuple-element.24.refs_0_, bf16[768,768]{1,0:T(8,128)(2,1)S(1)} %bitcast.33, bf16[4,48,768]{2,1,0:T(8,128)(2,1)S(1)} %shard_map.160.refs_2_), custom_call_target="tpu_custom_call" | custom-call | flops 1 | bytes 4000000 | tf_op jit(solution)/shard_map/pallas_call | solution.py:113
  77.5 4.0 %all-to-all-start.4 = ((bf16[8,128,768]{2,1,0:T(8,128)(2,1)}), bf16[8,128,768]{2,1,0:T(8,128)(2,1)S(1)}, u32[]{:S(2)}, u32[]{:S(2)}) async-start(bf16[8,128,768]{2,1,0:T(8,128)(2,1)} %get-tuple-element.27), calls=%async_computation.4 | async-start | bytes 3145728 | tf_op jit(solution)/shard_map/all_to_all | solution.py:29
  81.4 0.7 collective-permute-start.7
  82.1 1.1 collective-permute-start.6
  83.2 0.0 collective-permute-start.5
  83.3 4.0 %collective-permute-done.7.refs_5_ = bf16[4,48,768]{2,1,0:T(8,128)(2,1)S(1)} collective-permute-done((bf16[4,48,768]{2,1,0:T(8,128)(2,1)}, bf16[4,48,768]{2,1,0:T(8,128)(2,1)S(1)}, u32[]{:S(2)}, u32[]{:S(2)}) %collective-permute-start.7) | collective-permute-done | bytes 294944 | tf_op jit(solution)/shard_map/ppermute | solution.py:38
  87.2 2.3 %collective-permute-done.6.refs_4_ = bf16[4,48,768]{2,1,0:T(8,128)(2,1)S(1)} collective-permute-done((bf16[4,48,768]{2,1,0:T(8,128)(2,1)}, bf16[4,48,768]{2,1,0:T(8,128)(2,1)S(1)}, u32[]{:S(2)}, u32[]{:S(2)}) %collective-permute-start.6) | collective-permute-done | bytes 294944 | tf_op jit(solution)/shard_map/ppermute | solution.py:38
  89.5 0.7 copy-done.15
  90.2 2.6 %collective-permute-done.5.refs_3_ = bf16[4,48,768]{2,1,0:T(8,128)(2,1)} collective-permute-done((bf16[4,48,768]{2,1,0:T(8,128)(2,1)}, bf16[4,48,768]{2,1,0:T(8,128)(2,1)}, u32[]{:S(2)}, u32[]{:S(2)}) %collective-permute-start.5) | collective-permute-done | bytes 294944 | tf_op jit(solution)/shard_map/ppermute | solution.py:38
  92.9 4.6 %all-to-all-done.4.refs_1_ = bf16[8,128,768]{2,1,0:T(8,128)(2,1)S(1)} async-done(((bf16[8,128,768]{2,1,0:T(8,128)(2,1)}), bf16[8,128,768]{2,1,0:T(8,128)(2,1)S(1)}, u32[]{:S(2)}, u32[]{:S(2)}) %all-to-all-start.4) | async-done | bytes 1572896 | tf_op jit(solution)/shard_map/all_to_all | solution.py:29
  97.4 3.8 %shard_map.162 = bf16[8,16,3456]{2,1,0:T(8,128)(2,1)S(1)} custom-call(s32[20]{0:T(128)S(1)} %concatenate.3.refs_1_.refs_0_, bf16[8,128,768]{2,1,0:T(8,128)(2,1)S(1)} %all-to-all-done.4.refs_1_, bf16[4,48,768]{2,1,0:T(8,128)(2,1)} %get-tuple-element.28.refs_2_, bf16[4,48,768]{2,1,0:T(8,128)(2,1)} %collective-permute-done.5.refs_3_, ...), custom_call_target="tpu_custom_call" | custom-call | flops 1 | bytes 4000000 | tf_op jit(solution)/shard_map/pallas_call | solution.py:113
  101.2 13.7 %all_to_all.41.refs_0_ = bf16[8,16,3456]{2,1,0:T(8,128)(2,1)S(1)} all-to-all(bf16[8,16,3456]{2,1,0:T(8,128)(2,1)S(1)} %shard_map.162), channel_id=1, replica_groups=mesh['dp'=16,'section'=2,'tensor'=8] {'tensor'}, dimensions={0} | all-to-all | bytes 1769472 | tf_op jit(solution)/shard_map/all_to_all | solution.py:29
  114.9 0.0 copy-done.11
  114.9 1.1 shard_map.163
  116.0 16.9 %all_to_all.42.refs_1_ = bf16[16,16,768]{2,1,0:T(8,128)(2,1)S(1)} all-to-all(bf16[16,16,768]{2,1,0:T(8,128)(2,1)S(1)} %get-tuple-element.34), channel_id=1, replica_groups=mesh['dp'=16,'section'=2,'tensor'=8] {'dp'}, dimensions={0} | all-to-all | bytes 786432 | tf_op jit(solution)/shard_map/all_to_all | solution.py:29
  132.9 0.2 shard_map.164
  133.1 10.3 %all_to_all.43.refs_1_ = bf16[8,16,1536]{2,1,0:T(8,128)(2,1)S(1)} all-to-all(bf16[8,16,1536]{2,1,0:T(8,128)(2,1)S(1)} %shard_map.164), channel_id=1, replica_groups=mesh['dp'=16,'section'=2,'tensor'=8] {'tensor'}, dimensions={0} | all-to-all | bytes 786432 | tf_op jit(solution)/shard_map/all_to_all | solution.py:29
  143.3 0.7 shard_map.165.refs_0_
  144.0 6.2 %collective-permute-start.8 = (bf16[16,768]{1,0:T(8,128)(2,1)S(1)}, bf16[16,768]{1,0:T(8,128)(2,1)S(1)}, u32[]{:S(2)}, u32[]{:S(2)}) collective-permute-start(bf16[16,768]{1,0:T(8,128)(2,1)S(1)} %shard_map.165.refs_0_), channel_id=1, source_target_pairs={{0,8},{8,0},{1,9},{9,1},{2,10},{10,2},{3,11},{11,3},{4,12},{12,4},... | collective-permute-start | bytes 73736 | tf_op jit(solution)/shard_map/ppermute | solution.py:25
  150.2 0.0 copy-done.4
  150.2 1.8 %shard_map.166 = (bf16[128,768]{1,0:T(8,128)(2,1)}, bf16[128,768]{1,0:T(8,128)(2,1)}, bf16[128,768]{1,0:T(8,128)(2,1)}) custom-call(bf16[16,768]{1,0:T(8,128)(2,1)S(1)} %shard_map.165.refs_0_, bf16[8,16,1536]{2,1,0:T(8,128)(2,1)S(1)} %all_to_all.43.refs_1_, bf16[768,768]{1,0:T(8,128)(2,1)S(1)} %bitcast.34, bf16[128,768]{1,0:T(8,128)(2,1)S(1)} %bitcast.39, ...), custom_call_target="tpu_custom_call" | custom-call | flops 1 | bytes 4000000 | tf_op jit(solution)/shard_map/pallas_call | solution.py:113
  152.0 0.0 collective-permute-done.8
  152.0 0.6 copy.20
  (24 shorter events, 0.1 us)
Async XLA Ops:
  0.6 1.1 copy-start
  4.6 14.2 %copy-start.1 = (bf16[1,1,128,6144]{3,2,1,0:T(8,128)(2,1)S(1)}, bf16[1,1,128,6144]{3,2,1,0:T(8,128)(2,1)}, u32[]{:S(2)}) copy-start(bf16[1,1,128,6144]{3,2,1,0:T(8,128)(2,1)} %param.12) | copy-start | bytes 4718596
  4.6 14.2 %copy-start.12 = (f32[1,6144]{1,0:T(1,128)S(1)}, f32[1,6144]{1,0:T(1,128)}, u32[]{:S(2)}) copy-start(f32[1,6144]{1,0:T(1,128)} %refs_4_.1) | copy-start | bytes 73732
  4.6 14.2 %copy-start.13 = (f32[1,6144]{1,0:T(1,128)S(1)}, f32[1,6144]{1,0:T(1,128)}, u32[]{:S(2)}) copy-start(f32[1,6144]{1,0:T(1,128)} %refs_5_.1) | copy-start | bytes 73732
  4.6 19.9 %all-to-all-start = ((bf16[4,192,768]{2,1,0:T(8,128)(2,1)}), bf16[4,192,768]{2,1,0:T(8,128)(2,1)S(1)}, u32[]{:S(2)}, u32[]{:S(2)}) async-start(bf16[4,192,768]{2,1,0:T(8,128)(2,1)} %bitcast.10), calls=%async_computation | async-start | bytes 2359296 | tf_op jit(solution)/shard_map/all_to_all | solution.py:29
  9.7 8.2 %collective-permute-start = (s32[1]{0:T(128)}, s32[1]{0:T(128)}, u32[]{:S(2)}, u32[]{:S(2)}) collective-permute-start(s32[1]{0:T(128)} %bitcast), channel_id=1, source_target_pairs={{0,8},{8,0},{1,9},{9,1},{2,10},{10,2},{3,11},{11,3},{4,12},{12,4},... | collective-permute-start | bytes 20 | tf_op jit(solution)/shard_map/ppermute | solution.py:25
  12.2 10.3 %collective-permute-start.1 = (bf16[48,768]{1,0:T(8,128)(2,1)}, bf16[48,768]{1,0:T(8,128)(2,1)}, u32[]{:S(2)}, u32[]{:S(2)}) collective-permute-start(bf16[48,768]{1,0:T(8,128)(2,1)} %dynamic-slice_bitcast_fusion), channel_id=1, source_target_pairs={{5,0},{18,1},{38,2},{48,3},{71,4},{84,5},{102,6},{117,7},{3,16},{2... | collective-permute-start | bytes 221192 | tf_op jit(solution)/shard_map/ppermute | solution.py:66
  18.8 1.4 copy-start.2
  22.5 11.9 %copy-start.16 = (s32[1,1,4,4]{3,2,1,0:T(4,128)S(1)}, s32[1,1,4,4]{3,2,1,0:T(4,128)}, u32[]{:S(2)}) copy-start(s32[1,1,4,4]{3,2,1,0:T(4,128)} %param.16) | copy-start | bytes 196
  22.5 12.3 %copy-start.5 = (bf16[1,1,128,768]{3,2,1,0:T(8,128)(2,1)S(1)}, bf16[1,1,128,768]{3,2,1,0:T(8,128)(2,1)}, u32[]{:S(2)}) copy-start(bf16[1,1,128,768]{3,2,1,0:T(8,128)(2,1)} %param.13) | copy-start | bytes 589828
  22.5 12.3 %copy-start.6 = (bf16[1,1,128,768]{3,2,1,0:T(8,128)(2,1)S(1)}, bf16[1,1,128,768]{3,2,1,0:T(8,128)(2,1)}, u32[]{:S(2)}) copy-start(bf16[1,1,128,768]{3,2,1,0:T(8,128)(2,1)} %param.14) | copy-start | bytes 589828
  22.5 12.3 %copy-start.8 = (bf16[1,1,128,768]{3,2,1,0:T(8,128)(2,1)S(1)}, bf16[1,1,128,768]{3,2,1,0:T(8,128)(2,1)}, u32[]{:S(2)}) copy-start(bf16[1,1,128,768]{3,2,1,0:T(8,128)(2,1)} %param.15) | copy-start | bytes 589828
  25.4 17.3 %all-to-all-start.1 = ((bf16[4,48,768]{2,1,0:T(8,128)(2,1)}), bf16[4,48,768]{2,1,0:T(8,128)(2,1)S(1)}, u32[]{:S(2)}, u32[]{:S(2)}) async-start(bf16[4,48,768]{2,1,0:T(8,128)(2,1)} %bitcast.16), calls=%async_computation.1 | async-start | bytes 589824 | tf_op jit(solution)/shard_map/all_to_all | solution.py:29
  36.9 20.7 %copy-start.3 = (f32[12,128,128]{2,1,0:T(8,128)}, f32[12,128,128]{2,1,0:T(8,128)S(1)}, u32[]{:S(2)}) copy-start(f32[12,128,128]{2,1,0:T(8,128)S(1)} %get-tuple-element.37.refs_6_) | copy-start | bytes 2359300
  57.6 18.3 %all-to-all-start.3 = ((bf16[4,192,768]{2,1,0:T(8,128)(2,1)}), bf16[4,192,768]{2,1,0:T(8,128)(2,1)S(1)}, u32[]{:S(2)}, u32[]{:S(2)}) async-start(bf16[4,192,768]{2,1,0:T(8,128)(2,1)} %get-tuple-element.25), calls=%async_computation.3 | async-start | bytes 2359296 | tf_op jit(solution)/shard_map/all_to_all | solution.py:29
  62.8 4.5 %collective-permute-start.4 = (bf16[48,768]{1,0:T(8,128)(2,1)S(1)}, bf16[48,768]{1,0:T(8,128)(2,1)S(1)}, u32[]{:S(2)}, u32[]{:S(2)}) collective-permute-start(bf16[48,768]{1,0:T(8,128)(2,1)S(1)} %get-tuple-element.26.refs_1_), channel_id=1, source_target_pairs={{0,192},{16,208},{32,224},{48,240},{64,0},{80,16},{96,32},{112,48}... | collective-permute-start | bytes 221192 | tf_op jit(solution)/shard_map/ppermute | solution.py:38
  63.1 8.1 %collective-permute-start.3 = (bf16[48,768]{1,0:T(8,128)(2,1)S(1)}, bf16[48,768]{1,0:T(8,128)(2,1)S(1)}, u32[]{:S(2)}, u32[]{:S(2)}) collective-permute-start(bf16[48,768]{1,0:T(8,128)(2,1)S(1)} %get-tuple-element.26.refs_1_), channel_id=1, source_target_pairs={{0,128},{16,144},{32,160},{48,176},{64,192},{80,208},{96,224},{112... | collective-permute-start | bytes 221192 | tf_op jit(solution)/shard_map/ppermute | solution.py:38
  65.5 6.8 %collective-permute-start.2 = (bf16[48,768]{1,0:T(8,128)(2,1)S(1)}, bf16[48,768]{1,0:T(8,128)(2,1)S(1)}, u32[]{:S(2)}, u32[]{:S(2)}) collective-permute-start(bf16[48,768]{1,0:T(8,128)(2,1)S(1)} %get-tuple-element.26.refs_1_), channel_id=1, source_target_pairs={{0,64},{16,80},{32,96},{48,112},{64,128},{80,144},{96,160},{112,17... | collective-permute-start | bytes 221192 | tf_op jit(solution)/shard_map/ppermute | solution.py:38
  77.5 20.0 %all-to-all-start.4 = ((bf16[8,128,768]{2,1,0:T(8,128)(2,1)}), bf16[8,128,768]{2,1,0:T(8,128)(2,1)S(1)}, u32[]{:S(2)}, u32[]{:S(2)}) async-start(bf16[8,128,768]{2,1,0:T(8,128)(2,1)} %get-tuple-element.27), calls=%async_computation.4 | async-start | bytes 3145728 | tf_op jit(solution)/shard_map/all_to_all | solution.py:29
  81.4 5.8 %collective-permute-start.7 = (bf16[4,48,768]{2,1,0:T(8,128)(2,1)}, bf16[4,48,768]{2,1,0:T(8,128)(2,1)S(1)}, u32[]{:S(2)}, u32[]{:S(2)}) collective-permute-start(bf16[4,48,768]{2,1,0:T(8,128)(2,1)} %get-tuple-element.28.refs_2_), channel_id=1, source_target_pairs={{0,48},{16,0},{32,16},{48,32},{64,112},{80,64},{96,80},{112,96},{1... | collective-permute-start | bytes 884744 | tf_op jit(solution)/shard_map/ppermute | solution.py:38
  82.1 7.4 %collective-permute-start.6 = (bf16[4,48,768]{2,1,0:T(8,128)(2,1)}, bf16[4,48,768]{2,1,0:T(8,128)(2,1)S(1)}, u32[]{:S(2)}, u32[]{:S(2)}) collective-permute-start(bf16[4,48,768]{2,1,0:T(8,128)(2,1)} %get-tuple-element.28.refs_2_), channel_id=1, source_target_pairs={{0,32},{16,48},{32,0},{48,16},{64,96},{80,112},{96,64},{112,80},{1... | collective-permute-start | bytes 884744 | tf_op jit(solution)/shard_map/ppermute | solution.py:38
  83.2 9.6 %collective-permute-start.5 = (bf16[4,48,768]{2,1,0:T(8,128)(2,1)}, bf16[4,48,768]{2,1,0:T(8,128)(2,1)}, u32[]{:S(2)}, u32[]{:S(2)}) collective-permute-start(bf16[4,48,768]{2,1,0:T(8,128)(2,1)} %get-tuple-element.28.refs_2_), channel_id=1, source_target_pairs={{0,16},{16,32},{32,48},{48,0},{64,80},{80,96},{96,112},{112,64},{1... | collective-permute-start | bytes 884744 | tf_op jit(solution)/shard_map/ppermute | solution.py:38
  87.2 2.3 %copy-start.14 = (bf16[4,48,768]{2,1,0:T(8,128)(2,1)}, bf16[4,48,768]{2,1,0:T(8,128)(2,1)S(1)}, u32[]{:S(2)}) copy-start(bf16[4,48,768]{2,1,0:T(8,128)(2,1)S(1)} %collective-permute-done.7.refs_5_) | copy-start | bytes 884740
  89.5 0.7 copy-start.15
  101.2 13.7 %copy-start.10 = (f32[16,6144]{1,0:T(8,128)S(1)}, f32[16,6144]{1,0:T(8,128)}, u32[]{:S(2)}) copy-start(f32[16,6144]{1,0:T(8,128)} %get-tuple-element.31.refs_1_) | copy-start | bytes 1179652
  101.2 13.7 %copy-start.11 = (f32[16,6144]{1,0:T(8,128)S(1)}, f32[16,6144]{1,0:T(8,128)}, u32[]{:S(2)}) copy-start(f32[16,6144]{1,0:T(8,128)} %get-tuple-element.32.refs_2_) | copy-start | bytes 1179652
  116.0 34.3 %copy-start.4 = (f32[12,128,128]{2,1,0:T(8,128)S(1)}, f32[12,128,128]{2,1,0:T(8,128)}, u32[]{:S(2)}) copy-start(f32[12,128,128]{2,1,0:T(8,128)} %copy-done.3) | copy-start | bytes 2359300
  116.0 34.3 %copy-start.7 = (bf16[1,1,128,768]{3,2,1,0:T(8,128)(2,1)S(1)}, bf16[1,1,128,768]{3,2,1,0:T(8,128)(2,1)}, u32[]{:S(2)}) copy-start(bf16[1,1,128,768]{3,2,1,0:T(8,128)(2,1)} %param.14) | copy-start | bytes 589828
  116.0 34.3 %copy-start.9 = (bf16[1,1,128,768]{3,2,1,0:T(8,128)(2,1)S(1)}, bf16[1,1,128,768]{3,2,1,0:T(8,128)(2,1)}, u32[]{:S(2)}) copy-start(bf16[1,1,128,768]{3,2,1,0:T(8,128)(2,1)} %param.15) | copy-start | bytes 589828
  144.0 8.0 %collective-permute-start.8 = (bf16[16,768]{1,0:T(8,128)(2,1)S(1)}, bf16[16,768]{1,0:T(8,128)(2,1)S(1)}, u32[]{:S(2)}, u32[]{:S(2)}) collective-permute-start(bf16[16,768]{1,0:T(8,128)(2,1)S(1)} %shard_map.165.refs_0_), channel_id=1, source_target_pairs={{0,8},{8,0},{1,9},{9,1},{2,10},{10,2},{3,11},{11,3},{4,12},{12,4},... | collective-permute-start | bytes 73736 | tf_op jit(solution)/shard_map/ppermute | solution.py:25

commit v9 on v8

--- a/solution.py
+++ b/solution.py
@@ -222,18 +222,23 @@
     decoded = times_transposed(code, book)
     put(3 * width, decoded)
     copies[N_LOW].wait()
-    put(2 * width, times(here_ref[0], book))
     hidden = here_ref[1].astype(jnp.float32) + here_ref[2].astype(jnp.float32) + decoded
-    put(0, times(hidden.astype(jnp.bfloat16), book))
-    put(width, times((hidden * gain_ref[...]).astype(jnp.bfloat16), book))
     row = lax.broadcasted_iota(jnp.int32, (EXTRA_ROWS, features), 0)
     rest = jnp.where(row == 0, 1.0, jnp.where(row == 1, gain_ref[...], 0.0))
     rest = jnp.where(row == 2, bias_ref[...], rest)
-    sums = jnp.zeros((EXTRA_ROWS, width), jnp.float32)
+    left = [hidden.astype(jnp.bfloat16), (hidden * gain_ref[...]).astype(jnp.bfloat16), here_ref[0]]
     for _ in range(3):
         top = rest.astype(jnp.bfloat16)
         rest = rest - top.astype(jnp.float32)
-        sums += times(top, book)
+        left.append(top)
+    length = count * rows
+    products = times(jnp.concatenate(left, axis=0), book)
+    for place in range(3):
+        put(place * width, products[place * length : (place + 1) * length])
+    sums = products[3 * length : 3 * length + EXTRA_ROWS]
+    for place in (1, 2):
+        start = 3 * length + place * EXTRA_ROWS
+        sums += products[start : start + EXTRA_ROWS]
     upper = sums.astype(jnp.bfloat16).astype(jnp.float32)
     lower = pltpu.roll(sums - upper, 3, 0)
     row = lax.broadcasted_iota(jnp.int32, sums.shape, 0)

time: 153 us -> 153 us (level)
  no operation moved by 1% of the time
where the time goes in v9:
time: 153 us; the launch traced here: 152 us
  blocking collectives  53.8 us (35%)
  starting transfers between devices  41.1 us (27%)
  waiting for transfers between devices  30.8 us (20%)
  Pallas kernels  16.6 us (11%)
  local copies, waits for them, and re-layouts  6.36 us (4%)
  matrix products  2.88 us (2%)
    all_to_all x4, blocking collectives, exchanged(): return lax.all_to_all(value, axis, 0, 0, axis_index_groups=groups)  53.8 us
    all_to_all x4, starting transfers between devices, exchanged(): return lax.all_to_all(value, axis, 0, 0, axis_index_groups=groups)  23.2 us
    pallas_call x12, Pallas kernels, call(): pl.pallas_call(body, out_shape=[pltpu.HBM(shape, dtype) if place in far_o...  16.6 us
    ppermute x6, waiting for transfers between devices, turned(): return lax.ppermute(value, 'dp', pairs)  15.4 us
    all_to_all x4, waiting for transfers between devices, exchanged(): return lax.all_to_all(value, axis, 0, 0, axis_index_groups=groups)  15.4 us
    ppermute x2, starting transfers between devices, swapped_2(): lax.ppermute(value, axis, [(i, i ^ 1 << distance) for i in range(lax.axis...  8.01 us
    ppermute x1, starting transfers between devices, transposed_owner(): return lax.ppermute(value, ('dp', 'tensor'), pairs)  5.06 us
    ppermute x6, starting transfers between devices, turned(): return lax.ppermute(value, 'dp', pairs)  4.8 us
  transfers between devices with their start and end apart: 13, of which 10 were waited for; matrix products, arithmetic and copies ran while one was open for 2% of the time, Pallas kernels for 4%

profile of v9, /device:TPU:1, one launch (start us, length us, event | category | flops | bytes accessed | tf_op | source)
XLA Modules:
  0.0 152.3 jit_solution(14063508250198051165)
XLA Ops:
  0.6 0.0 copy-start
  0.6 1.1 copy-done
  1.7 2.9 %convolution_convert_fusion.refs_0_ = bf16[768,768]{1,0:T(8,128)(2,1)} fusion(bf16[1,384,768]{2,1,0:T(8,128)(2,1)S(1)} %copy-done, bf16[1,768,384]{2,1,0:T(8,128)(2,1)} %param.17), kind=kOutput, calls=%fused_computation | convolution fusion | flops 453574656 | bytes 2359296 | tf_op jit(solution)/shard_map/dot_general | solution.py:85
  4.6 5.1 %all-to-all-start = ((bf16[4,192,768]{2,1,0:T(8,128)(2,1)}), bf16[4,192,768]{2,1,0:T(8,128)(2,1)S(1)}, u32[]{:S(2)}, u32[]{:S(2)}) async-start(bf16[4,192,768]{2,1,0:T(8,128)(2,1)} %bitcast.10), calls=%async_computation | async-start | bytes 2359296 | tf_op jit(solution)/shard_map/all_to_all | solution.py:29
  9.7 1.9 %collective-permute-start = (s32[1]{0:T(128)}, s32[1]{0:T(128)}, u32[]{:S(2)}, u32[]{:S(2)}) collective-permute-start(s32[1]{0:T(128)} %bitcast), channel_id=1, source_target_pairs={{0,8},{8,0},{1,9},{9,1},{2,10},{10,2},{3,11},{11,3},{4,12},{12,4},... | collective-permute-start | bytes 20 | tf_op jit(solution)/shard_map/ppermute | solution.py:25
  11.6 0.6 dynamic-slice_bitcast_fusion
  12.2 5.1 %collective-permute-start.1 = (bf16[48,768]{1,0:T(8,128)(2,1)}, bf16[48,768]{1,0:T(8,128)(2,1)}, u32[]{:S(2)}, u32[]{:S(2)}) collective-permute-start(bf16[48,768]{1,0:T(8,128)(2,1)} %dynamic-slice_bitcast_fusion), channel_id=1, source_target_pairs={{5,0},{18,1},{38,2},{48,3},{71,4},{84,5},{102,6},{117,7},{3,16},{2... | collective-permute-start | bytes 221192 | tf_op jit(solution)/shard_map/ppermute | solution.py:66
  17.3 0.7 dynamic-slice_bitcast_fusion.1
  18.0 0.0 collective-permute-done.refs_0_
  18.0 0.8 concatenate.3.refs_1_.refs_0_
  18.7 0.0 copy-done.1
  18.8 0.0 copy-done.12
  18.8 0.0 copy-done.13
  18.8 0.0 copy-start.2
  18.8 1.4 copy-done.2
  20.2 2.3 %shard_map.155 = (bf16[3,128,768]{2,1,0:T(8,128)(2,1)}, f32[1,768]{1,0:T(1,128)S(1)}, f32[1,768]{1,0:T(1,128)S(1)}, f32[16,6144]{1,0:T(8,128)}, f32[16,6144]{1,0:T(8,128)}) custom-call(bf16[768,768]{1,0:T(8,128)(2,1)} %convolution_convert_fusion.refs_0_, s32[20]{0:T(128)S(1)} %concatenate.3.refs_1_.refs_0_, bf16[128,6144]{1,0:T(8,128)(2,1)S(1)} %bitcast.35, ...), custom_call_target="tpu_custom_call" | custom-call | flops 1 | bytes 4000000 | tf_op jit(solution)/shard_map/pallas_call | solution.py:113
  22.5 0.0 collective-permute-done.1.refs_0_.refs_1_
  22.5 2.0 %all-to-all-done.refs_2_ = bf16[4,192,768]{2,1,0:T(8,128)(2,1)S(1)} async-done(((bf16[4,192,768]{2,1,0:T(8,128)(2,1)}), bf16[4,192,768]{2,1,0:T(8,128)(2,1)S(1)}, u32[]{:S(2)}, u32[]{:S(2)}) %all-to-all-start) | async-done | bytes 1179680 | tf_op jit(solution)/shard_map/all_to_all | solution.py:29
  24.5 0.9 shard_map.156.refs_0_
  25.4 9.0 %all-to-all-start.1 = ((bf16[4,48,768]{2,1,0:T(8,128)(2,1)}), bf16[4,48,768]{2,1,0:T(8,128)(2,1)S(1)}, u32[]{:S(2)}, u32[]{:S(2)}) async-start(bf16[4,48,768]{2,1,0:T(8,128)(2,1)} %bitcast.16), calls=%async_computation.1 | async-start | bytes 589824 | tf_op jit(solution)/shard_map/all_to_all | solution.py:29
  34.4 0.0 copy-done.16
  34.4 0.1 copy.17
  34.5 0.1 broadcast_in_dim.21
  34.6 0.1 eq.22
  34.7 0.1 copy.18
  34.8 0.0 copy-done.5
  34.8 2.1 %shard_map.157 = (bf16[128,768]{1,0:T(8,128)(2,1)S(1)}, f32[12,128,128]{2,1,0:T(8,128)S(1)}) custom-call(bf16[192,768]{1,0:T(8,128)(2,1)} %shard_map.156.refs_0_, bf16[128,768]{1,0:T(8,128)(2,1)S(1)} %bitcast.38, bf16[128,768]{1,0:T(8,128)(2,1)S(1)} %bitcast.40, bf16[128,768]{1,0:T(8,128)(2,1)S(1)} %bitcast.42, f32[128,128]{1,0:T(8,128)S(1)} %fusion.3.refs_4_), custom_call_target="tpu_custom_call" | custom-call | flops 1 | bytes 4000000 | tf_op jit(solution)/shard_map/pallas_call | solution.py:113
  36.9 5.8 %all-to-all-done.1.refs_1_ = bf16[4,48,768]{2,1,0:T(8,128)(2,1)S(1)} async-done(((bf16[4,48,768]{2,1,0:T(8,128)(2,1)}), bf16[4,48,768]{2,1,0:T(8,128)(2,1)S(1)}, u32[]{:S(2)}, u32[]{:S(2)}) %all-to-all-start.1) | async-done | bytes 294944 | tf_op jit(solution)/shard_map/all_to_all | solution.py:29
  42.7 12.9 %all_to_all.40 = bf16[4,48,768]{2,1,0:T(8,128)(2,1)S(1)} all-to-all(bf16[4,48,768]{2,1,0:T(8,128)(2,1)S(1)} %shard_map.158), channel_id=1, replica_groups={{0,64,128,192},{16,80,144,208},{32,96,160,224},{48,112,176,240},{1,65,1..., dimensions={0} | all-to-all | bytes 589824 | tf_op jit(solution)/shard_map/all_to_all | solution.py:29
  55.6 2.0 %shard_map.159 = (bf16[4,192,768]{2,1,0:T(8,128)(2,1)}, bf16[48,768]{1,0:T(8,128)(2,1)S(1)}) custom-call(bf16[192,768]{1,0:T(8,128)(2,1)S(1)} %bitcast.37, bf16[48,768]{1,0:T(8,128)(2,1)} %collective-permute-done.1.refs_0_.refs_1_), custom_call_target="tpu_custom_call" | custom-call | flops 1 | bytes 4000000 | tf_op jit(solution)/shard_map/pallas_call | solution.py:113
  57.6 5.1 %all-to-all-start.3 = ((bf16[4,192,768]{2,1,0:T(8,128)(2,1)}), bf16[4,192,768]{2,1,0:T(8,128)(2,1)S(1)}, u32[]{:S(2)}, u32[]{:S(2)}) async-start(bf16[4,192,768]{2,1,0:T(8,128)(2,1)} %get-tuple-element.25), calls=%async_computation.3 | async-start | bytes 2359296 | tf_op jit(solution)/shard_map/all_to_all | solution.py:29
  62.8 0.3 collective-permute-start.4
  63.1 2.4 %collective-permute-start.3 = (bf16[48,768]{1,0:T(8,128)(2,1)S(1)}, bf16[48,768]{1,0:T(8,128)(2,1)S(1)}, u32[]{:S(2)}, u32[]{:S(2)}) collective-permute-start(bf16[48,768]{1,0:T(8,128)(2,1)S(1)} %get-tuple-element.26.refs_1_), channel_id=1, source_target_pairs={{0,128},{16,144},{32,160},{48,176},{64,192},{80,208},{96,224},{112... | collective-permute-start | bytes 221192 | tf_op jit(solution)/shard_map/ppermute | solution.py:38
  65.5 0.2 collective-permute-start.2
  65.7 1.5 %collective-permute-done.4.refs_4_ = bf16[48,768]{1,0:T(8,128)(2,1)S(1)} collective-permute-done((bf16[48,768]{1,0:T(8,128)(2,1)S(1)}, bf16[48,768]{1,0:T(8,128)(2,1)S(1)}, u32[]{:S(2)}, u32[]{:S(2)}) %collective-permute-start.4) | collective-permute-done | bytes 73760 | tf_op jit(solution)/shard_map/ppermute | solution.py:38
  67.3 3.9 %collective-permute-done.3.refs_3_ = bf16[48,768]{1,0:T(8,128)(2,1)S(1)} collective-permute-done((bf16[48,768]{1,0:T(8,128)(2,1)S(1)}, bf16[48,768]{1,0:T(8,128)(2,1)S(1)}, u32[]{:S(2)}, u32[]{:S(2)}) %collective-permute-start.3) | collective-permute-done | bytes 73760 | tf_op jit(solution)/shard_map/ppermute | solution.py:38
  71.2 1.1 collective-permute-done.2.refs_2_
  72.3 0.6 shard_map.160.refs_2_
  72.9 3.0 %all-to-all-done.3 = bf16[4,192,768]{2,1,0:T(8,128)(2,1)S(1)} async-done(((bf16[4,192,768]{2,1,0:T(8,128)(2,1)}), bf16[4,192,768]{2,1,0:T(8,128)(2,1)S(1)}, u32[]{:S(2)}, u32[]{:S(2)}) %all-to-all-start.3) | async-done | bytes 1179680 | tf_op jit(solution)/shard_map/all_to_all | solution.py:29
  75.9 1.6 %shard_map.161 = (bf16[8,128,768]{2,1,0:T(8,128)(2,1)}, bf16[4,48,768]{2,1,0:T(8,128)(2,1)}) custom-call(bf16[128,768]{1,0:T(8,128)(2,1)S(1)} %get-tuple-element.24.refs_0_, bf16[768,768]{1,0:T(8,128)(2,1)S(1)} %bitcast.33, bf16[4,48,768]{2,1,0:T(8,128)(2,1)S(1)} %shard_map.160.refs_2_), custom_call_target="tpu_custom_call" | custom-call | flops 1 | bytes 4000000 | tf_op jit(solution)/shard_map/pallas_call | solution.py:113
  77.5 4.0 %all-to-all-start.4 = ((bf16[8,128,768]{2,1,0:T(8,128)(2,1)}), bf16[8,128,768]{2,1,0:T(8,128)(2,1)S(1)}, u32[]{:S(2)}, u32[]{:S(2)}) async-start(bf16[8,128,768]{2,1,0:T(8,128)(2,1)} %get-tuple-element.27), calls=%async_computation.4 | async-start | bytes 3145728 | tf_op jit(solution)/shard_map/all_to_all | solution.py:29
  81.4 0.7 collective-permute-start.7
  82.1 1.1 collective-permute-start.6
  83.2 0.0 collective-permute-start.5
  83.3 4.0 %collective-permute-done.7.refs_5_ = bf16[4,48,768]{2,1,0:T(8,128)(2,1)S(1)} collective-permute-done((bf16[4,48,768]{2,1,0:T(8,128)(2,1)}, bf16[4,48,768]{2,1,0:T(8,128)(2,1)S(1)}, u32[]{:S(2)}, u32[]{:S(2)}) %collective-permute-start.7) | collective-permute-done | bytes 294944 | tf_op jit(solution)/shard_map/ppermute | solution.py:38
  87.2 2.3 %collective-permute-done.6.refs_4_ = bf16[4,48,768]{2,1,0:T(8,128)(2,1)S(1)} collective-permute-done((bf16[4,48,768]{2,1,0:T(8,128)(2,1)}, bf16[4,48,768]{2,1,0:T(8,128)(2,1)S(1)}, u32[]{:S(2)}, u32[]{:S(2)}) %collective-permute-start.6) | collective-permute-done | bytes 294944 | tf_op jit(solution)/shard_map/ppermute | solution.py:38
  89.5 0.7 copy-done.15
  90.2 2.6 %collective-permute-done.5.refs_3_ = bf16[4,48,768]{2,1,0:T(8,128)(2,1)} collective-permute-done((bf16[4,48,768]{2,1,0:T(8,128)(2,1)}, bf16[4,48,768]{2,1,0:T(8,128)(2,1)}, u32[]{:S(2)}, u32[]{:S(2)}) %collective-permute-start.5) | collective-permute-done | bytes 294944 | tf_op jit(solution)/shard_map/ppermute | solution.py:38
  92.9 4.6 %all-to-all-done.4.refs_1_ = bf16[8,128,768]{2,1,0:T(8,128)(2,1)S(1)} async-done(((bf16[8,128,768]{2,1,0:T(8,128)(2,1)}), bf16[8,128,768]{2,1,0:T(8,128)(2,1)S(1)}, u32[]{:S(2)}, u32[]{:S(2)}) %all-to-all-start.4) | async-done | bytes 1572896 | tf_op jit(solution)/shard_map/all_to_all | solution.py:29
  97.4 3.4 %shard_map.162 = bf16[8,16,3456]{2,1,0:T(8,128)(2,1)S(1)} custom-call(s32[20]{0:T(128)S(1)} %concatenate.3.refs_1_.refs_0_, bf16[8,128,768]{2,1,0:T(8,128)(2,1)S(1)} %all-to-all-done.4.refs_1_, bf16[4,48,768]{2,1,0:T(8,128)(2,1)} %get-tuple-element.28.refs_2_, bf16[4,48,768]{2,1,0:T(8,128)(2,1)} %collective-permute-done.5.refs_3_, ...), custom_call_target="tpu_custom_call" | custom-call | flops 1 | bytes 4000000 | tf_op jit(solution)/shard_map/pallas_call | solution.py:113
  100.8 0.0 copy-start.10
  100.9 0.0 copy-start.11
  100.9 13.7 %all_to_all.41.refs_0_ = bf16[8,16,3456]{2,1,0:T(8,128)(2,1)S(1)} all-to-all(bf16[8,16,3456]{2,1,0:T(8,128)(2,1)S(1)} %shard_map.162), channel_id=1, replica_groups=mesh['dp'=16,'section'=2,'tensor'=8] {'tensor'}, dimensions={0} | all-to-all | bytes 1769472 | tf_op jit(solution)/shard_map/all_to_all | solution.py:29
  114.5 0.0 copy-done.10
  114.6 1.1 shard_map.163
  115.6 16.9 %all_to_all.42.refs_1_ = bf16[16,16,768]{2,1,0:T(8,128)(2,1)S(1)} all-to-all(bf16[16,16,768]{2,1,0:T(8,128)(2,1)S(1)} %get-tuple-element.34), channel_id=1, replica_groups=mesh['dp'=16,'section'=2,'tensor'=8] {'dp'}, dimensions={0} | all-to-all | bytes 786432 | tf_op jit(solution)/shard_map/all_to_all | solution.py:29
  132.5 0.2 shard_map.164
  132.7 10.3 %all_to_all.43.refs_1_ = bf16[8,16,1536]{2,1,0:T(8,128)(2,1)S(1)} all-to-all(bf16[8,16,1536]{2,1,0:T(8,128)(2,1)S(1)} %shard_map.164), channel_id=1, replica_groups=mesh['dp'=16,'section'=2,'tensor'=8] {'tensor'}, dimensions={0} | all-to-all | bytes 786432 | tf_op jit(solution)/shard_map/all_to_all | solution.py:29
  143.0 0.7 shard_map.165.refs_0_
  143.7 6.2 %collective-permute-start.8 = (bf16[16,768]{1,0:T(8,128)(2,1)S(1)}, bf16[16,768]{1,0:T(8,128)(2,1)S(1)}, u32[]{:S(2)}, u32[]{:S(2)}) collective-permute-start(bf16[16,768]{1,0:T(8,128)(2,1)S(1)} %shard_map.165.refs_0_), channel_id=1, source_target_pairs={{0,8},{8,0},{1,9},{9,1},{2,10},{10,2},{3,11},{11,3},{4,12},{12,4},... | collective-permute-start | bytes 73736 | tf_op jit(solution)/shard_map/ppermute | solution.py:25
  149.9 0.0 copy-done.7
  149.9 1.8 %shard_map.166 = (bf16[128,768]{1,0:T(8,128)(2,1)}, bf16[128,768]{1,0:T(8,128)(2,1)}, bf16[128,768]{1,0:T(8,128)(2,1)}) custom-call(bf16[16,768]{1,0:T(8,128)(2,1)S(1)} %shard_map.165.refs_0_, bf16[8,16,1536]{2,1,0:T(8,128)(2,1)S(1)} %all_to_all.43.refs_1_, bf16[768,768]{1,0:T(8,128)(2,1)S(1)} %bitcast.34, bf16[128,768]{1,0:T(8,128)(2,1)S(1)} %bitcast.39, ...), custom_call_target="tpu_custom_call" | custom-call | flops 1 | bytes 4000000 | tf_op jit(solution)/shard_map/pallas_call | solution.py:113
  151.7 0.0 collective-permute-done.8
  151.7 0.6 copy.20
  (24 shorter events, 0.1 us)
Async XLA Ops:
  0.6 1.1 copy-start
  4.6 14.2 %copy-start.1 = (bf16[1,1,128,6144]{3,2,1,0:T(8,128)(2,1)S(1)}, bf16[1,1,128,6144]{3,2,1,0:T(8,128)(2,1)}, u32[]{:S(2)}) copy-start(bf16[1,1,128,6144]{3,2,1,0:T(8,128)(2,1)} %param.12) | copy-start | bytes 4718596
  4.6 14.2 %copy-start.12 = (f32[1,6144]{1,0:T(1,128)S(1)}, f32[1,6144]{1,0:T(1,128)}, u32[]{:S(2)}) copy-start(f32[1,6144]{1,0:T(1,128)} %refs_4_.1) | copy-start | bytes 73732
  4.6 14.2 %copy-start.13 = (f32[1,6144]{1,0:T(1,128)S(1)}, f32[1,6144]{1,0:T(1,128)}, u32[]{:S(2)}) copy-start(f32[1,6144]{1,0:T(1,128)} %refs_5_.1) | copy-start | bytes 73732
  4.6 19.9 %all-to-all-start = ((bf16[4,192,768]{2,1,0:T(8,128)(2,1)}), bf16[4,192,768]{2,1,0:T(8,128)(2,1)S(1)}, u32[]{:S(2)}, u32[]{:S(2)}) async-start(bf16[4,192,768]{2,1,0:T(8,128)(2,1)} %bitcast.10), calls=%async_computation | async-start | bytes 2359296 | tf_op jit(solution)/shard_map/all_to_all | solution.py:29
  9.7 8.2 %collective-permute-start = (s32[1]{0:T(128)}, s32[1]{0:T(128)}, u32[]{:S(2)}, u32[]{:S(2)}) collective-permute-start(s32[1]{0:T(128)} %bitcast), channel_id=1, source_target_pairs={{0,8},{8,0},{1,9},{9,1},{2,10},{10,2},{3,11},{11,3},{4,12},{12,4},... | collective-permute-start | bytes 20 | tf_op jit(solution)/shard_map/ppermute | solution.py:25
  12.2 10.3 %collective-permute-start.1 = (bf16[48,768]{1,0:T(8,128)(2,1)}, bf16[48,768]{1,0:T(8,128)(2,1)}, u32[]{:S(2)}, u32[]{:S(2)}) collective-permute-start(bf16[48,768]{1,0:T(8,128)(2,1)} %dynamic-slice_bitcast_fusion), channel_id=1, source_target_pairs={{5,0},{18,1},{38,2},{48,3},{71,4},{84,5},{102,6},{117,7},{3,16},{2... | collective-permute-start | bytes 221192 | tf_op jit(solution)/shard_map/ppermute | solution.py:66
  18.8 1.4 copy-start.2
  22.5 11.9 %copy-start.16 = (s32[1,1,4,4]{3,2,1,0:T(4,128)S(1)}, s32[1,1,4,4]{3,2,1,0:T(4,128)}, u32[]{:S(2)}) copy-start(s32[1,1,4,4]{3,2,1,0:T(4,128)} %param.16) | copy-start | bytes 196
  22.5 12.3 %copy-start.5 = (bf16[1,1,128,768]{3,2,1,0:T(8,128)(2,1)S(1)}, bf16[1,1,128,768]{3,2,1,0:T(8,128)(2,1)}, u32[]{:S(2)}) copy-start(bf16[1,1,128,768]{3,2,1,0:T(8,128)(2,1)} %param.13) | copy-start | bytes 589828
  22.5 12.3 %copy-start.6 = (bf16[1,1,128,768]{3,2,1,0:T(8,128)(2,1)S(1)}, bf16[1,1,128,768]{3,2,1,0:T(8,128)(2,1)}, u32[]{:S(2)}) copy-start(bf16[1,1,128,768]{3,2,1,0:T(8,128)(2,1)} %param.14) | copy-start | bytes 589828
  22.5 12.3 %copy-start.8 = (bf16[1,1,128,768]{3,2,1,0:T(8,128)(2,1)S(1)}, bf16[1,1,128,768]{3,2,1,0:T(8,128)(2,1)}, u32[]{:S(2)}) copy-start(bf16[1,1,128,768]{3,2,1,0:T(8,128)(2,1)} %param.15) | copy-start | bytes 589828
  25.4 17.3 %all-to-all-start.1 = ((bf16[4,48,768]{2,1,0:T(8,128)(2,1)}), bf16[4,48,768]{2,1,0:T(8,128)(2,1)S(1)}, u32[]{:S(2)}, u32[]{:S(2)}) async-start(bf16[4,48,768]{2,1,0:T(8,128)(2,1)} %bitcast.16), calls=%async_computation.1 | async-start | bytes 589824 | tf_op jit(solution)/shard_map/all_to_all | solution.py:29
  36.9 20.7 %copy-start.3 = (f32[12,128,128]{2,1,0:T(8,128)}, f32[12,128,128]{2,1,0:T(8,128)S(1)}, u32[]{:S(2)}) copy-start(f32[12,128,128]{2,1,0:T(8,128)S(1)} %get-tuple-element.37.refs_6_) | copy-start | bytes 2359300
  57.6 18.3 %all-to-all-start.3 = ((bf16[4,192,768]{2,1,0:T(8,128)(2,1)}), bf16[4,192,768]{2,1,0:T(8,128)(2,1)S(1)}, u32[]{:S(2)}, u32[]{:S(2)}) async-start(bf16[4,192,768]{2,1,0:T(8,128)(2,1)} %get-tuple-element.25), calls=%async_computation.3 | async-start | bytes 2359296 | tf_op jit(solution)/shard_map/all_to_all | solution.py:29
  62.8 4.5 %collective-permute-start.4 = (bf16[48,768]{1,0:T(8,128)(2,1)S(1)}, bf16[48,768]{1,0:T(8,128)(2,1)S(1)}, u32[]{:S(2)}, u32[]{:S(2)}) collective-permute-start(bf16[48,768]{1,0:T(8,128)(2,1)S(1)} %get-tuple-element.26.refs_1_), channel_id=1, source_target_pairs={{0,192},{16,208},{32,224},{48,240},{64,0},{80,16},{96,32},{112,48}... | collective-permute-start | bytes 221192 | tf_op jit(solution)/shard_map/ppermute | solution.py:38
  63.1 8.1 %collective-permute-start.3 = (bf16[48,768]{1,0:T(8,128)(2,1)S(1)}, bf16[48,768]{1,0:T(8,128)(2,1)S(1)}, u32[]{:S(2)}, u32[]{:S(2)}) collective-permute-start(bf16[48,768]{1,0:T(8,128)(2,1)S(1)} %get-tuple-element.26.refs_1_), channel_id=1, source_target_pairs={{0,128},{16,144},{32,160},{48,176},{64,192},{80,208},{96,224},{112... | collective-permute-start | bytes 221192 | tf_op jit(solution)/shard_map/ppermute | solution.py:38
  65.5 6.8 %collective-permute-start.2 = (bf16[48,768]{1,0:T(8,128)(2,1)S(1)}, bf16[48,768]{1,0:T(8,128)(2,1)S(1)}, u32[]{:S(2)}, u32[]{:S(2)}) collective-permute-start(bf16[48,768]{1,0:T(8,128)(2,1)S(1)} %get-tuple-element.26.refs_1_), channel_id=1, source_target_pairs={{0,64},{16,80},{32,96},{48,112},{64,128},{80,144},{96,160},{112,17... | collective-permute-start | bytes 221192 | tf_op jit(solution)/shard_map/ppermute | solution.py:38
  77.5 20.0 %all-to-all-start.4 = ((bf16[8,128,768]{2,1,0:T(8,128)(2,1)}), bf16[8,128,768]{2,1,0:T(8,128)(2,1)S(1)}, u32[]{:S(2)}, u32[]{:S(2)}) async-start(bf16[8,128,768]{2,1,0:T(8,128)(2,1)} %get-tuple-element.27), calls=%async_computation.4 | async-start | bytes 3145728 | tf_op jit(solution)/shard_map/all_to_all | solution.py:29
  81.4 5.8 %collective-permute-start.7 = (bf16[4,48,768]{2,1,0:T(8,128)(2,1)}, bf16[4,48,768]{2,1,0:T(8,128)(2,1)S(1)}, u32[]{:S(2)}, u32[]{:S(2)}) collective-permute-start(bf16[4,48,768]{2,1,0:T(8,128)(2,1)} %get-tuple-element.28.refs_2_), channel_id=1, source_target_pairs={{0,48},{16,0},{32,16},{48,32},{64,112},{80,64},{96,80},{112,96},{1... | collective-permute-start | bytes 884744 | tf_op jit(solution)/shard_map/ppermute | solution.py:38
  82.1 7.4 %collective-permute-start.6 = (bf16[4,48,768]{2,1,0:T(8,128)(2,1)}, bf16[4,48,768]{2,1,0:T(8,128)(2,1)S(1)}, u32[]{:S(2)}, u32[]{:S(2)}) collective-permute-start(bf16[4,48,768]{2,1,0:T(8,128)(2,1)} %get-tuple-element.28.refs_2_), channel_id=1, source_target_pairs={{0,32},{16,48},{32,0},{48,16},{64,96},{80,112},{96,64},{112,80},{1... | collective-permute-start | bytes 884744 | tf_op jit(solution)/shard_map/ppermute | solution.py:38
  83.2 9.6 %collective-permute-start.5 = (bf16[4,48,768]{2,1,0:T(8,128)(2,1)}, bf16[4,48,768]{2,1,0:T(8,128)(2,1)}, u32[]{:S(2)}, u32[]{:S(2)}) collective-permute-start(bf16[4,48,768]{2,1,0:T(8,128)(2,1)} %get-tuple-element.28.refs_2_), channel_id=1, source_target_pairs={{0,16},{16,32},{32,48},{48,0},{64,80},{80,96},{96,112},{112,64},{1... | collective-permute-start | bytes 884744 | tf_op jit(solution)/shard_map/ppermute | solution.py:38
  87.2 2.3 %copy-start.14 = (bf16[4,48,768]{2,1,0:T(8,128)(2,1)}, bf16[4,48,768]{2,1,0:T(8,128)(2,1)S(1)}, u32[]{:S(2)}) copy-start(bf16[4,48,768]{2,1,0:T(8,128)(2,1)S(1)} %collective-permute-done.7.refs_5_) | copy-start | bytes 884740
  89.5 0.7 copy-start.15
  100.8 13.7 %copy-start.10 = (f32[16,6144]{1,0:T(8,128)S(1)}, f32[16,6144]{1,0:T(8,128)}, u32[]{:S(2)}) copy-start(f32[16,6144]{1,0:T(8,128)} %get-tuple-element.31.refs_1_) | copy-start | bytes 1179652
  100.9 13.7 %copy-start.11 = (f32[16,6144]{1,0:T(8,128)S(1)}, f32[16,6144]{1,0:T(8,128)}, u32[]{:S(2)}) copy-start(f32[16,6144]{1,0:T(8,128)} %get-tuple-element.32.refs_2_) | copy-start | bytes 1179652
  115.6 34.3 %copy-start.4 = (f32[12,128,128]{2,1,0:T(8,128)S(1)}, f32[12,128,128]{2,1,0:T(8,128)}, u32[]{:S(2)}) copy-start(f32[12,128,128]{2,1,0:T(8,128)} %copy-done.3) | copy-start | bytes 2359300
  115.6 34.3 %copy-start.7 = (bf16[1,1,128,768]{3,2,1,0:T(8,128)(2,1)S(1)}, bf16[1,1,128,768]{3,2,1,0:T(8,128)(2,1)}, u32[]{:S(2)}) copy-start(bf16[1,1,128,768]{3,2,1,0:T(8,128)(2,1)} %param.14) | copy-start | bytes 589828
  115.6 34.3 %copy-start.9 = (bf16[1,1,128,768]{3,2,1,0:T(8,128)(2,1)S(1)}, bf16[1,1,128,768]{3,2,1,0:T(8,128)(2,1)}, u32[]{:S(2)}) copy-start(bf16[1,1,128,768]{3,2,1,0:T(8,128)(2,1)} %param.15) | copy-start | bytes 589828
  143.7 8.0 %collective-permute-start.8 = (bf16[16,768]{1,0:T(8,128)(2,1)S(1)}, bf16[16,768]{1,0:T(8,128)(2,1)S(1)}, u32[]{:S(2)}, u32[]{:S(2)}) collective-permute-start(bf16[16,768]{1,0:T(8,128)(2,1)S(1)} %shard_map.165.refs_0_), channel_id=1, source_target_pairs={{0,8},{8,0},{1,9},{9,1},{2,10},{10,2},{3,11},{11,3},{4,12},{12,4},... | collective-permute-start | bytes 73736 | tf_op jit(solution)/shard_map/ppermute | solution.py:25
